TPU v7x, 256 devices: a whole 4x4x8 slice. The times are simulated.
256 devices in a mesh: group: 16 (over y_lo, x, core), tensor: 16 (over y_hi, z).
Axes of the slice: x: 4, y: 4 (y_hi: 2, y_lo: 2; y = y_hi * 2 + y_lo), z: 8, core: 2. Of those that a mesh axis runs over, the one named last changes fastest.
Arguments:
- queries: bfloat16 [4, 256, 64, 128], P(None, 'group', 'tensor')
- new_keys: bfloat16 [4, 256, 16, 128], P(None, 'group', 'tensor')
- new_values: bfloat16 [4, 256, 16, 128], P(None, 'group', 'tensor')
- key_cache: bfloat16 [256, 16, 512, 128], P('group', 'tensor')
- value_cache: bfloat16 [256, 16, 512, 128], P('group', 'tensor')
- cache_len: int32 [256], replicated, may hold values from 8 to 508, as said below
- remaining: int32 [256], replicated, may hold values from 0 to 6
- dest_table: int32 [256], replicated, may hold values from 0 to 255, as said below
- residual_in: bfloat16 [4, 256, 5120], P(None, 'group')
- out_weight: bfloat16 [8192, 5120], P('tensor'), may hold values from -0.0625 to 0.0625
- norm_gain: bfloat16 [5120], replicated, may hold values from 0.5 to 1.5
Outputs:
- residual_out: bfloat16 [4, 256, 5120], P(None, 'group')
- normed: bfloat16 [4, 256, 5120], P(None, 'group')
- key_out: bfloat16 [256, 16, 512, 128], P('group', 'tensor')
- value_out: bfloat16 [256, 16, 512, 128], P('group', 'tensor')
Inputs may be any that keep to these rules, and one draw needn't show every extreme that they name: dest_table is a permutation of the 256 slots, old slot g * 16 + j being slot j of group g. Each group sends exactly one of its sequences to every group, itself included, and the one that group g sends lands in slot g of its new group (dest_table % 16 equals the sending group). `cache_len`: some sequence has exactly 508 cached tokens in every draw.
All inputs are finite; a program needn't handle non-finite values.
Results may differ from a plain program's by a relative error of at most 0.0033.
Values may be sent and summed in bfloat16 or wider, within the bound.
No kernel may reach another device: no remote copies, remote signals or barrier semaphores. Data moves between devices by JAX's collectives and lax.ppermute only.
A program may use at most 128 MiB of HBM per device.

v0:
```python
import jax
import jax.numpy as jnp
from jax import lax
from jax.sharding import PartitionSpec as P

neg_fill = -1e30
eps = 1e-06


def weigh(scores):
    top = jnp.max(scores, axis=-1)
    weights = jnp.exp(scores - top[..., None])
    summed = jnp.sum(weights, axis=-1)
    return (top, weights.astype(jnp.bfloat16), summed)


def cache_block(query_rows, old_keys, old_values, lengths):
    step_count, slot_count, head_count, head_width = query_rows.shape
    copies = old_keys.shape[1]
    grouped = query_rows.reshape(step_count, slot_count, copies, head_count // copies, head_width)
    scores = jnp.einsum(
        "tskgd,skld->tskgl", grouped, old_keys, preferred_element_type=jnp.float32
    ) * head_width ** (-0.5)
    places = lax.broadcasted_iota(jnp.int32, (1, 1, 1, 1, old_keys.shape[2]), 4)
    scores = jnp.where(places < lengths[None, :, None, None, None], scores, neg_fill)
    top, weights, summed = weigh(scores)
    mixed = jnp.einsum("tskgl,skld->tskgd", weights, old_values, preferred_element_type=jnp.float32)
    return (top, mixed, summed)


def fresh_block(query_rows, fresh_keys, fresh_values):
    step_count, slot_count, head_count, head_width = query_rows.shape
    copies = fresh_keys.shape[2]
    grouped = query_rows.reshape(step_count, slot_count, copies, head_count // copies, head_width)
    scores = jnp.einsum(
        "tskgd,uskd->tskgu", grouped, fresh_keys, preferred_element_type=jnp.float32
    ) * head_width ** (-0.5)
    later = lax.broadcasted_iota(
        jnp.int32, (step_count, 1, 1, 1, step_count), 4
    ) <= lax.broadcasted_iota(jnp.int32, (step_count, 1, 1, 1, step_count), 0)
    scores = jnp.where(later, scores, neg_fill)
    top, weights, summed = weigh(scores)
    mixed = jnp.einsum(
        "tskgu,uskd->tskgd", weights, fresh_values, preferred_element_type=jnp.float32
    )
    return (top, mixed, summed)


def on_device(
    queries,
    new_keys,
    new_values,
    key_cache,
    value_cache,
    cache_len,
    remaining,
    dest_table,
    residual_in,
    out_weight,
    norm_gain,
):
    position = lax.axis_index("group")
    slot_count = key_cache.shape[0]
    all_slots = dest_table.shape[0]
    numbers = jnp.arange(slot_count, dtype=jnp.int32)
    outgoing = lax.dynamic_slice_in_dim(dest_table, position * slot_count, slot_count)
    target_group = outgoing // slot_count
    send_order = jnp.zeros((slot_count,), jnp.int32).at[target_group].set(numbers)
    source = (
        jnp.zeros((all_slots,), jnp.int32)
        .at[dest_table]
        .set(jnp.arange(all_slots, dtype=jnp.int32))
    )
    arrived_from = lax.dynamic_slice_in_dim(source, position * slot_count, slot_count)
    lengths = cache_len[arrived_from]
    rests = remaining[arrived_from]
    arrived_keys, arrived_values = (
        lax.all_to_all(key_cache[send_order], "group", split_axis=0, concat_axis=0, tiled=True),
        lax.all_to_all(value_cache[send_order], "group", split_axis=0, concat_axis=0, tiled=True),
    )
    top_one, mixed_one, total_one = cache_block(queries, arrived_keys, arrived_values, lengths)
    top_two, mixed_two, total_two = fresh_block(queries, new_keys, new_values)
    highest = jnp.maximum(top_one, top_two)
    first_factor = jnp.exp(top_one - highest)
    second_factor = jnp.exp(top_two - highest)
    merged = (first_factor[..., None] * mixed_one + second_factor[..., None] * mixed_two) / (
        first_factor * total_one + second_factor * total_two
    )[..., None]
    step_count = merged.shape[0]
    living = lax.broadcasted_iota(jnp.int32, (step_count, slot_count), 0) < rests[None, :]
    merged = jnp.where(living[:, :, None, None, None], merged, 0.0).astype(jnp.bfloat16)
    partial_value = jnp.dot(
        merged.reshape(step_count * slot_count, -1), out_weight, preferred_element_type=jnp.float32
    )
    places = lax.broadcasted_iota(jnp.int32, (slot_count, 1, key_cache.shape[2], 1), 2)
    length_grid = lengths[:, None, None, None]
    rest_grid = rests[:, None, None, None]
    retained = (places < length_grid) & (rest_grid > 0)
    key_new = jnp.where(retained, arrived_keys, jnp.zeros((), arrived_keys.dtype))
    value_new = jnp.where(retained, arrived_values, jnp.zeros((), arrived_values.dtype))
    for step in range(step_count):
        placed = (places == length_grid + step) & (rest_grid > step)
        key_new = jnp.where(placed, new_keys[step][:, :, None, :], key_new)
        value_new = jnp.where(placed, new_values[step][:, :, None, :], value_new)
    gain_full = norm_gain.astype(jnp.float32)
    model_width = out_weight.shape[1]
    summed_heads = lax.psum(partial_value, "tensor").reshape(step_count, slot_count, model_width)
    level = residual_in.astype(jnp.float32) + summed_heads
    residual_out = level.astype(jnp.bfloat16)
    normed = (
        level * lax.rsqrt(jnp.mean(level * level, axis=-1, keepdims=True) + eps) * gain_full
    ).astype(jnp.bfloat16)
    return (residual_out, normed, key_new, value_new)


def solution(mesh):
    placed = (
        P(None, "group", "tensor", None),
        P(None, "group", "tensor", None),
        P(None, "group", "tensor", None),
        P("group", "tensor", None, None),
        P("group", "tensor", None, None),
        P(),
        P(),
        P(),
        P(None, "group", None),
        P("tensor", None),
        P(),
    )
    return jax.shard_map(
        on_device,
        mesh=mesh,
        in_specs=placed,
        out_specs=(
            P(None, "group", None),
            P(None, "group", None),
            P("group", "tensor", None, None),
            P("group", "tensor", None, None),
        ),
        check_vma=False,
    )
```

profile of v0, /device:TPU:24, one launch (start us, length us, event | category | flops | bytes accessed | tf_op | source)
XLA Modules:
  0.0 256.3 jit_solution(17992812843087385777)
XLA Ops:
  7.2 0.0 copy-start
  7.2 0.8 compare_select_fusion
  8.0 1.4 scatter_custom_fusion
  9.4 0.8 compare_select_fusion.2
  10.2 0.6 scatter_custom_fusion.1
  10.9 2.1 gather_fusion.2
  13.0 5.8 %all-to-all-start = ((bf16[16,1,512,128]{3,2,1,0:T(8,128)(2,1)}), bf16[16,1,512,128]{3,2,1,0:T(8,128)(2,1)}, u32[]{:S(2)}, u32[]{:S(2)}) async-start(bf16[16,1,512,128]{3,2,1,0:T(8,128)(2,1)} %bitcast.121), calls=%async_computation | async-start | bytes 4194304 | tf_op jit(solution)/shard_map/all_to_all | solution.py:78
  18.8 3.8 %gather_fusion.3 = bf16[16,512,128]{2,1,0:T(8,128)(2,1)} fusion(bf16[16,512,128]{2,1,0:T(8,128)(2,1)} %bitcast.123, s32[1024]{0:T(1024)S(1)} %pad_clamp_fusion), kind=kCustom, calls=%fused_computation.3 | custom fusion | bytes 4194368 | tf_op jit(solution)/shard_map/gather | solution.py:79
  22.6 0.7 gather_fusion.1
  23.3 0.7 fusion.67
  24.0 22.3 %all-to-all-done = bf16[16,1,512,128]{3,2,1,0:T(8,128)(2,1)} async-done(((bf16[16,1,512,128]{3,2,1,0:T(8,128)(2,1)}), bf16[16,1,512,128]{3,2,1,0:T(8,128)(2,1)}, u32[]{:S(2)}, u32[]{:S(2)}) %all-to-all-start) | async-done | bytes 2097184 | tf_op jit(solution)/shard_map/all_to_all | solution.py:78
  46.3 5.4 %all-to-all-start.1 = ((bf16[16,1,512,128]{3,2,1,0:T(8,128)(2,1)}), bf16[16,1,512,128]{3,2,1,0:T(8,128)(2,1)}, u32[]{:S(2)}, u32[]{:S(2)}) async-start(bf16[16,1,512,128]{3,2,1,0:T(8,128)(2,1)} %bitcast.120), calls=%async_computation.1 | async-start | bytes 4194304 | tf_op jit(solution)/shard_map/all_to_all | solution.py:79
  51.6 0.0 all-reduce.2.cloned.1.call-start
  51.7 0.7 gather_fusion
  52.4 0.1 fusion.43
  52.5 0.1 iota_compare_fusion.5
  52.6 0.1 fusion.55
  52.7 0.1 fusion.58
  52.8 2.5 fusion.68
  55.3 0.4 fusion.38
  55.7 0.3 fusion.26
  55.9 23.2 %all-to-all-done.1 = bf16[16,1,512,128]{3,2,1,0:T(8,128)(2,1)} async-done(((bf16[16,1,512,128]{3,2,1,0:T(8,128)(2,1)}), bf16[16,1,512,128]{3,2,1,0:T(8,128)(2,1)}, u32[]{:S(2)}, u32[]{:S(2)}) %all-to-all-start.1) | async-done | bytes 2097184 | tf_op jit(solution)/shard_map/all_to_all | solution.py:79
  79.2 2.1 fusion.27
  81.3 4.6 %fusion.47 = f32[64,5120]{1,0:T(8,128)} fusion(bf16[512,5120]{1,0:T(8,128)(2,1)} %param.20, bf16[8,8,4,128]{3,2,1,0:T(4,128)(2,1)S(1)} %bitcast.124), kind=kOutput, calls=%fused_computation.40 | convolution fusion | flops 335544320 | bytes 6619136 | tf_op jit(solution)/shard_map/dot_general | solution.py:92
  86.0 0.0 all-reduce.2.cloned.1.call-update
  86.0 0.1 fusion.57
  86.1 0.1 fusion.56
  86.2 8.8 %select_select_fusion = (bf16[16,1,512,128]{3,2,1,0:T(8,128)(2,1)}, bf16[16,1,512,128]{3,2,1,0:T(8,128)(2,1)}) fusion(bf16[16,1,512,128]{3,2,1,0:T(8,128)(2,1)} %all-to-all-done.1, pred[16,512]{1,0:T(8,128)(4,1)S(1)} %get-tuple-element.28, pred[16,512]{1,0:T(8,128)(4,1)S(1)} %get-tuple-element.27, pred[16,512]{1,0:T(8,128)(4,1)S(1)} %fusion.57, ...), kind=kLoop, calls=%fused_computation.10 | loop fusion | flops 10485760 | bytes 8462336 | tf_op jit(solution)/shard_map/jit(_where)/select_n | solution.py:104
  95.0 151.4 %all-reduce.2.cloned.1.call-done = f32[4,16,5120]{2,1,0:T(8,128)} async-done(((f32[4,16,5120]{2,1,0:T(8,128)}), f32[4,16,5120]{2,1,0:T(8,128)}) %all-reduce.2.cloned.1.call-update) | async-done | bytes 1310736 | tf_op jit(solution)/shard_map/psum | solution.py:107
  246.4 1.7 multiply_reduce_fusion
  248.0 0.0 copy-done.3
  248.1 1.3 multiply_convert_fusion
  (29 shorter events, 0.1 us)
Async XLA Ops:
  7.2 3.7 %copy-start = (bf16[16,1,512,128]{3,2,1,0:T(8,128)(2,1)S(1)}, bf16[16,1,512,128]{3,2,1,0:T(8,128)(2,1)}, u32[]{:S(2)}) copy-start(bf16[16,1,512,128]{3,2,1,0:T(8,128)(2,1)} %param.14) | copy-start | bytes 6291460
  13.0 33.3 %all-to-all-start = ((bf16[16,1,512,128]{3,2,1,0:T(8,128)(2,1)}), bf16[16,1,512,128]{3,2,1,0:T(8,128)(2,1)}, u32[]{:S(2)}, u32[]{:S(2)}) async-start(bf16[16,1,512,128]{3,2,1,0:T(8,128)(2,1)} %bitcast.121), calls=%async_computation | async-start | bytes 4194304 | tf_op jit(solution)/shard_map/all_to_all | solution.py:78
  18.8 3.8 %copy-start.1 = (s32[256]{0:T(256)S(1)}, s32[256]{0:T(256)}, u32[]{:S(2)}) copy-start(s32[256]{0:T(256)} %param.16) | copy-start | bytes 3076
  18.8 4.5 %copy-start.5 = (bf16[4,16,1,128]{3,1,2,0:T(8,128)(2,1)S(1)}, bf16[4,16,1,128]{3,1,2,0:T(8,128)(2,1)}, u32[]{:S(2)}) copy-start(bf16[4,16,1,128]{3,1,2,0:T(8,128)(2,1)} %param.12) | copy-start | bytes 49156
  18.8 4.5 %copy-start.8 = (bf16[4,16,4,128]{3,2,1,0:T(4,128)(2,1)S(1)}, bf16[4,16,4,128]{3,2,1,0:T(4,128)(2,1)}, u32[]{:S(2)}) copy-start(bf16[4,16,4,128]{3,2,1,0:T(4,128)(2,1)} %param.11) | copy-start | bytes 196612
  46.3 5.4 %copy-start.2 = (s32[256]{0:T(256)S(1)}, s32[256]{0:T(256)}, u32[]{:S(2)}) copy-start(s32[256]{0:T(256)} %param.17) | copy-start | bytes 3076
  46.3 32.9 %all-to-all-start.1 = ((bf16[16,1,512,128]{3,2,1,0:T(8,128)(2,1)}), bf16[16,1,512,128]{3,2,1,0:T(8,128)(2,1)}, u32[]{:S(2)}, u32[]{:S(2)}) async-start(bf16[16,1,512,128]{3,2,1,0:T(8,128)(2,1)} %bitcast.120), calls=%async_computation.1 | async-start | bytes 4194304 | tf_op jit(solution)/shard_map/all_to_all | solution.py:79
  51.6 194.7 %all-reduce.2.cloned.1.call-start = ((), (), s32[]{:S(2)}) async-start(), calls=%async_computation.2 | async-start | bytes 2621440 | tf_op jit(solution)/shard_map/psum | solution.py:107
  52.4 3.3 %copy-start.6 = (bf16[4,16,1,128]{3,1,2,0:T(8,128)(2,1)S(1)}, bf16[4,16,1,128]{3,1,2,0:T(8,128)(2,1)}, u32[]{:S(2)}) copy-start(bf16[4,16,1,128]{3,1,2,0:T(8,128)(2,1)} %param.13) | copy-start | bytes 49156
  81.3 4.8 %copy-start.7 = (bf16[5120]{0:T(1024)(128)(2,1)S(1)}, bf16[5120]{0:T(1024)(128)(2,1)}, u32[]{:S(2)}) copy-start(bf16[5120]{0:T(1024)(128)(2,1)} %param.21) | copy-start | bytes 30724
  86.2 160.2 %copy-start.4 = (bf16[4,16,5120]{2,1,0:T(8,128)(2,1)S(1)}, bf16[4,16,5120]{2,1,0:T(8,128)(2,1)}, u32[]{:S(2)}) copy-start(bf16[4,16,5120]{2,1,0:T(8,128)(2,1)} %param.19) | copy-start | bytes 1966084
  246.4 1.7 copy-start.3
Sparse Core Ops, SparseCore 0:
  86.1 160.2 all-reduce.1
where the time goes:
time: 259 us; the launch traced here: 256 us
  waiting for transfers between devices  197 us (76%)
  other arithmetic  14.4 us (6%)
  between operations  14.2 us (5%)
  starting transfers between devices  11.2 us (4%)
  matrix products  10.2 us (4%)
  local copies, waits for them, and re-layouts  9.36 us (4%)
    psum x1, waiting for transfers between devices, on_device(): lax.psum(partial_value, 'tensor')  151 us
    all_to_all x1, waiting for transfers between devices, on_device(): lax.all_to_all(value_cache[send_order], 'group', split_axis=0, concat_axi...  23.2 us
    all_to_all x1, waiting for transfers between devices, on_device(): lax.all_to_all(key_cache[send_order], 'group', split_axis=0, concat_axis=...  22.3 us
    select_n x1, other arithmetic, on_device(): value_new = jnp.where(placed, new_values[step][:, :, None, :], value_new)  8.81 us
    all_to_all x1, starting transfers between devices, on_device(): lax.all_to_all(key_cache[send_order], 'group', split_axis=0, concat_axis=...  5.78 us
    all_to_all x1, starting transfers between devices, on_device(): lax.all_to_all(value_cache[send_order], 'group', split_axis=0, concat_axi...  5.37 us
  transfers between devices with their start and end apart: 3, of which 3 were waited for; matrix products, arithmetic and copies ran while one was open for 7% of the time, Pallas kernels for 0%

commit v1 on v0

v1 whole, which is shorter than its diff:
```python
import functools

import jax
import jax.numpy as jnp
from jax import lax
from jax.experimental import pallas as pl
from jax.experimental.pallas import tpu as pltpu
from jax.sharding import PartitionSpec as P

neg_fill = -1e30
eps = 1e-06
ORDER = (0, 8, 4, 12, 2, 10, 6, 14, 1, 9, 5, 13, 3, 11, 7, 15)
f32 = jnp.float32
bf16 = jnp.bfloat16


def order_kernel(table, keys, values, keys_out, values_out, sems):
    n = keys.shape[0]

    def copies(d):
        j = table[0, d]
        return (
            pltpu.make_async_copy(keys.at[j], keys_out.at[d], sems.at[0, d]),
            pltpu.make_async_copy(values.at[j], values_out.at[d], sems.at[1, d]),
        )

    for d in range(n):
        for c in copies(d):
            c.start()
    for d in range(n):
        for c in copies(d):
            c.wait()


def order_cache(table, keys, values):
    n = keys.shape[0]
    return pl.pallas_call(
        order_kernel,
        out_shape=(
            jax.ShapeDtypeStruct(keys.shape, keys.dtype),
            jax.ShapeDtypeStruct(values.shape, values.dtype),
        ),
        in_specs=[
            pl.BlockSpec(memory_space=pltpu.SMEM),
            pl.BlockSpec(memory_space=pl.ANY),
            pl.BlockSpec(memory_space=pl.ANY),
        ],
        out_specs=(pl.BlockSpec(memory_space=pl.ANY),) * 2,
        scratch_shapes=[pltpu.SemaphoreType.DMA((2, n))],
        cost_estimate=pl.CostEstimate(
            flops=0, bytes_accessed=4 * keys.size * 2, transcendentals=0
        ),
        name="order_cache",
    )(table, keys, values)


def attend_kernel(table, msg, keys, values, weight, keep, send, att, kbuf, vbuf, wbuf, sems):
    t = table[5, 0]
    n = msg.shape[0]
    slots = kbuf.shape[0]
    wcopy = pltpu.make_async_copy(weight, wbuf, sems.at[2, 0])

    def fetch(p):
        c = t ^ ORDER[p]
        s = p % slots
        return (
            pltpu.make_async_copy(keys.at[c], kbuf.at[s], sems.at[0, s]),
            pltpu.make_async_copy(values.at[c], vbuf.at[s], sems.at[1, s]),
        )

    for p in range(min(slots, n)):
        for c in fetch(p):
            c.start()
    wcopy.start()
    col = lax.broadcasted_iota(jnp.int32, (16, keys.shape[1]), 1)
    row8 = lax.broadcasted_iota(jnp.int32, (16, 8), 0) % 4
    col8 = lax.broadcasted_iota(jnp.int32, (16, 8), 1)
    rowd = lax.broadcasted_iota(jnp.int32, (16, 128), 0) % 4
    scale = 128 ** (-0.5)
    nt = (((1,), (1,)), ((), ()))
    for p in range(n):
        c = t ^ ORDER[p]
        s = p % slots
        for cp in fetch(p):
            cp.wait()
        q = msg[c, 0:16, :]
        new_k = msg[c, 16:24, :]
        new_v = msg[c, 24:32, :]
        s1 = lax.dot_general(q, kbuf[s], nt, preferred_element_type=f32) * scale
        s1 = jnp.where(col < table[1, c], s1, neg_fill)
        m1 = jnp.max(s1, axis=1, keepdims=True)
        p1 = jnp.exp(s1 - m1)
        l1 = jnp.sum(p1, axis=1, keepdims=True)
        o1 = jnp.dot(p1.astype(bf16), vbuf[s], preferred_element_type=f32)
        s2 = lax.dot_general(q, new_k, nt, preferred_element_type=f32) * scale
        s2 = jnp.where(col8 <= row8, s2, neg_fill)
        m2 = jnp.max(s2, axis=1, keepdims=True)
        p2 = jnp.exp(s2 - m2)
        l2 = jnp.sum(p2, axis=1, keepdims=True)
        o2 = jnp.dot(p2.astype(bf16), new_v, preferred_element_type=f32)
        top = jnp.maximum(m1, m2)
        e1 = jnp.exp(m1 - top)
        e2 = jnp.exp(m2 - top)
        o = (e1 * o1 + e2 * o2) / (e1 * l1 + e2 * l2)
        o = jnp.where(rowd < table[2, c], o, 0.0)
        for h in range(4):
            att[4 * p : 4 * p + 4, 128 * h : 128 * h + 128] = o[4 * h : 4 * h + 4, :]
        if p + slots < n:
            for cp in fetch(p + slots):
                cp.start()
    wcopy.wait()
    a = att[...].astype(bf16)
    half = a.shape[0] // 2
    width = wbuf.shape[1]
    step = 512
    for k in range(0, width, step):
        y = jnp.dot(a, wbuf[:, k : k + step], preferred_element_type=f32)
        keep[:, k : k + step] = y[:half]
        send[:, k : k + step] = y[half:].astype(bf16)


def attend(table, msg, keys, values, weight):
    n, rows, width = msg.shape
    depth, out_width = weight.shape
    slots = 8
    return pl.pallas_call(
        attend_kernel,
        out_shape=(
            jax.ShapeDtypeStruct((2 * n, out_width), f32),
            jax.ShapeDtypeStruct((2 * n, out_width), bf16),
        ),
        in_specs=[
            pl.BlockSpec(memory_space=pltpu.SMEM),
            pl.BlockSpec(memory_space=pltpu.VMEM),
            pl.BlockSpec(memory_space=pl.ANY),
            pl.BlockSpec(memory_space=pl.ANY),
            pl.BlockSpec(memory_space=pl.ANY),
        ],
        out_specs=(pl.BlockSpec(memory_space=pltpu.VMEM),) * 2,
        scratch_shapes=[
            pltpu.VMEM((4 * n, depth), f32),
            pltpu.VMEM((slots,) + keys.shape[1:], bf16),
            pltpu.VMEM((slots,) + values.shape[1:], bf16),
            pltpu.VMEM((depth, out_width), bf16),
            pltpu.SemaphoreType.DMA((3, slots)),
        ],
        compiler_params=pltpu.CompilerParams(vmem_limit_bytes=32 * 1024 * 1024),
        cost_estimate=pl.CostEstimate(
            flops=4 * n * 16 * 512 * 128 + 2 * 4 * n * depth * out_width,
            bytes_accessed=4 * keys.size + 2 * weight.size,
            transcendentals=0,
        ),
        name="attend",
    )(table, msg, keys, values, weight)


def place_kernel(table, fresh, got, out, rows):
    s = pl.program_id(0)

    @pl.when(s == 0)
    def _():
        rows[...] = fresh[...].astype(f32)

    length = table[3, s]
    rest = table[4, s]
    held = jnp.where(rest > 0, length, 0)
    places = lax.broadcasted_iota(jnp.int32, got.shape[1:], 0)
    block = got[0]
    out[0] = jnp.where(places < held, block, jnp.zeros((), block.dtype))
    start = pl.multiple_of(jnp.minimum(length // 16 * 16, got.shape[1] - 32), 16)
    window = out[0, pl.ds(start, 32), :].astype(f32)
    inner = lax.broadcasted_iota(jnp.int32, window.shape, 0) + start
    for u in range(fresh.shape[0]):
        row = rows[u, pl.ds(s, 1), :]
        window = jnp.where((inner == length + u) & (rest > u), row, window)
    out[0, pl.ds(start, 32), :] = window.astype(bf16)


def place(table, fresh, got):
    n, length, width = got.shape
    return pl.pallas_call(
        place_kernel,
        out_shape=jax.ShapeDtypeStruct(got.shape, got.dtype),
        grid=(n,),
        in_specs=[
            pl.BlockSpec(memory_space=pltpu.SMEM),
            pl.BlockSpec(fresh.shape, lambda i: (0, 0, 0)),
            pl.BlockSpec((1, length, width), lambda i: (i, 0, 0)),
        ],
        out_specs=pl.BlockSpec((1, length, width), lambda i: (i, 0, 0)),
        scratch_shapes=[pltpu.VMEM(fresh.shape, f32)],
        cost_estimate=pl.CostEstimate(
            flops=0, bytes_accessed=4 * got.size, transcendentals=0
        ),
        name="place",
    )(table, fresh, got)


def finish_kernel(table, first, second, third, residual, gain, out, normed, sums, squares):
    t = table[5, 0]
    rows = residual.shape[0]
    row = lax.broadcasted_iota(jnp.int32, (rows, rows), 0)
    col = lax.broadcasted_iota(jnp.int32, (rows, rows), 1)
    i = col // 4
    turned = (i & 1) * 8 + (i // 2 & 1) * 4 + (i // 4 & 1) * 2 + (i // 8 & 1)
    target = (col % 4) * 16 + (t ^ turned)
    pick = jnp.where(row == target, 1.0, 0.0).astype(bf16)
    a, b = first.shape[0], first.shape[0] + second.shape[0]
    step = 512
    total = jnp.zeros((rows, 128), f32)
    for k in range(0, residual.shape[1], step):
        cut = slice(k, k + step)
        piece = jnp.concatenate([first[:, cut], second[:, cut], third[:, cut]], axis=0)
        level = residual[:, cut].astype(f32) + jnp.dot(pick, piece, preferred_element_type=f32)
        out[:, cut] = level.astype(bf16)
        sums[:, cut] = level
        sq = level * level
        for j in range(0, step, 128):
            total = total + sq[:, j : j + 128]
    mean = jnp.sum(total, axis=1, keepdims=True) / residual.shape[1]
    factor = lax.rsqrt(mean + eps)
    for k in range(0, residual.shape[1], step):
        cut = slice(k, k + step)
        normed[:, cut] = (sums[:, cut] * factor * gain[:, cut].astype(f32)).astype(bf16)


def finish(table, first, second, third, residual, gain):
    rows, width = residual.shape
    vm = pl.BlockSpec(memory_space=pltpu.VMEM)
    return pl.pallas_call(
        finish_kernel,
        out_shape=(jax.ShapeDtypeStruct((rows, width), bf16),) * 2,
        in_specs=[pl.BlockSpec(memory_space=pltpu.SMEM)] + [vm] * 5,
        out_specs=(vm, vm),
        scratch_shapes=[pltpu.VMEM((rows, width), f32), pltpu.VMEM((rows, 128), f32)],
        compiler_params=pltpu.CompilerParams(vmem_limit_bytes=16 * 1024 * 1024),
        cost_estimate=pl.CostEstimate(
            flops=2 * rows * rows * width, bytes_accessed=8 * rows * width, transcendentals=0
        ),
        name="finish",
    )(table, first, second, third, residual, gain)


def swap(x, mask):
    return lax.ppermute(x, "tensor", [(t, t ^ mask) for t in range(16)])


def hand_over(x, mask):
    return lax.ppermute(
        x,
        ("group", "tensor"),
        [(g * 16 + t, t * 16 + (g ^ mask)) for g in range(16) for t in range(16)],
    )


def on_device(
    queries,
    new_keys,
    new_values,
    key_cache,
    value_cache,
    cache_len,
    remaining,
    dest_table,
    residual_in,
    out_weight,
    norm_gain,
):
    group = lax.axis_index("group")
    tensor = lax.axis_index("tensor")
    steps, n, heads, width = queries.shape
    out_width = out_weight.shape[1]
    asked = jnp.transpose(queries, (1, 2, 0, 3)).reshape(n, heads * steps, width)
    pad = ((0, 0), (0, 4), (0, 0))
    msg = jnp.concatenate(
        [
            asked,
            jnp.pad(jnp.swapaxes(new_keys[:, :, 0, :], 0, 1), pad),
            jnp.pad(jnp.swapaxes(new_values[:, :, 0, :], 0, 1), pad),
        ],
        axis=1,
    )
    msg = lax.all_to_all(msg, "group", split_axis=0, concat_axis=0, tiled=True)

    numbers = jnp.arange(n, dtype=jnp.int32)
    dest = dest_table.reshape(n, n)
    lens = cache_len.reshape(n, n)
    rest = remaining.reshape(n, n)
    mine = numbers[:, None] == group
    own_dest = jnp.sum(jnp.where(mine, dest, 0), axis=0)
    own_len = jnp.sum(jnp.where(mine, lens, 0), axis=0)
    own_rest = jnp.sum(jnp.where(mine, rest, 0), axis=0)
    goes = own_dest[None, :] // n == numbers[:, None]
    comes = dest == group * n + numbers[:, None]
    table = jnp.stack(
        [
            jnp.sum(jnp.where(goes, numbers[None, :], 0), axis=1),
            jnp.sum(jnp.where(goes, own_len[None, :], 0), axis=1),
            jnp.sum(jnp.where(goes, own_rest[None, :], 0), axis=1),
            jnp.sum(jnp.where(comes, lens, 0), axis=1),
            jnp.sum(jnp.where(comes, rest, 0), axis=1),
            jnp.full((n,), tensor, jnp.int32),
        ]
    )
    keys, values = order_cache(table, key_cache[:, 0], value_cache[:, 0])
    keys_got = lax.all_to_all(keys, "group", split_axis=0, concat_axis=0, tiled=True)
    keep, send = attend(table, msg, keys, values, out_weight)
    s = keep + swap(send, 1).astype(f32)
    s = s[:16] + swap(s[16:].astype(bf16), 2).astype(f32)
    s = s[:8] + swap(s[8:].astype(bf16), 4).astype(f32)
    s = s[:4] + swap(s[4:].astype(bf16), 8).astype(f32)
    s = s.astype(bf16)
    s, values_now = lax.optimization_barrier((s, values))
    values_got = lax.all_to_all(values_now, "group", split_axis=0, concat_axis=0, tiled=True)
    first = jnp.concatenate([hand_over(s, m) for m in (0, 8, 4, 12)], axis=0)
    second = swap(first, 2)
    third = swap(jnp.concatenate([first, second], axis=0), 1)
    residual_out, normed = finish(
        table,
        first,
        second,
        third,
        residual_in.reshape(steps * n, out_width),
        norm_gain.reshape(1, out_width),
    )
    key_out = place(table, new_keys[:, :, 0, :], keys_got)
    value_out = place(table, new_values[:, :, 0, :], values_got)
    return (
        residual_out.reshape(steps, n, out_width),
        normed.reshape(steps, n, out_width),
        key_out[:, None],
        value_out[:, None],
    )


def solution(mesh):
    placed = (
        P(None, "group", "tensor", None),
        P(None, "group", "tensor", None),
        P(None, "group", "tensor", None),
        P("group", "tensor", None, None),
        P("group", "tensor", None, None),
        P(),
        P(),
        P(),
        P(None, "group", None),
        P("tensor", None),
        P(),
    )
    return jax.shard_map(
        on_device,
        mesh=mesh,
        in_specs=placed,
        out_specs=(
            P(None, "group", None),
            P(None, "group", None),
            P("group", "tensor", None, None),
            P("group", "tensor", None, None),
        ),
        check_vma=False,
    )
```

time: 259 us -> 292 us (1.13)
  Pallas kernels: 0 us -> 163 us
  waiting for transfers between devices: 197 us -> 73.1 us
  starting transfers between devices: 11.2 us -> 41.8 us
  between operations: 14.2 us -> 0.84 us
  other arithmetic: 14.4 us -> 1.29 us
  matrix products: 10.2 us -> 0 us
    pallas_call x0 -> x5, Pallas kernels: none -> 163 us  [the longest x1 129 us: order_cache(): pl.pallas_call(order_kernel, out_shape=(jax.ShapeDtypeStruct(keys.shape,...]
    psum x1 -> x0, waiting for transfers between devices: 151 us -> none  [on_device(): lax.psum(partial_value, 'tensor')]
    ppermute x0 -> x10, waiting for transfers between devices: none -> 69.3 us  [the longest x6 50.9 us: swap(): return lax.ppermute(x, 'tensor', [(t, t ^ mask) for t in range(16)])]
    all_to_all x2 -> x3, waiting for transfers between devices: 45.5 us -> 3.87 us  [the longest x1 3.86 us: on_device(): lax.all_to_all(keys, 'group', split_axis=0, concat_axis=0, tiled=True)]
    ppermute x0 -> x10, starting transfers between devices: none -> 25.1 us  [the longest x6 13.1 us: swap(): return lax.ppermute(x, 'tensor', [(t, t ^ mask) for t in range(16)])]
    select_n x4 -> x1, other arithmetic: 10.4 us -> 0.01 us  [on_device(): goes = own_dest[None, :] // n == numbers[:, None]]
    dot_general x5 -> x0, matrix products: 10.2 us -> none  [the longest x1 4.63 us: on_device(): jnp.dot(merged.reshape(step_count * slot_count, -1), out_weight, preferre...]
    gather x4 -> x0, local copies, waits for them, and re-layouts: 7.22 us -> none  [the longest x1 3.76 us: on_device(): value_cache[send_order]]
  transfers between devices with their start and end apart: 3 -> 13, of which waited for: 3 -> 9; matrix products, arithmetic and copies ran while one was open for 7% -> 1% of each run, Pallas kernels for 0% -> 49%
where the time goes in v1:
time: 292 us; the launch traced here: 288 us
  Pallas kernels  163 us (56%)
  waiting for transfers between devices  73.1 us (25%)
  starting transfers between devices  41.8 us (14%)
  local copies, waits for them, and re-layouts  8 us (3%)
    pallas_call x1, Pallas kernels, order_cache(): pl.pallas_call(order_kernel, out_shape=(jax.ShapeDtypeStruct(keys.shape,...  129 us
    ppermute x6, waiting for transfers between devices, swap(): return lax.ppermute(x, 'tensor', [(t, t ^ mask) for t in range(16)])  50.9 us
    pallas_call x2, Pallas kernels, place(): pl.pallas_call(place_kernel, out_shape=jax.ShapeDtypeStruct(got.shape, go...  19.6 us
    ppermute x4, waiting for transfers between devices, hand_over(): lax.ppermute(x, ('group', 'tensor'), [(g * 16 + t, t * 16 + (g ^ mask)) f...  18.4 us
    ppermute x6, starting transfers between devices, swap(): return lax.ppermute(x, 'tensor', [(t, t ^ mask) for t in range(16)])  13.1 us
    ppermute x4, starting transfers between devices, hand_over(): lax.ppermute(x, ('group', 'tensor'), [(g * 16 + t, t * 16 + (g ^ mask)) f...  12 us
    pallas_call x1, Pallas kernels, attend(): pl.pallas_call(attend_kernel, out_shape=(jax.ShapeDtypeStruct((2 * n, out...  11.9 us
  transfers between devices with their start and end apart: 13, of which 9 were waited for; matrix products, arithmetic and copies ran while one was open for 1% of the time, Pallas kernels for 49%

profile of v1, /device:TPU:24, one launch (start us, length us, event | category | flops | bytes accessed | tf_op | source)
XLA Modules:
  0.0 287.9 jit_solution(17845580159763403347)
XLA Ops:
  0.6 0.9 copy.20
  1.5 0.7 copy.25
  2.3 0.7 copy.26
  3.0 0.7 fusion.4
  3.7 5.8 %all-to-all-start = ((bf16[16,32,128]{2,1,0:T(8,128)(2,1)}), bf16[16,32,128]{2,1,0:T(8,128)(2,1)S(1)}, u32[]{:S(2)}, u32[]{:S(2)}) async-start(bf16[16,32,128]{2,1,0:T(8,128)(2,1)} %fusion.4), calls=%async_computation | async-start | bytes 262144 | tf_op jit(solution)/shard_map/all_to_all | solution.py:283
  9.5 0.8 reshape.79
  10.2 0.8 reshape.80
  11.0 0.8 reshape.81
  12.1 0.6 stack.23.table
  12.7 129.3 %order_cache.1 = (bf16[16,512,128]{2,1,0:T(8,128)(2,1)}, bf16[16,512,128]{2,1,0:T(8,128)(2,1)}) custom-call(s32[6,16]{1,0:T(8,128)} %stack.23.table, bf16[16,512,128]{2,1,0:T(8,128)(2,1)} %bitcast.25, bf16[16,512,128]{2,1,0:T(8,128)(2,1)} %bitcast.26), custom_call_target="tpu_custom_call" | custom-call | bytes 8388608 | tf_op jit(solution)/shard_map/order_cache/pallas_call | solution.py:37
  142.1 2.5 copy-done
  144.5 11.9 %attend.1 = (f32[32,5120]{1,0:T(8,128)S(1)}, bf16[32,5120]{1,0:T(8,128)(2,1)S(1)}) custom-call(s32[6,16]{1,0:T(8,128)S(1)} %copy-done.2, bf16[16,32,128]{2,1,0:T(8,128)(2,1)S(1)} %all-to-all-done.msg, bf16[16,512,128]{2,1,0:T(8,128)(2,1)} %get-tuple-element.12.keys, bf16[16,512,128]{2,1,0:T(8,128)(2,1)} %get-tuple-element.19.values, ...), custom_call_target="tpu_custom_call" | custom-call | flops 402653184 | bytes 9437184 | tf_op jit(solution)/shard_map/attend/pallas_call | solution.py:126
  156.4 2.0 collective-permute-start
  158.4 8.0 %collective-permute-done = bf16[32,5120]{1,0:T(8,128)(2,1)S(1)} collective-permute-done((bf16[32,5120]{1,0:T(8,128)(2,1)S(1)}, bf16[32,5120]{1,0:T(8,128)(2,1)S(1)}, u32[]{:S(2)}, u32[]{:S(2)}) %collective-permute-start) | collective-permute-done | bytes 327712 | tf_op jit(solution)/shard_map/ppermute | solution.py:245
  166.6 3.4 %collective-permute-start.1 = (bf16[16,5120]{1,0:T(8,128)(2,1)S(1)}, bf16[16,5120]{1,0:T(8,128)(2,1)S(1)}, u32[]{:S(2)}, u32[]{:S(2)}) collective-permute-start(bf16[16,5120]{1,0:T(8,128)(2,1)S(1)} %slice.41), channel_id=1, source_target_pairs={{0,2},{1,3},{2,0},{3,1},{4,6},{5,7},{6,4},{7,5},{8,10},{9,11},{10,... | collective-permute-start | bytes 491528 | tf_op jit(solution)/shard_map/ppermute | solution.py:245
  169.9 7.4 %collective-permute-done.1 = bf16[16,5120]{1,0:T(8,128)(2,1)S(1)} collective-permute-done((bf16[16,5120]{1,0:T(8,128)(2,1)S(1)}, bf16[16,5120]{1,0:T(8,128)(2,1)S(1)}, u32[]{:S(2)}, u32[]{:S(2)}) %collective-permute-start.1) | collective-permute-done | bytes 163872 | tf_op jit(solution)/shard_map/ppermute | solution.py:245
  177.4 6.3 %collective-permute-start.2 = (bf16[8,5120]{1,0:T(8,128)(2,1)S(1)}, bf16[8,5120]{1,0:T(8,128)(2,1)S(1)}, u32[]{:S(2)}, u32[]{:S(2)}) collective-permute-start(bf16[8,5120]{1,0:T(8,128)(2,1)S(1)} %slice.42), channel_id=1, source_target_pairs={{0,4},{1,5},{2,6},{3,7},{4,0},{5,1},{6,2},{7,3},{8,12},{9,13},{10,... | collective-permute-start | bytes 245768 | tf_op jit(solution)/shard_map/ppermute | solution.py:245
  183.6 5.7 %all-to-all-start.1 = ((bf16[16,512,128]{2,1,0:T(8,128)(2,1)}), bf16[16,512,128]{2,1,0:T(8,128)(2,1)S(1)}, u32[]{:S(2)}, u32[]{:S(2)}) async-start(bf16[16,512,128]{2,1,0:T(8,128)(2,1)} %get-tuple-element.12.keys), calls=%async_computation.1 | async-start | bytes 4194304 | tf_op jit(solution)/shard_map/all_to_all | solution.py:306
  189.4 1.3 collective-permute-start.3
  190.7 22.2 %collective-permute-done.3 = bf16[4,5120]{1,0:T(4,128)(2,1)S(1)} collective-permute-done((bf16[4,5120]{1,0:T(4,128)(2,1)S(1)}, bf16[4,5120]{1,0:T(4,128)(2,1)S(1)}, u32[]{:S(2)}, u32[]{:S(2)}) %collective-permute-start.3) | collective-permute-done | bytes 40992 | tf_op jit(solution)/shard_map/ppermute | solution.py:245
  212.9 3.9 %all-to-all-done.1.got = bf16[16,512,128]{2,1,0:T(8,128)(2,1)S(1)} async-done(((bf16[16,512,128]{2,1,0:T(8,128)(2,1)}), bf16[16,512,128]{2,1,0:T(8,128)(2,1)S(1)}, u32[]{:S(2)}, u32[]{:S(2)}) %all-to-all-start.1) | async-done | bytes 2097184 | tf_op jit(solution)/shard_map/all_to_all | solution.py:306
  216.8 5.1 %all-to-all-start.2 = ((bf16[16,512,128]{2,1,0:T(8,128)(2,1)}), bf16[16,512,128]{2,1,0:T(8,128)(2,1)}, u32[]{:S(2)}, u32[]{:S(2)}) async-start(bf16[16,512,128]{2,1,0:T(8,128)(2,1)} %get-tuple-element.19.values), calls=%async_computation.2 | async-start | bytes 4194304 | tf_op jit(solution)/shard_map/all_to_all | solution.py:314
  221.9 0.7 collective-permute-start.4
  222.6 3.5 %collective-permute-start.5 = (bf16[4,5120]{1,0:T(4,128)(2,1)S(1)}, bf16[4,5120]{1,0:T(4,128)(2,1)S(1)}, u32[]{:S(2)}, u32[]{:S(2)}) collective-permute-start(bf16[4,5120]{1,0:T(4,128)(2,1)S(1)} %fusion.5), channel_id=1, source_target_pairs={{0,8},{1,24},{2,40},{3,56},{4,72},{5,88},{6,104},{7,120},{8,136},{... | collective-permute-start | bytes 122888 | tf_op jit(solution)/shard_map/ppermute | solution.py:249
  226.2 7.2 %collective-permute-start.6 = (bf16[4,5120]{1,0:T(4,128)(2,1)S(1)}, bf16[4,5120]{1,0:T(4,128)(2,1)S(1)}, u32[]{:S(2)}, u32[]{:S(2)}) collective-permute-start(bf16[4,5120]{1,0:T(4,128)(2,1)S(1)} %fusion.5), channel_id=1, source_target_pairs={{0,4},{1,20},{2,36},{3,52},{4,68},{5,84},{6,100},{7,116},{8,132},{... | collective-permute-start | bytes 122888 | tf_op jit(solution)/shard_map/ppermute | solution.py:249
  234.0 5.6 %collective-permute-done.5 = bf16[4,5120]{1,0:T(4,128)(2,1)S(1)} collective-permute-done((bf16[4,5120]{1,0:T(4,128)(2,1)S(1)}, bf16[4,5120]{1,0:T(4,128)(2,1)S(1)}, u32[]{:S(2)}, u32[]{:S(2)}) %collective-permute-start.5) | collective-permute-done | bytes 40992 | tf_op jit(solution)/shard_map/ppermute | solution.py:249
  239.5 12.4 %collective-permute-done.6 = bf16[4,5120]{1,0:T(4,128)(2,1)S(1)} collective-permute-done((bf16[4,5120]{1,0:T(4,128)(2,1)S(1)}, bf16[4,5120]{1,0:T(4,128)(2,1)S(1)}, u32[]{:S(2)}, u32[]{:S(2)}) %collective-permute-start.6) | collective-permute-done | bytes 40992 | tf_op jit(solution)/shard_map/ppermute | solution.py:249
  252.5 6.3 %collective-permute-done.8.second = bf16[16,5120]{1,0:T(8,128)(2,1)S(1)} collective-permute-done((bf16[16,5120]{1,0:T(8,128)(2,1)S(1)}, bf16[16,5120]{1,0:T(8,128)(2,1)S(1)}, u32[]{:S(2)}, u32[]{:S(2)}) %collective-permute-start.8) | collective-permute-done | bytes 163872 | tf_op jit(solution)/shard_map/ppermute | solution.py:245
  259.2 7.0 %collective-permute-done.9.third = bf16[32,5120]{1,0:T(8,128)(2,1)S(1)} collective-permute-done((bf16[32,5120]{1,0:T(8,128)(2,1)S(1)}, bf16[32,5120]{1,0:T(8,128)(2,1)S(1)}, u32[]{:S(2)}, u32[]{:S(2)}) %collective-permute-start.9) | collective-permute-done | bytes 327712 | tf_op jit(solution)/shard_map/ppermute | solution.py:245
  266.2 2.1 finish.1
  268.3 9.8 %place.2 = bf16[16,512,128]{2,1,0:T(8,128)(2,1)} custom-call(s32[6,16]{1,0:T(8,128)} %stack.23.table, bf16[4,16,128]{2,1,0:T(8,128)(2,1)} %bitcast.31, bf16[16,512,128]{2,1,0:T(8,128)(2,1)} %copy-done.3), custom_call_target="tpu_custom_call" | custom-call | bytes 4194304 | tf_op jit(solution)/shard_map/place/pallas_call | solution.py:181
  278.1 9.8 %place.3 = bf16[16,512,128]{2,1,0:T(8,128)(2,1)} custom-call(s32[6,16]{1,0:T(8,128)} %stack.23.table, bf16[4,16,128]{2,1,0:T(8,128)(2,1)} %bitcast.33, bf16[16,512,128]{2,1,0:T(8,128)(2,1)} %all-to-all-done.2.got), custom_call_target="tpu_custom_call" | custom-call | bytes 4194304 | tf_op jit(solution)/shard_map/place/pallas_call | solution.py:181
  (33 shorter events, 2.1 us)
Async XLA Ops:
  3.7 138.4 %all-to-all-start = ((bf16[16,32,128]{2,1,0:T(8,128)(2,1)}), bf16[16,32,128]{2,1,0:T(8,128)(2,1)S(1)}, u32[]{:S(2)}, u32[]{:S(2)}) async-start(bf16[16,32,128]{2,1,0:T(8,128)(2,1)} %fusion.4), calls=%async_computation | async-start | bytes 262144 | tf_op jit(solution)/shard_map/all_to_all | solution.py:283
  12.7 129.3 %copy-start.2 = (s32[6,16]{1,0:T(8,128)S(1)}, s32[6,16]{1,0:T(8,128)}, u32[]{:S(2)}) copy-start(s32[6,16]{1,0:T(8,128)} %stack.23.table) | copy-start | bytes 1156
  142.1 2.5 copy-start
  156.4 10.0 %collective-permute-start = (bf16[32,5120]{1,0:T(8,128)(2,1)S(1)}, bf16[32,5120]{1,0:T(8,128)(2,1)S(1)}, u32[]{:S(2)}, u32[]{:S(2)}) collective-permute-start(bf16[32,5120]{1,0:T(8,128)(2,1)S(1)} %get-tuple-element.15), channel_id=1, source_target_pairs={{0,1},{1,0},{2,3},{3,2},{4,5},{5,4},{6,7},{7,6},{8,9},{9,8},{10,11... | collective-permute-start | bytes 983048 | tf_op jit(solution)/shard_map/ppermute | solution.py:245
  166.6 10.7 %collective-permute-start.1 = (bf16[16,5120]{1,0:T(8,128)(2,1)S(1)}, bf16[16,5120]{1,0:T(8,128)(2,1)S(1)}, u32[]{:S(2)}, u32[]{:S(2)}) collective-permute-start(bf16[16,5120]{1,0:T(8,128)(2,1)S(1)} %slice.41), channel_id=1, source_target_pairs={{0,2},{1,3},{2,0},{3,1},{4,6},{5,7},{6,4},{7,5},{8,10},{9,11},{10,... | collective-permute-start | bytes 491528 | tf_op jit(solution)/shard_map/ppermute | solution.py:245
  177.4 12.0 %collective-permute-start.2 = (bf16[8,5120]{1,0:T(8,128)(2,1)S(1)}, bf16[8,5120]{1,0:T(8,128)(2,1)S(1)}, u32[]{:S(2)}, u32[]{:S(2)}) collective-permute-start(bf16[8,5120]{1,0:T(8,128)(2,1)S(1)} %slice.42), channel_id=1, source_target_pairs={{0,4},{1,5},{2,6},{3,7},{4,0},{5,1},{6,2},{7,3},{8,12},{9,13},{10,... | collective-permute-start | bytes 245768 | tf_op jit(solution)/shard_map/ppermute | solution.py:245
  183.6 33.2 %all-to-all-start.1 = ((bf16[16,512,128]{2,1,0:T(8,128)(2,1)}), bf16[16,512,128]{2,1,0:T(8,128)(2,1)S(1)}, u32[]{:S(2)}, u32[]{:S(2)}) async-start(bf16[16,512,128]{2,1,0:T(8,128)(2,1)} %get-tuple-element.12.keys), calls=%async_computation.1 | async-start | bytes 4194304 | tf_op jit(solution)/shard_map/all_to_all | solution.py:306
  189.4 23.5 %collective-permute-start.3 = (bf16[4,5120]{1,0:T(4,128)(2,1)S(1)}, bf16[4,5120]{1,0:T(4,128)(2,1)S(1)}, u32[]{:S(2)}, u32[]{:S(2)}) collective-permute-start(bf16[4,5120]{1,0:T(4,128)(2,1)S(1)} %slice.43), channel_id=1, source_target_pairs={{0,8},{1,9},{2,10},{3,11},{4,12},{5,13},{6,14},{7,15},{8,0},{9,1},... | collective-permute-start | bytes 122888 | tf_op jit(solution)/shard_map/ppermute | solution.py:245
  212.9 46.2 %copy-start.4 = (bf16[5120]{0:T(1024)(128)(2,1)S(1)}, bf16[5120]{0:T(1024)(128)(2,1)}, u32[]{:S(2)}) copy-start(bf16[5120]{0:T(1024)(128)(2,1)} %param.21) | copy-start | bytes 30724
  212.9 53.3 %copy-start.1 = (bf16[4,16,5120]{2,1,0:T(8,128)(2,1)S(1)}, bf16[4,16,5120]{2,1,0:T(8,128)(2,1)}, u32[]{:S(2)}) copy-start(bf16[4,16,5120]{2,1,0:T(8,128)(2,1)} %param.19) | copy-start | bytes 1966084
  216.8 35.6 %copy-start.3 = (bf16[16,512,128]{2,1,0:T(8,128)(2,1)}, bf16[16,512,128]{2,1,0:T(8,128)(2,1)S(1)}, u32[]{:S(2)}) copy-start(bf16[16,512,128]{2,1,0:T(8,128)(2,1)S(1)} %all-to-all-done.1.got) | copy-start | bytes 6291460
  216.8 61.2 %all-to-all-start.2 = ((bf16[16,512,128]{2,1,0:T(8,128)(2,1)}), bf16[16,512,128]{2,1,0:T(8,128)(2,1)}, u32[]{:S(2)}, u32[]{:S(2)}) async-start(bf16[16,512,128]{2,1,0:T(8,128)(2,1)} %get-tuple-element.19.values), calls=%async_computation.2 | async-start | bytes 4194304 | tf_op jit(solution)/shard_map/all_to_all | solution.py:314
  221.9 12.0 %collective-permute-start.4 = (bf16[4,5120]{1,0:T(4,128)(2,1)S(1)}, bf16[4,5120]{1,0:T(4,128)(2,1)S(1)}, u32[]{:S(2)}, u32[]{:S(2)}) collective-permute-start(bf16[4,5120]{1,0:T(4,128)(2,1)S(1)} %fusion.5), channel_id=1, source_target_pairs={{0,0},{1,16},{2,32},{3,48},{4,64},{5,80},{6,96},{7,112},{8,128},{9... | collective-permute-start | bytes 122888 | tf_op jit(solution)/shard_map/ppermute | solution.py:249
  222.6 16.9 %collective-permute-start.5 = (bf16[4,5120]{1,0:T(4,128)(2,1)S(1)}, bf16[4,5120]{1,0:T(4,128)(2,1)S(1)}, u32[]{:S(2)}, u32[]{:S(2)}) collective-permute-start(bf16[4,5120]{1,0:T(4,128)(2,1)S(1)} %fusion.5), channel_id=1, source_target_pairs={{0,8},{1,24},{2,40},{3,56},{4,72},{5,88},{6,104},{7,120},{8,136},{... | collective-permute-start | bytes 122888 | tf_op jit(solution)/shard_map/ppermute | solution.py:249
  226.2 25.8 %collective-permute-start.6 = (bf16[4,5120]{1,0:T(4,128)(2,1)S(1)}, bf16[4,5120]{1,0:T(4,128)(2,1)S(1)}, u32[]{:S(2)}, u32[]{:S(2)}) collective-permute-start(bf16[4,5120]{1,0:T(4,128)(2,1)S(1)} %fusion.5), channel_id=1, source_target_pairs={{0,4},{1,20},{2,36},{3,52},{4,68},{5,84},{6,100},{7,116},{8,132},{... | collective-permute-start | bytes 122888 | tf_op jit(solution)/shard_map/ppermute | solution.py:249
  233.4 18.9 %collective-permute-start.7 = (bf16[4,5120]{1,0:T(4,128)(2,1)S(1)}, bf16[4,5120]{1,0:T(4,128)(2,1)S(1)}, u32[]{:S(2)}, u32[]{:S(2)}) collective-permute-start(bf16[4,5120]{1,0:T(4,128)(2,1)S(1)} %fusion.5), channel_id=1, source_target_pairs={{0,12},{1,28},{2,44},{3,60},{4,76},{5,92},{6,108},{7,124},{8,140},... | collective-permute-start | bytes 122888 | tf_op jit(solution)/shard_map/ppermute | solution.py:249
  252.4 6.4 %collective-permute-start.8 = (bf16[16,5120]{1,0:T(8,128)(2,1)S(1)}, bf16[16,5120]{1,0:T(8,128)(2,1)S(1)}, u32[]{:S(2)}, u32[]{:S(2)}) collective-permute-start(bf16[16,5120]{1,0:T(8,128)(2,1)S(1)} %pad_maximum_fusion.first), channel_id=1, source_target_pairs={{0,2},{1,3},{2,0},{3,1},{4,6},{5,7},{6,4},{7,5},{8,10},{9,11},{10,... | collective-permute-start | bytes 491528 | tf_op jit(solution)/shard_map/ppermute | solution.py:245
  259.0 7.2 %collective-permute-start.9 = (bf16[32,5120]{1,0:T(8,128)(2,1)S(1)}, bf16[32,5120]{1,0:T(8,128)(2,1)S(1)}, u32[]{:S(2)}, u32[]{:S(2)}) collective-permute-start(bf16[32,5120]{1,0:T(8,128)(2,1)S(1)} %concatenate.12), channel_id=1, source_target_pairs={{0,1},{1,0},{2,3},{3,2},{4,5},{5,4},{6,7},{7,6},{8,9},{9,8},{10,11... | collective-permute-start | bytes 983048 | tf_op jit(solution)/shard_map/ppermute | solution.py:245

commit v2 on v1

v2 whole, which is shorter than its diff:
```python
import functools

import jax
import jax.numpy as jnp
from jax import lax
from jax.experimental import pallas as pl
from jax.experimental.pallas import tpu as pltpu
from jax.sharding import PartitionSpec as P

neg_fill = -1e30
eps = 1e-06
ORDER = (0, 8, 4, 12, 2, 10, 6, 14, 1, 9, 5, 13, 3, 11, 7, 15)
f32 = jnp.float32
bf16 = jnp.bfloat16


def ask_kernel(queries, new_keys, new_values, msg, asked, built):
    steps, n, heads, width = queries.shape
    rows = msg.shape[1]
    asked[...] = queries[...].astype(f32).reshape(asked.shape)
    built[...] = jnp.zeros(built.shape, f32)
    for t in range(steps):
        for h in range(heads):
            built[pl.ds(4 * h + t, n, stride=rows), :] = asked[
                pl.ds(t * n * heads + h, n, stride=heads), :
            ]
        built[pl.ds(16 + t, n, stride=rows), :] = new_keys[t].astype(f32)
        built[pl.ds(24 + t, n, stride=rows), :] = new_values[t].astype(f32)
    msg[...] = built[...].astype(bf16).reshape(msg.shape)


def ask(queries, new_keys, new_values):
    steps, n, heads, width = queries.shape
    vm = pl.BlockSpec(memory_space=pltpu.VMEM)
    return pl.pallas_call(
        ask_kernel,
        out_shape=jax.ShapeDtypeStruct((n, 32, width), bf16),
        in_specs=[vm] * 3,
        out_specs=vm,
        scratch_shapes=[
            pltpu.VMEM((steps * n * heads, width), f32),
            pltpu.VMEM((n * 32, width), f32),
        ],
        compiler_params=pltpu.CompilerParams(vmem_limit_bytes=60 * 1024 * 1024),
        cost_estimate=pl.CostEstimate(flops=0, bytes_accessed=400000, transcendentals=0),
        name="ask",
    )(queries, new_keys, new_values)


def order_kernel(dest, lens, rest, keys, values, large, small, table, kbuf, vbuf, sems):
    n, length, _ = keys.shape
    part = length - small.shape[1]
    group = lax.axis_index("group")
    table[5, 0] = lax.axis_index("tensor") ^ group
    for j in range(n):
        d = dest[group * n + j] // n
        table[0, d] = j
        table[1, d] = lens[group * n + j]
        table[2, d] = rest[group * n + j]

    def fetch(d):
        j = table[0, d]
        return (
            pltpu.make_async_copy(keys.at[j], kbuf.at[d], sems.at[0, d]),
            pltpu.make_async_copy(values.at[j], vbuf.at[d], sems.at[1, d]),
        )

    def store(d):
        return (
            pltpu.make_async_copy(kbuf.at[d], large.at[d, pl.ds(0, length)], sems.at[2, d]),
            pltpu.make_async_copy(
                vbuf.at[d, pl.ds(0, part)], large.at[d, pl.ds(length, part)], sems.at[3, d]
            ),
            pltpu.make_async_copy(
                vbuf.at[d, pl.ds(part, length - part)], small.at[d], sems.at[4, d]
            ),
        )

    for d in range(n):
        for c in fetch(d):
            c.start()

    def note(s, _):
        place = s * n
        for j in range(n):
            place = jnp.where(dest[s * n + j] // n == group, s * n + j, place)
        table[3, s] = lens[place]
        table[4, s] = rest[place]
        return 0

    lax.fori_loop(0, n, note, 0)
    for d in range(n):
        for c in fetch(d):
            c.wait()
        for c in store(d):
            c.start()
    for d in range(n):
        for c in store(d):
            c.wait()


def order_cache(dest, lens, rest, keys, values, part):
    n, length, width = keys.shape
    sm = pl.BlockSpec(memory_space=pltpu.SMEM)
    hbm = pl.BlockSpec(memory_space=pl.ANY)
    return pl.pallas_call(
        order_kernel,
        out_shape=(
            jax.ShapeDtypeStruct((n, length + part, width), keys.dtype),
            jax.ShapeDtypeStruct((n, length - part, width), keys.dtype),
            jax.ShapeDtypeStruct((6, n), jnp.int32),
        ),
        in_specs=[sm, sm, sm, hbm, hbm],
        out_specs=(hbm, hbm, sm),
        scratch_shapes=[
            pltpu.VMEM(keys.shape, keys.dtype),
            pltpu.VMEM(values.shape, values.dtype),
            pltpu.SemaphoreType.DMA((5, n)),
        ],
        compiler_params=pltpu.CompilerParams(vmem_limit_bytes=60 * 1024 * 1024),
        cost_estimate=pl.CostEstimate(
            flops=0, bytes_accessed=8 * keys.size, transcendentals=0
        ),
        name="order_cache",
    )(dest, lens, rest, keys, values)


def attend_kernel(turn, table, msg, keys, values, weight, keep, near, far, att, kbuf, vbuf, wbuf, sems):
    t = table[5, 0]
    n = kbuf.shape[0]
    wcopy = pltpu.make_async_copy(weight, wbuf, sems.at[2, 0])

    def fetch(p):
        j = table[0, t ^ ORDER[p]]
        return (
            pltpu.make_async_copy(keys.at[j], kbuf.at[p], sems.at[0, p]),
            pltpu.make_async_copy(values.at[j], vbuf.at[p], sems.at[1, p]),
        )

    for p in range(n):
        for c in fetch(p):
            c.start()
    wcopy.start()
    col = lax.broadcasted_iota(jnp.int32, (16, keys.shape[1]), 1)
    row8 = lax.broadcasted_iota(jnp.int32, (16, 8), 0) % 4
    col8 = lax.broadcasted_iota(jnp.int32, (16, 8), 1)
    rowd = lax.broadcasted_iota(jnp.int32, (16, 128), 0) % 4
    scale = 128 ** (-0.5)
    nt = (((1,), (1,)), ((), ()))
    batch = 4
    for start in range(0, n, batch):
        ps = range(start, start + batch)
        for p in ps:
            for cp in fetch(p):
                cp.wait()
        cs = [t ^ ORDER[p] for p in ps]
        qs = [msg[c, 0:16, :] for c in cs]
        nks = [msg[c, 16:24, :] for c in cs]
        nvs = [msg[c, 24:32, :] for c in cs]
        s1 = [lax.dot_general(q, kbuf[p], nt, preferred_element_type=f32) for q, p in zip(qs, ps)]
        s2 = [lax.dot_general(q, k, nt, preferred_element_type=f32) for q, k in zip(qs, nks)]
        s1 = [jnp.where(col < table[1, c], s * scale, neg_fill) for s, c in zip(s1, cs)]
        s2 = [jnp.where(col8 <= row8, s * scale, neg_fill) for s in s2]
        m1 = [jnp.max(s, axis=1, keepdims=True) for s in s1]
        m2 = [jnp.max(s, axis=1, keepdims=True) for s in s2]
        p1 = [jnp.exp(s - m) for s, m in zip(s1, m1)]
        p2 = [jnp.exp(s - m) for s, m in zip(s2, m2)]
        o1 = [
            jnp.dot(w.astype(bf16), vbuf[p], preferred_element_type=f32) for w, p in zip(p1, ps)
        ]
        o2 = [
            jnp.dot(w.astype(bf16), v, preferred_element_type=f32) for w, v in zip(p2, nvs)
        ]
        l1 = [jnp.sum(w, axis=1, keepdims=True) for w in p1]
        l2 = [jnp.sum(w, axis=1, keepdims=True) for w in p2]
        for i, p in enumerate(ps):
            top = jnp.maximum(m1[i], m2[i])
            e1 = jnp.exp(m1[i] - top)
            e2 = jnp.exp(m2[i] - top)
            o = (e1 * o1[i] + e2 * o2[i]) / (e1 * l1[i] + e2 * l2[i])
            o = jnp.where(rowd < table[2, cs[i]], o, 0.0)
            for h in range(4):
                att[4 * p : 4 * p + 4, 128 * h : 128 * h + 128] = o[4 * h : 4 * h + 4, :]
    wcopy.wait()
    a = att[...].astype(bf16)
    rows = a.shape[0]
    width = wbuf.shape[1]
    step = 512
    for k in range(0, width, step):
        y = jnp.dot(a, wbuf[:, k : k + step], preferred_element_type=f32)
        keep[:, k : k + step] = y[: rows // 2]
        near[:, k : k + step] = y[rows // 2 : rows * 3 // 4].astype(bf16)
        far[:, k : k + step] = y[rows * 3 // 4 :].astype(bf16)


def attend(turn, table, msg, keys, values, weight):
    n = msg.shape[0]
    depth, out_width = weight.shape
    vm = pl.BlockSpec(memory_space=pltpu.VMEM)
    sm = pl.BlockSpec(memory_space=pltpu.SMEM)
    hbm = pl.BlockSpec(memory_space=pl.ANY)
    return pl.pallas_call(
        attend_kernel,
        out_shape=(
            jax.ShapeDtypeStruct((2 * n, out_width), f32),
            jax.ShapeDtypeStruct((n, out_width), bf16),
            jax.ShapeDtypeStruct((n, out_width), bf16),
        ),
        in_specs=[sm, sm, vm, hbm, hbm, hbm],
        out_specs=(vm, vm, vm),
        scratch_shapes=[
            pltpu.VMEM((4 * n, depth), f32),
            pltpu.VMEM(keys.shape, bf16),
            pltpu.VMEM(values.shape, bf16),
            pltpu.VMEM((depth, out_width), bf16),
            pltpu.SemaphoreType.DMA((3, n)),
        ],
        compiler_params=pltpu.CompilerParams(vmem_limit_bytes=48 * 1024 * 1024),
        cost_estimate=pl.CostEstimate(
            flops=4 * n * 16 * 512 * 128 + 2 * 4 * n * depth * out_width,
            bytes_accessed=4 * keys.size + 2 * weight.size,
            transcendentals=0,
        ),
        name="attend",
    )(turn, table, msg, keys, values, weight)


def place_kernel(table, fresh, *refs):
    *got, out, rows = refs
    count, total, _ = out.shape

    @pl.when(pl.program_id(0) == 0)
    def _():
        rows[...] = fresh[...].astype(f32)

    slots = [pl.program_id(0) * count + b for b in range(count)]
    lengths = [table[3, s] for s in slots]
    rests = [table[4, s] for s in slots]
    helds = [jnp.where(r > 0, l, 0) for l, r in zip(lengths, rests)]
    step = 32
    for b in range(count):
        base = 0
        for piece in got:
            for k in range(0, piece.shape[1], step):
                block = piece[b, k : k + step, :]
                out[b, base : base + step, :] = jnp.where(
                    base < helds[b], block, jnp.zeros((), block.dtype)
                )
                base += step
    starts = [pl.multiple_of(jnp.minimum(l // 16 * 16, total - 32), 16) for l in lengths]
    windows = [out[b, pl.ds(start, 32), :].astype(f32) for b, start in enumerate(starts)]
    news = [[rows[u, pl.ds(s, 1), :] for u in range(fresh.shape[0])] for s in slots]
    place_in = lax.broadcasted_iota(jnp.int32, windows[0].shape, 0)
    for b in range(count):
        inner = place_in + starts[b]
        window = jnp.where(inner < helds[b], windows[b], 0.0)
        for u, row in enumerate(news[b]):
            spot = jnp.where(rests[b] > u, lengths[b] + u, -1)
            window = jnp.where(inner == spot, row, window)
        windows[b] = window.astype(bf16)
    for b, start in enumerate(starts):
        out[b, pl.ds(start, 32), :] = windows[b]


def place(table, fresh, *pieces):
    n, _, width = pieces[0][0].shape
    length = sum(rows for _, _, rows in pieces)
    count = 4
    return pl.pallas_call(
        place_kernel,
        out_shape=jax.ShapeDtypeStruct((n, length, width), bf16),
        grid=(n // count,),
        in_specs=[
            pl.BlockSpec(memory_space=pltpu.SMEM),
            pl.BlockSpec(fresh.shape, lambda i: (0, 0, 0)),
        ]
        + [
            pl.BlockSpec((count, rows, width), functools.partial(lambda k, i: (i, k, 0), first // rows))
            for _, first, rows in pieces
        ],
        out_specs=pl.BlockSpec((count, length, width), lambda i: (i, 0, 0)),
        scratch_shapes=[pltpu.VMEM(fresh.shape, f32)],
        compiler_params=pltpu.CompilerParams(vmem_limit_bytes=8 * 1024 * 1024),
        cost_estimate=pl.CostEstimate(
            flops=0, bytes_accessed=4 * n * length * width, transcendentals=0
        ),
        name="place",
    )(table, fresh, *[array for array, _, _ in pieces])


def finish_kernel(table, first, second, third, fourth, residual, gain, out, normed, sums, squares):
    t = table[5, 0]
    rows = residual.shape[0]
    row = lax.broadcasted_iota(jnp.int32, (rows, rows), 0)
    col = lax.broadcasted_iota(jnp.int32, (rows, rows), 1)
    i = col // 4
    turned = (i & 1) * 8 + (i // 2 & 1) * 4 + (i // 4 & 1) * 2 + (i // 8 & 1)
    target = (col % 4) * 16 + (t ^ turned)
    pick = jnp.where(row == target, 1.0, 0.0).astype(bf16)
    step = 512
    total = jnp.zeros((rows, 128), f32)
    for k in range(0, residual.shape[1], step):
        cut = slice(k, k + step)
        piece = jnp.concatenate([x[:, cut] for x in (first, second, third, fourth)], axis=0)
        level = residual[:, cut].astype(f32) + jnp.dot(pick, piece, preferred_element_type=f32)
        out[:, cut] = level.astype(bf16)
        sums[:, cut] = level
        sq = level * level
        for j in range(0, step, 128):
            total = total + sq[:, j : j + 128]
    mean = jnp.sum(total, axis=1, keepdims=True) / residual.shape[1]
    factor = lax.rsqrt(mean + eps)
    for k in range(0, residual.shape[1], step):
        cut = slice(k, k + step)
        normed[:, cut] = (sums[:, cut] * factor * gain[:, cut].astype(f32)).astype(bf16)


def finish(table, first, second, third, fourth, residual, gain):
    rows, width = residual.shape
    vm = pl.BlockSpec(memory_space=pltpu.VMEM)
    return pl.pallas_call(
        finish_kernel,
        out_shape=(jax.ShapeDtypeStruct((rows, width), bf16),) * 2,
        in_specs=[pl.BlockSpec(memory_space=pltpu.SMEM)] + [vm] * 6,
        out_specs=(vm, vm),
        scratch_shapes=[pltpu.VMEM((rows, width), f32), pltpu.VMEM((rows, 128), f32)],
        compiler_params=pltpu.CompilerParams(vmem_limit_bytes=16 * 1024 * 1024),
        cost_estimate=pl.CostEstimate(
            flops=2 * rows * rows * width, bytes_accessed=8 * rows * width, transcendentals=0
        ),
        name="finish",
    )(table, first, second, third, fourth, residual, gain)


def swap(x, mask):
    return lax.ppermute(x, "tensor", [(t, t ^ mask) for t in range(16)])


def hand_over(x, mask):
    return lax.ppermute(
        x,
        ("group", "tensor"),
        [(g * 16 + t, (g ^ t) * 16 + (t ^ mask)) for g in range(16) for t in range(16)],
    )


def on_device(
    queries,
    new_keys,
    new_values,
    key_cache,
    value_cache,
    cache_len,
    remaining,
    dest_table,
    residual_in,
    out_weight,
    norm_gain,
):
    steps, n, heads, width = queries.shape
    out_width = out_weight.shape[1]
    fresh_keys = new_keys[:, :, 0, :]
    fresh_values = new_values[:, :, 0, :]
    msg = ask(queries, fresh_keys, fresh_values)
    msg = lax.all_to_all(msg, "group", split_axis=0, concat_axis=0, tiled=True)
    old_keys, old_values = key_cache[:, 0], value_cache[:, 0]
    part = 64
    large, small, table = order_cache(
        dest_table, cache_len, remaining, old_keys, old_values, part
    )
    large = lax.all_to_all(large, "group", split_axis=0, concat_axis=0, tiled=True)

    def first_steps(turn):
        keep, near, far = attend(turn[None], table, msg, old_keys, old_values, out_weight)
        far, near = swap(far, 1), swap(near, 1)
        s = keep[16:] + far.astype(f32)
        s = keep[:16] + near.astype(f32) + swap(s.astype(bf16), 2).astype(f32)
        s = s[:8] + swap(s[8:].astype(bf16), 4).astype(f32)
        return s[:4], s[4:].astype(bf16)

    def no_steps(turn):
        return jnp.zeros((4, out_width), f32), jnp.zeros((4, out_width), bf16)

    tensor = lax.axis_index("tensor")
    s, send = lax.cond(tensor >= 0, first_steps, no_steps, tensor)
    s, send, large = lax.optimization_barrier((s, send, large))
    s = s + swap(send, 8).astype(f32)
    s = s.astype(bf16)
    first = jnp.concatenate([hand_over(s, m) for m in (0, 8)], axis=0)
    first, small = lax.optimization_barrier((first, small))
    small = lax.all_to_all(small, "group", split_axis=0, concat_axis=0, tiled=True)
    first = jnp.concatenate([first, swap(first, 4)], axis=0)
    second = swap(first, 2)
    third = swap(first, 1)
    fourth = swap(second, 1)
    length = old_keys.shape[1]
    key_out = place(table, fresh_keys, (large, 0, length))
    value_out = place(table, fresh_values, (large, length, part), (small, 0, length - part))
    fourth, value_out = lax.optimization_barrier((fourth, value_out))
    residual_out, normed = finish(
        table,
        first,
        second,
        third,
        fourth,
        residual_in.reshape(steps * n, out_width),
        norm_gain.reshape(1, out_width),
    )
    return (
        residual_out.reshape(steps, n, out_width),
        normed.reshape(steps, n, out_width),
        key_out[:, None],
        value_out[:, None],
    )


def solution(mesh):
    placed = (
        P(None, "group", "tensor", None),
        P(None, "group", "tensor", None),
        P(None, "group", "tensor", None),
        P("group", "tensor", None, None),
        P("group", "tensor", None, None),
        P(),
        P(),
        P(),
        P(None, "group", None),
        P("tensor", None),
        P(),
    )
    return jax.shard_map(
        on_device,
        mesh=mesh,
        in_specs=placed,
        out_specs=(
            P(None, "group", None),
            P(None, "group", None),
            P("group", "tensor", None, None),
            P("group", "tensor", None, None),
        ),
        check_vma=False,
    )
```

time: 292 us -> 106 us (0.36)
  Pallas kernels: 163 us -> 22.8 us
  waiting for transfers between devices: 73.1 us -> 35.4 us
  local copies, waits for them, and re-layouts: 8 us -> 0.09 us
  starting transfers between devices: 41.8 us -> 44.9 us
    pallas_call x3 -> x4, Pallas kernels: 149 us -> 14.4 us  [the longest x2 7.08 us: place(): pl.pallas_call(place_kernel, out_shape=jax.ShapeDtypeStruct((n, length, w...]
    ppermute x6 -> x9, waiting for transfers between devices: 50.9 us -> 32 us  [swap(): return lax.ppermute(x, 'tensor', [(t, t ^ mask) for t in range(16)])]
    ppermute x4 -> x2, waiting for transfers between devices: 18.4 us -> 3.45 us  [hand_over(): lax.ppermute(x, ('group', 'tensor'), [(g * 16 + t, (g ^ t) * 16 + (t ^ ma...]
    ppermute x6 -> x9, starting transfers between devices: 13.1 us -> 24.9 us  [swap(): return lax.ppermute(x, 'tensor', [(t, t ^ mask) for t in range(16)])]
    ppermute x4 -> x2, starting transfers between devices: 12 us -> 3.18 us  [hand_over(): lax.ppermute(x, ('group', 'tensor'), [(g * 16 + t, (g ^ t) * 16 + (t ^ ma...]
    pallas_call x1, Pallas kernels: 11.9 us -> 5.93 us  [attend(): pl.pallas_call(attend_kernel, out_shape=(jax.ShapeDtypeStruct((2 * n, out...]
    unnamed x12 -> x9, local copies, waits for them, and re-layouts: 3.95 us -> 0.03 us
    all_to_all x2, waiting for transfers between devices: 3.87 us -> 0.01 us  [the longest x1 0.01 us: on_device(): lax.all_to_all(large, 'group', split_axis=0, concat_axis=0, tiled=True)]
  transfers between devices with their start and end apart: 13 -> 14, of which waited for: 9 -> 8; matrix products, arithmetic and copies ran while one was open for 1% -> 0% of each run, Pallas kernels for 49% -> 18%
where the time goes in v2:
time: 106 us; the launch traced here: 104 us
  starting transfers between devices  44.9 us (42%)
  waiting for transfers between devices  35.4 us (33%)
  Pallas kernels  22.8 us (22%)
    ppermute x9, waiting for transfers between devices, swap(): return lax.ppermute(x, 'tensor', [(t, t ^ mask) for t in range(16)])  32 us
    ppermute x9, starting transfers between devices, swap(): return lax.ppermute(x, 'tensor', [(t, t ^ mask) for t in range(16)])  24.9 us
    pallas_call x2, Pallas kernels, place(): pl.pallas_call(place_kernel, out_shape=jax.ShapeDtypeStruct((n, length, w...  7.08 us
    pallas_call x1, Pallas kernels, attend(): pl.pallas_call(attend_kernel, out_shape=(jax.ShapeDtypeStruct((2 * n, out...  5.93 us
    all_to_all x1, starting transfers between devices, on_device(): msg = lax.all_to_all(msg, 'group', split_axis=0, concat_axis=0, tiled=True)  5.78 us
    all_to_all x1, starting transfers between devices, on_device(): lax.all_to_all(large, 'group', split_axis=0, concat_axis=0, tiled=True)  5.73 us
    pallas_call x1, Pallas kernels, order_cache(): pl.pallas_call(order_kernel, out_shape=(jax.ShapeDtypeStruct((n, length +...  5.65 us
    all_to_all x1, starting transfers between devices, on_device(): lax.all_to_all(small, 'group', split_axis=0, concat_axis=0, tiled=True)  5.38 us
  transfers between devices with their start and end apart: 14, of which 8 were waited for; matrix products, arithmetic and copies ran while one was open for 0% of the time, Pallas kernels for 18%

profile of v2, /device:TPU:24, one launch (start us, length us, event | category | flops | bytes accessed | tf_op | source)
XLA Modules:
  0.0 104.2 jit_solution(14009806170602926053)
XLA Ops:
  0.6 1.7 %ask.1 = bf16[16,32,128]{2,1,0:T(8,128)(2,1)} custom-call(bf16[4,16,4,128]{3,2,1,0:T(4,128)(2,1)} %queries.1, bf16[4,16,128]{2,1,0:T(8,128)(2,1)} %bitcast.15, bf16[4,16,128]{2,1,0:T(8,128)(2,1)} %bitcast.17), custom_call_target="tpu_custom_call" | custom-call | bytes 400000 | tf_op jit(solution)/shard_map/ask/pallas_call | solution.py:35
  2.3 5.8 %all-to-all-start = ((bf16[16,32,128]{2,1,0:T(8,128)(2,1)}), bf16[16,32,128]{2,1,0:T(8,128)(2,1)S(1)}, u32[]{:S(2)}, u32[]{:S(2)}) async-start(bf16[16,32,128]{2,1,0:T(8,128)(2,1)} %ask.1), calls=%async_computation | async-start | bytes 262144 | tf_op jit(solution)/shard_map/all_to_all | solution.py:365
  8.1 5.7 %order_cache.1 = (bf16[16,576,128]{2,1,0:T(8,128)(2,1)}, bf16[16,448,128]{2,1,0:T(8,128)(2,1)}, s32[6,16]{1,0:T(8,128)S(1)}) custom-call(s32[256]{0:T(256)} %dest.1, s32[256]{0:T(256)} %lens.1, s32[256]{0:T(256)} %rest.1, bf16[16,512,128]{2,1,0:T(8,128)(2,1)} %bitcast.19, bf16[16,512,128]{2,1,0:T(8,128)(2,1)} %bitcast.21), custom_call_target="tpu_custom_call" | custom-call | bytes 8388608 | tf_op jit(solution)/shard_map/order_cache/pallas_call | solution.py:106
  13.8 0.0 all-to-all-done
  13.8 5.7 %all-to-all-start.1 = ((bf16[16,576,128]{2,1,0:T(8,128)(2,1)}), bf16[16,576,128]{2,1,0:T(8,128)(2,1)S(1)}, u32[]{:S(2)}, u32[]{:S(2)}) async-start(bf16[16,576,128]{2,1,0:T(8,128)(2,1)} %get-tuple-element.42), calls=%async_computation.1 | async-start | bytes 4718592 | tf_op jit(solution)/shard_map/all_to_all | solution.py:371
  19.5 32.6 %conditional.1 = (f32[4,5120]{1,0:T(4,128)S(1)}, bf16[4,5120]{1,0:T(4,128)(2,1)S(1)}) conditional(s32[]{:T(128)} %convert_element_type.26, () %tuple.19, (s32[]{:T(128)}, s32[6,16]{1,0:T(8,128)S(1)}, bf16[16,32,128]{2,1,0:T(8,128)(2,1)S(1)}, bf16[16,512,128]{2,1,0:T(8,128)(2,1)}, bf16[16,512,128]{2,1,0:T(8,128)(2,1)}, ...), branch_computations={%region_0.0_spmd, %region_1.0_spmd} | conditional | flops 403308544 | bytes 14188720 | solution.py:385
  19.5 5.9 %attend.1 = (f32[32,5120]{1,0:T(8,128)S(1)}, bf16[16,5120]{1,0:T(8,128)(2,1)S(1)}, bf16[16,5120]{1,0:T(8,128)(2,1)S(1)}) custom-call(s32[1]{0:T(128)} %bitcast.turn, s32[6,16]{1,0:T(8,128)S(1)} %get-tuple-element.13.table, bf16[16,32,128]{2,1,0:T(8,128)(2,1)S(1)} %get-tuple-element.14.msg, bf16[16,512,128]{2,1,0:T(8,128)(2,1)} %get-tuple-element.15.keys, ...), custom_call_target="tpu_custom_call" | custom-call | flops 402653184 | bytes 9437184 | tf_op jit(solution)/shard_map/cond/branch_1_fun/attend/pallas_call | solution.py:202
  25.5 2.0 %collective-permute-start.1 = (bf16[16,5120]{1,0:T(8,128)(2,1)S(1)}, bf16[16,5120]{1,0:T(8,128)(2,1)S(1)}, u32[]{:S(2)}, u32[]{:S(2)}) collective-permute-start(bf16[16,5120]{1,0:T(8,128)(2,1)S(1)} %get-tuple-element.20), channel_id=1, source_target_pairs={{0,1},{1,0},{2,3},{3,2},{4,5},{5,4},{6,7},{7,6},{8,9},{9,8},{10,11... | collective-permute-start | bytes 491528 | tf_op jit(solution)/shard_map/cond/branch_1_fun/ppermute | solution.py:336
  27.5 0.1 collective-permute-start
  27.6 5.0 %collective-permute-done.1 = bf16[16,5120]{1,0:T(8,128)(2,1)S(1)} collective-permute-done((bf16[16,5120]{1,0:T(8,128)(2,1)S(1)}, bf16[16,5120]{1,0:T(8,128)(2,1)S(1)}, u32[]{:S(2)}, u32[]{:S(2)}) %collective-permute-start.1) | collective-permute-done | bytes 163872 | tf_op jit(solution)/shard_map/cond/branch_1_fun/ppermute | solution.py:336
  32.6 3.4 %collective-permute-start.2 = (bf16[16,5120]{1,0:T(8,128)(2,1)S(1)}, bf16[16,5120]{1,0:T(8,128)(2,1)S(1)}, u32[]{:S(2)}, u32[]{:S(2)}) collective-permute-start(bf16[16,5120]{1,0:T(8,128)(2,1)S(1)} %add_convert_fusion), channel_id=1, source_target_pairs={{0,2},{1,3},{2,0},{3,1},{4,6},{5,7},{6,4},{7,5},{8,10},{9,11},{10,... | collective-permute-start | bytes 491528 | tf_op jit(solution)/shard_map/cond/branch_1_fun/ppermute | solution.py:336
  36.0 0.0 collective-permute-done
  36.0 6.8 %collective-permute-done.2 = bf16[16,5120]{1,0:T(8,128)(2,1)S(1)} collective-permute-done((bf16[16,5120]{1,0:T(8,128)(2,1)S(1)}, bf16[16,5120]{1,0:T(8,128)(2,1)S(1)}, u32[]{:S(2)}, u32[]{:S(2)}) %collective-permute-start.2) | collective-permute-done | bytes 163872 | tf_op jit(solution)/shard_map/cond/branch_1_fun/ppermute | solution.py:336
  42.8 6.3 %collective-permute-start.3 = (bf16[8,5120]{1,0:T(8,128)(2,1)S(1)}, bf16[8,5120]{1,0:T(8,128)(2,1)S(1)}, u32[]{:S(2)}, u32[]{:S(2)}) collective-permute-start(bf16[8,5120]{1,0:T(8,128)(2,1)S(1)} %slice.29), channel_id=1, source_target_pairs={{0,4},{1,5},{2,6},{3,7},{4,0},{5,1},{6,2},{7,3},{8,12},{9,13},{10,... | collective-permute-start | bytes 245768 | tf_op jit(solution)/shard_map/cond/branch_1_fun/ppermute | solution.py:336
  49.1 3.0 %collective-permute-done.3 = bf16[8,5120]{1,0:T(8,128)(2,1)S(1)} collective-permute-done((bf16[8,5120]{1,0:T(8,128)(2,1)S(1)}, bf16[8,5120]{1,0:T(8,128)(2,1)S(1)}, u32[]{:S(2)}, u32[]{:S(2)}) %collective-permute-start.3) | collective-permute-done | bytes 81952 | tf_op jit(solution)/shard_map/cond/branch_1_fun/ppermute | solution.py:336
  52.2 1.3 %collective-permute-start.4 = (bf16[4,5120]{1,0:T(4,128)(2,1)S(1)}, bf16[4,5120]{1,0:T(4,128)(2,1)S(1)}, u32[]{:S(2)}, u32[]{:S(2)}) collective-permute-start(bf16[4,5120]{1,0:T(4,128)(2,1)S(1)} %get-tuple-element.44), channel_id=1, source_target_pairs={{0,8},{1,9},{2,10},{3,11},{4,12},{5,13},{6,14},{7,15},{8,0},{9,1},... | collective-permute-start | bytes 122888 | tf_op jit(solution)/shard_map/ppermute | solution.py:336
  53.5 4.3 %collective-permute-done.4 = bf16[4,5120]{1,0:T(4,128)(2,1)S(1)} collective-permute-done((bf16[4,5120]{1,0:T(4,128)(2,1)S(1)}, bf16[4,5120]{1,0:T(4,128)(2,1)S(1)}, u32[]{:S(2)}, u32[]{:S(2)}) %collective-permute-start.4) | collective-permute-done | bytes 40992 | tf_op jit(solution)/shard_map/ppermute | solution.py:336
  57.8 0.0 copy-start.3
  57.8 0.0 copy-start.1
  57.8 0.8 collective-permute-start.6
  58.6 2.4 %collective-permute-start.5 = (bf16[4,5120]{1,0:T(4,128)(2,1)S(1)}, bf16[4,5120]{1,0:T(4,128)(2,1)S(1)}, u32[]{:S(2)}, u32[]{:S(2)}) collective-permute-start(bf16[4,5120]{1,0:T(4,128)(2,1)S(1)} %add_convert_fusion.1), channel_id=1, source_target_pairs={{0,0},{1,17},{2,34},{3,51},{4,68},{5,85},{6,102},{7,119},{8,136},{... | collective-permute-start | bytes 122888 | tf_op jit(solution)/shard_map/ppermute | solution.py:340
  61.0 2.4 %collective-permute-done.6 = bf16[4,5120]{1,0:T(4,128)(2,1)S(1)} collective-permute-done((bf16[4,5120]{1,0:T(4,128)(2,1)S(1)}, bf16[4,5120]{1,0:T(4,128)(2,1)S(1)}, u32[]{:S(2)}, u32[]{:S(2)}) %collective-permute-start.6) | collective-permute-done | bytes 40992 | tf_op jit(solution)/shard_map/ppermute | solution.py:340
  63.4 1.1 %collective-permute-done.5 = bf16[4,5120]{1,0:T(4,128)(2,1)S(1)} collective-permute-done((bf16[4,5120]{1,0:T(4,128)(2,1)S(1)}, bf16[4,5120]{1,0:T(4,128)(2,1)S(1)}, u32[]{:S(2)}, u32[]{:S(2)}) %collective-permute-start.5) | collective-permute-done | bytes 40992 | tf_op jit(solution)/shard_map/ppermute | solution.py:340
  64.5 5.4 %all-to-all-start.2 = ((bf16[16,448,128]{2,1,0:T(8,128)(2,1)}), bf16[16,448,128]{2,1,0:T(8,128)(2,1)}, u32[]{:S(2)}, u32[]{:S(2)}) async-start(bf16[16,448,128]{2,1,0:T(8,128)(2,1)} %get-tuple-element.48), calls=%async_computation.2 | async-start | bytes 3670016 | tf_op jit(solution)/shard_map/all_to_all | solution.py:391
  69.9 9.8 %collective-permute-start.7 = (bf16[8,5120]{1,0:T(8,128)(2,1)S(1)}, bf16[8,5120]{1,0:T(8,128)(2,1)S(1)}, u32[]{:S(2)}, u32[]{:S(2)}) collective-permute-start(bf16[8,5120]{1,0:T(8,128)(2,1)S(1)} %pad_maximum_fusion), channel_id=1, source_target_pairs={{0,4},{1,5},{2,6},{3,7},{4,0},{5,1},{6,2},{7,3},{8,12},{9,13},{10,... | collective-permute-start | bytes 245768 | tf_op jit(solution)/shard_map/ppermute | solution.py:336
  79.7 2.7 %collective-permute-done.7 = bf16[8,5120]{1,0:T(8,128)(2,1)S(1)} collective-permute-done((bf16[8,5120]{1,0:T(8,128)(2,1)S(1)}, bf16[8,5120]{1,0:T(8,128)(2,1)S(1)}, u32[]{:S(2)}, u32[]{:S(2)}) %collective-permute-start.7) | collective-permute-done | bytes 81952 | tf_op jit(solution)/shard_map/ppermute | solution.py:336
  82.4 10.1 %collective-permute-done.8.second = bf16[16,5120]{1,0:T(8,128)(2,1)S(1)} collective-permute-done((bf16[16,5120]{1,0:T(8,128)(2,1)S(1)}, bf16[16,5120]{1,0:T(8,128)(2,1)S(1)}, u32[]{:S(2)}, u32[]{:S(2)}) %collective-permute-start.8) | collective-permute-done | bytes 163872 | tf_op jit(solution)/shard_map/ppermute | solution.py:336
  92.6 2.0 %collective-permute-start.9 = (bf16[16,5120]{1,0:T(8,128)(2,1)S(1)}, bf16[16,5120]{1,0:T(8,128)(2,1)}, u32[]{:S(2)}, u32[]{:S(2)}) collective-permute-start(bf16[16,5120]{1,0:T(8,128)(2,1)S(1)} %constant_dynamic-update-slice_fusion.first), channel_id=1, source_target_pairs={{0,1},{1,0},{2,3},{3,2},{4,5},{5,4},{6,7},{7,6},{8,9},{9,8},{10,11... | collective-permute-start | bytes 491528 | tf_op jit(solution)/shard_map/ppermute | solution.py:336
  94.6 0.0 copy-start.2
  94.7 2.9 %place.3 = bf16[16,512,128]{2,1,0:T(8,128)(2,1)} custom-call(s32[6,16]{1,0:T(8,128)S(1)} %get-tuple-element.39.table, bf16[4,16,128]{2,1,0:T(8,128)(2,1)S(1)} %bitcast.16, bf16[16,576,128]{2,1,0:T(8,128)(2,1)S(1)} %all-to-all-done.1.refs_0_), custom_call_target="tpu_custom_call" | custom-call | bytes 4194304 | tf_op jit(solution)/shard_map/place/pallas_call | solution.py:269
  97.6 4.2 %place.2 = bf16[16,512,128]{2,1,0:T(8,128)(2,1)} custom-call(s32[6,16]{1,0:T(8,128)S(1)} %get-tuple-element.39.table, bf16[4,16,128]{2,1,0:T(8,128)(2,1)S(1)} %bitcast.18, bf16[16,576,128]{2,1,0:T(8,128)(2,1)S(1)} %all-to-all-done.1.refs_0_, bf16[16,448,128]{2,1,0:T(8,128)(2,1)} %all-to-all-done.2.refs_1_), custom_call_target="tpu_custom_call" | custom-call | bytes 4194304 | tf_op jit(solution)/shard_map/place/pallas_call | solution.py:269
  101.8 2.4 %finish.1 = (bf16[64,5120]{1,0:T(8,128)(2,1)}, bf16[64,5120]{1,0:T(8,128)(2,1)}) custom-call(s32[6,16]{1,0:T(8,128)S(1)} %get-tuple-element.39.table, bf16[16,5120]{1,0:T(8,128)(2,1)S(1)} %constant_dynamic-update-slice_fusion.first, bf16[16,5120]{1,0:T(8,128)(2,1)S(1)} %collective-permute-done.8.second, bf16[16,5120]{1,0:T(8,128)(2,1)} %collective-permute-done.9.third, ...), custom_call_target="tpu_custom_call" | custom-call | flops 41943040 | bytes 2621440 | tf_op jit(solution)/shard_map/finish/pallas_call | solution.py:321
  (22 shorter events, 0.3 us)
Async XLA Ops:
  2.3 11.4 %all-to-all-start = ((bf16[16,32,128]{2,1,0:T(8,128)(2,1)}), bf16[16,32,128]{2,1,0:T(8,128)(2,1)S(1)}, u32[]{:S(2)}, u32[]{:S(2)}) async-start(bf16[16,32,128]{2,1,0:T(8,128)(2,1)} %ask.1), calls=%async_computation | async-start | bytes 262144 | tf_op jit(solution)/shard_map/all_to_all | solution.py:365
  13.8 38.4 %all-to-all-start.1 = ((bf16[16,576,128]{2,1,0:T(8,128)(2,1)}), bf16[16,576,128]{2,1,0:T(8,128)(2,1)S(1)}, u32[]{:S(2)}, u32[]{:S(2)}) async-start(bf16[16,576,128]{2,1,0:T(8,128)(2,1)} %get-tuple-element.42), calls=%async_computation.1 | async-start | bytes 4718592 | tf_op jit(solution)/shard_map/all_to_all | solution.py:371
  25.5 7.1 %collective-permute-start.1 = (bf16[16,5120]{1,0:T(8,128)(2,1)S(1)}, bf16[16,5120]{1,0:T(8,128)(2,1)S(1)}, u32[]{:S(2)}, u32[]{:S(2)}) collective-permute-start(bf16[16,5120]{1,0:T(8,128)(2,1)S(1)} %get-tuple-element.20), channel_id=1, source_target_pairs={{0,1},{1,0},{2,3},{3,2},{4,5},{5,4},{6,7},{7,6},{8,9},{9,8},{10,11... | collective-permute-start | bytes 491528 | tf_op jit(solution)/shard_map/cond/branch_1_fun/ppermute | solution.py:336
  27.5 8.5 %collective-permute-start = (bf16[16,5120]{1,0:T(8,128)(2,1)S(1)}, bf16[16,5120]{1,0:T(8,128)(2,1)S(1)}, u32[]{:S(2)}, u32[]{:S(2)}) collective-permute-start(bf16[16,5120]{1,0:T(8,128)(2,1)S(1)} %get-tuple-element.19), channel_id=1, source_target_pairs={{0,1},{1,0},{2,3},{3,2},{4,5},{5,4},{6,7},{7,6},{8,9},{9,8},{10,11... | collective-permute-start | bytes 491528 | tf_op jit(solution)/shard_map/cond/branch_1_fun/ppermute | solution.py:336
  32.6 10.2 %collective-permute-start.2 = (bf16[16,5120]{1,0:T(8,128)(2,1)S(1)}, bf16[16,5120]{1,0:T(8,128)(2,1)S(1)}, u32[]{:S(2)}, u32[]{:S(2)}) collective-permute-start(bf16[16,5120]{1,0:T(8,128)(2,1)S(1)} %add_convert_fusion), channel_id=1, source_target_pairs={{0,2},{1,3},{2,0},{3,1},{4,6},{5,7},{6,4},{7,5},{8,10},{9,11},{10,... | collective-permute-start | bytes 491528 | tf_op jit(solution)/shard_map/cond/branch_1_fun/ppermute | solution.py:336
  42.8 9.3 %collective-permute-start.3 = (bf16[8,5120]{1,0:T(8,128)(2,1)S(1)}, bf16[8,5120]{1,0:T(8,128)(2,1)S(1)}, u32[]{:S(2)}, u32[]{:S(2)}) collective-permute-start(bf16[8,5120]{1,0:T(8,128)(2,1)S(1)} %slice.29), channel_id=1, source_target_pairs={{0,4},{1,5},{2,6},{3,7},{4,0},{5,1},{6,2},{7,3},{8,12},{9,13},{10,... | collective-permute-start | bytes 245768 | tf_op jit(solution)/shard_map/cond/branch_1_fun/ppermute | solution.py:336
  52.2 5.6 %collective-permute-start.4 = (bf16[4,5120]{1,0:T(4,128)(2,1)S(1)}, bf16[4,5120]{1,0:T(4,128)(2,1)S(1)}, u32[]{:S(2)}, u32[]{:S(2)}) collective-permute-start(bf16[4,5120]{1,0:T(4,128)(2,1)S(1)} %get-tuple-element.44), channel_id=1, source_target_pairs={{0,8},{1,9},{2,10},{3,11},{4,12},{5,13},{6,14},{7,15},{8,0},{9,1},... | collective-permute-start | bytes 122888 | tf_op jit(solution)/shard_map/ppermute | solution.py:336
  57.8 36.8 %copy-start.3 = (bf16[5120]{0:T(1024)(128)(2,1)S(1)}, bf16[5120]{0:T(1024)(128)(2,1)}, u32[]{:S(2)}) copy-start(bf16[5120]{0:T(1024)(128)(2,1)} %param.23) | copy-start | bytes 30724
  57.8 36.8 %copy-start.1 = (bf16[4,16,1,128]{3,1,2,0:T(8,128)(2,1)S(1)}, bf16[4,16,1,128]{3,1,2,0:T(8,128)(2,1)}, u32[]{:S(2)}) copy-start(bf16[4,16,1,128]{3,1,2,0:T(8,128)(2,1)} %param.14) | copy-start | bytes 49156
  57.8 5.6 %collective-permute-start.6 = (bf16[4,5120]{1,0:T(4,128)(2,1)S(1)}, bf16[4,5120]{1,0:T(4,128)(2,1)S(1)}, u32[]{:S(2)}, u32[]{:S(2)}) collective-permute-start(bf16[4,5120]{1,0:T(4,128)(2,1)S(1)} %add_convert_fusion.1), channel_id=1, source_target_pairs={{0,8},{1,25},{2,42},{3,59},{4,76},{5,93},{6,110},{7,127},{8,128},{... | collective-permute-start | bytes 122888 | tf_op jit(solution)/shard_map/ppermute | solution.py:340
  58.6 5.9 %collective-permute-start.5 = (bf16[4,5120]{1,0:T(4,128)(2,1)S(1)}, bf16[4,5120]{1,0:T(4,128)(2,1)S(1)}, u32[]{:S(2)}, u32[]{:S(2)}) collective-permute-start(bf16[4,5120]{1,0:T(4,128)(2,1)S(1)} %add_convert_fusion.1), channel_id=1, source_target_pairs={{0,0},{1,17},{2,34},{3,51},{4,68},{5,85},{6,102},{7,119},{8,136},{... | collective-permute-start | bytes 122888 | tf_op jit(solution)/shard_map/ppermute | solution.py:340
  64.5 33.1 %all-to-all-start.2 = ((bf16[16,448,128]{2,1,0:T(8,128)(2,1)}), bf16[16,448,128]{2,1,0:T(8,128)(2,1)}, u32[]{:S(2)}, u32[]{:S(2)}) async-start(bf16[16,448,128]{2,1,0:T(8,128)(2,1)} %get-tuple-element.48), calls=%async_computation.2 | async-start | bytes 3670016 | tf_op jit(solution)/shard_map/all_to_all | solution.py:391
  69.9 12.5 %collective-permute-start.7 = (bf16[8,5120]{1,0:T(8,128)(2,1)S(1)}, bf16[8,5120]{1,0:T(8,128)(2,1)S(1)}, u32[]{:S(2)}, u32[]{:S(2)}) collective-permute-start(bf16[8,5120]{1,0:T(8,128)(2,1)S(1)} %pad_maximum_fusion), channel_id=1, source_target_pairs={{0,4},{1,5},{2,6},{3,7},{4,0},{5,1},{6,2},{7,3},{8,12},{9,13},{10,... | collective-permute-start | bytes 245768 | tf_op jit(solution)/shard_map/ppermute | solution.py:336
  82.4 10.2 %collective-permute-start.8 = (bf16[16,5120]{1,0:T(8,128)(2,1)S(1)}, bf16[16,5120]{1,0:T(8,128)(2,1)S(1)}, u32[]{:S(2)}, u32[]{:S(2)}) collective-permute-start(bf16[16,5120]{1,0:T(8,128)(2,1)S(1)} %constant_dynamic-update-slice_fusion.first), channel_id=1, source_target_pairs={{0,2},{1,3},{2,0},{3,1},{4,6},{5,7},{6,4},{7,5},{8,10},{9,11},{10,... | collective-permute-start | bytes 491528 | tf_op jit(solution)/shard_map/ppermute | solution.py:336
  92.6 9.2 %collective-permute-start.10 = (bf16[16,5120]{1,0:T(8,128)(2,1)S(1)}, bf16[16,5120]{1,0:T(8,128)(2,1)S(1)}, u32[]{:S(2)}, u32[]{:S(2)}) collective-permute-start(bf16[16,5120]{1,0:T(8,128)(2,1)S(1)} %collective-permute-done.8.second), channel_id=1, source_target_pairs={{0,1},{1,0},{2,3},{3,2},{4,5},{5,4},{6,7},{7,6},{8,9},{9,8},{10,11... | collective-permute-start | bytes 491528 | tf_op jit(solution)/shard_map/ppermute | solution.py:336
  92.6 9.2 %collective-permute-start.9 = (bf16[16,5120]{1,0:T(8,128)(2,1)S(1)}, bf16[16,5120]{1,0:T(8,128)(2,1)}, u32[]{:S(2)}, u32[]{:S(2)}) collective-permute-start(bf16[16,5120]{1,0:T(8,128)(2,1)S(1)} %constant_dynamic-update-slice_fusion.first), channel_id=1, source_target_pairs={{0,1},{1,0},{2,3},{3,2},{4,5},{5,4},{6,7},{7,6},{8,9},{9,8},{10,11... | collective-permute-start | bytes 491528 | tf_op jit(solution)/shard_map/ppermute | solution.py:336
  94.6 2.9 %copy-start.2 = (bf16[4,16,1,128]{3,1,2,0:T(8,128)(2,1)S(1)}, bf16[4,16,1,128]{3,1,2,0:T(8,128)(2,1)}, u32[]{:S(2)}) copy-start(bf16[4,16,1,128]{3,1,2,0:T(8,128)(2,1)} %param.15) | copy-start | bytes 49156
  97.6 4.2 %copy-start = (bf16[4,16,5120]{2,1,0:T(8,128)(2,1)S(1)}, bf16[4,16,5120]{2,1,0:T(8,128)(2,1)}, u32[]{:S(2)}) copy-start(bf16[4,16,5120]{2,1,0:T(8,128)(2,1)} %param.21) | copy-start | bytes 1966084

commit v3 on v2

--- a/solution.py
+++ b/solution.py
@@ -47,11 +47,21 @@
     )(queries, new_keys, new_values)
 
 
+def fold(t):
+    return t ^ (3 * (t // 4 % 2))
+
+
 def order_kernel(dest, lens, rest, keys, values, large, small, table, kbuf, vbuf, sems):
     n, length, _ = keys.shape
     part = length - small.shape[1]
+    rest_rows = large.shape[1] - part
+    share = length - rest_rows
+    both = length - 2 * share
     group = lax.axis_index("group")
-    table[5, 0] = lax.axis_index("tensor") ^ group
+    tensor = lax.axis_index("tensor")
+    table[5, 0] = fold(tensor) ^ group
+    table[5, 1] = tensor & 1
+    base = pl.multiple_of((tensor & 1) * share, 16)
     for j in range(n):
         d = dest[group * n + j] // n
         table[0, d] = j
@@ -61,15 +71,20 @@
     def fetch(d):
         j = table[0, d]
         return (
-            pltpu.make_async_copy(keys.at[j], kbuf.at[d], sems.at[0, d]),
+            pltpu.make_async_copy(
+                keys.at[j, pl.ds(base, share)], kbuf.at[d, pl.ds(0, share)], sems.at[0, d]
+            ),
+            pltpu.make_async_copy(
+                keys.at[j, pl.ds(2 * share, both)], kbuf.at[d, pl.ds(share, both)], sems.at[5, d]
+            ),
             pltpu.make_async_copy(values.at[j], vbuf.at[d], sems.at[1, d]),
         )
 
     def store(d):
         return (
-            pltpu.make_async_copy(kbuf.at[d], large.at[d, pl.ds(0, length)], sems.at[2, d]),
+            pltpu.make_async_copy(kbuf.at[d], large.at[d, pl.ds(part, rest_rows)], sems.at[2, d]),
             pltpu.make_async_copy(
-                vbuf.at[d, pl.ds(0, part)], large.at[d, pl.ds(length, part)], sems.at[3, d]
+                vbuf.at[d, pl.ds(0, part)], large.at[d, pl.ds(0, part)], sems.at[3, d]
             ),
             pltpu.make_async_copy(
                 vbuf.at[d, pl.ds(part, length - part)], small.at[d], sems.at[4, d]
@@ -99,23 +114,23 @@
             c.wait()
 
 
-def order_cache(dest, lens, rest, keys, values, part):
+def order_cache(dest, lens, rest, keys, values, part, share):
     n, length, width = keys.shape
     sm = pl.BlockSpec(memory_space=pltpu.SMEM)
     hbm = pl.BlockSpec(memory_space=pl.ANY)
     return pl.pallas_call(
         order_kernel,
         out_shape=(
-            jax.ShapeDtypeStruct((n, length + part, width), keys.dtype),
+            jax.ShapeDtypeStruct((n, part + length - share, width), keys.dtype),
             jax.ShapeDtypeStruct((n, length - part, width), keys.dtype),
             jax.ShapeDtypeStruct((6, n), jnp.int32),
         ),
         in_specs=[sm, sm, sm, hbm, hbm],
         out_specs=(hbm, hbm, sm),
         scratch_shapes=[
-            pltpu.VMEM(keys.shape, keys.dtype),
+            pltpu.VMEM((n, length - share, width), keys.dtype),
             pltpu.VMEM(values.shape, values.dtype),
-            pltpu.SemaphoreType.DMA((5, n)),
+            pltpu.SemaphoreType.DMA((6, n)),
         ],
         compiler_params=pltpu.CompilerParams(vmem_limit_bytes=60 * 1024 * 1024),
         cost_estimate=pl.CostEstimate(
@@ -128,7 +143,13 @@
 def attend_kernel(turn, table, msg, keys, values, weight, keep, near, far, att, kbuf, vbuf, wbuf, sems):
     t = table[5, 0]
     n = kbuf.shape[0]
-    wcopy = pltpu.make_async_copy(weight, wbuf, sems.at[2, 0])
+    width = wbuf.shape[1]
+    chunk = width // 5
+
+    def fetch_weight(k):
+        cut = pl.ds(k * chunk, chunk)
+        return pltpu.make_async_copy(weight.at[:, cut], wbuf.at[:, cut], sems.at[2, k])
+
 
     def fetch(p):
         j = table[0, t ^ ORDER[p]]
@@ -140,7 +161,8 @@
     for p in range(n):
         for c in fetch(p):
             c.start()
-    wcopy.start()
+    for k in range(5):
+        fetch_weight(k).start()
     col = lax.broadcasted_iota(jnp.int32, (16, keys.shape[1]), 1)
     row8 = lax.broadcasted_iota(jnp.int32, (16, 8), 0) % 4
     col8 = lax.broadcasted_iota(jnp.int32, (16, 8), 1)
@@ -181,16 +203,16 @@
             o = jnp.where(rowd < table[2, cs[i]], o, 0.0)
             for h in range(4):
                 att[4 * p : 4 * p + 4, 128 * h : 128 * h + 128] = o[4 * h : 4 * h + 4, :]
-    wcopy.wait()
     a = att[...].astype(bf16)
     rows = a.shape[0]
-    width = wbuf.shape[1]
     step = 512
     for k in range(0, width, step):
+        if k % chunk == 0:
+            fetch_weight(k // chunk).wait()
         y = jnp.dot(a, wbuf[:, k : k + step], preferred_element_type=f32)
         keep[:, k : k + step] = y[: rows // 2]
-        near[:, k : k + step] = y[rows // 2 : rows * 3 // 4].astype(bf16)
-        far[:, k : k + step] = y[rows * 3 // 4 :].astype(bf16)
+        near[:, k : k + step] = y[rows // 2 : rows * 7 // 8].astype(bf16)
+        far[:, k : k + step] = y[rows * 7 // 8 :].astype(bf16)
 
 
 def attend(turn, table, msg, keys, values, weight):
@@ -203,8 +225,8 @@
         attend_kernel,
         out_shape=(
             jax.ShapeDtypeStruct((2 * n, out_width), f32),
-            jax.ShapeDtypeStruct((n, out_width), bf16),
-            jax.ShapeDtypeStruct((n, out_width), bf16),
+            jax.ShapeDtypeStruct((n * 3 // 2, out_width), bf16),
+            jax.ShapeDtypeStruct((n // 2, out_width), bf16),
         ),
         in_specs=[sm, sm, vm, hbm, hbm, hbm],
         out_specs=(vm, vm, vm),
@@ -225,7 +247,7 @@
     )(turn, table, msg, keys, values, weight)
 
 
-def place_kernel(table, fresh, *refs):
+def place_kernel(bases, table, fresh, *refs):
     *got, out, rows = refs
     count, total, _ = out.shape
 
@@ -239,14 +261,16 @@
     helds = [jnp.where(r > 0, l, 0) for l, r in zip(lengths, rests)]
     step = 32
     for b in range(count):
-        base = 0
-        for piece in got:
+        for piece, (even, odd) in zip(got, bases):
+            base = even
+            if odd != even:
+                base = pl.multiple_of(even + table[5, 1] * (odd - even), 16)
             for k in range(0, piece.shape[1], step):
-                block = piece[b, k : k + step, :]
-                out[b, base : base + step, :] = jnp.where(
-                    base < helds[b], block, jnp.zeros((), block.dtype)
+                size = min(step, piece.shape[1] - k)
+                block = piece[b, k : k + size, :]
+                out[b, pl.ds(base + k, size), :] = jnp.where(
+                    base + k < helds[b], block, jnp.zeros((), block.dtype)
                 )
-                base += step
     starts = [pl.multiple_of(jnp.minimum(l // 16 * 16, total - 32), 16) for l in lengths]
     windows = [out[b, pl.ds(start, 32), :].astype(f32) for b, start in enumerate(starts)]
     news = [[rows[u, pl.ds(s, 1), :] for u in range(fresh.shape[0])] for s in slots]
@@ -264,10 +288,10 @@
 
 def place(table, fresh, *pieces):
     n, _, width = pieces[0][0].shape
-    length = sum(rows for _, _, rows in pieces)
+    length = sum(rows for _, _, rows, _ in pieces)
     count = 4
     return pl.pallas_call(
-        place_kernel,
+        functools.partial(place_kernel, tuple(bases for _, _, _, bases in pieces)),
         out_shape=jax.ShapeDtypeStruct((n, length, width), bf16),
         grid=(n // count,),
         in_specs=[
@@ -275,20 +299,21 @@
             pl.BlockSpec(fresh.shape, lambda i: (0, 0, 0)),
         ]
         + [
-            pl.BlockSpec((count, rows, width), functools.partial(lambda k, i: (i, k, 0), first // rows))
-            for _, first, rows in pieces
+            pl.BlockSpec((count, rows, width), functools.partial(lambda k, i: (i, k, 0), start // rows))
+            for _, start, rows, _ in pieces
         ],
         out_specs=pl.BlockSpec((count, length, width), lambda i: (i, 0, 0)),
         scratch_shapes=[pltpu.VMEM(fresh.shape, f32)],
-        compiler_params=pltpu.CompilerParams(vmem_limit_bytes=8 * 1024 * 1024),
+        compiler_params=pltpu.CompilerParams(vmem_limit_bytes=62 * 1024 * 1024),
         cost_estimate=pl.CostEstimate(
             flops=0, bytes_accessed=4 * n * length * width, transcendentals=0
         ),
         name="place",
-    )(table, fresh, *[array for array, _, _ in pieces])
-
-
-def finish_kernel(table, first, second, third, fourth, residual, gain, out, normed, sums, squares):
+    )(table, fresh, *[array for array, _, _, _ in pieces])
+
+
+def finish_kernel(table, *refs):
+    *pieces, residual, gain, out, normed, sums = refs
     t = table[5, 0]
     rows = residual.shape[0]
     row = lax.broadcasted_iota(jnp.int32, (rows, rows), 0)
@@ -301,7 +326,7 @@
     total = jnp.zeros((rows, 128), f32)
     for k in range(0, residual.shape[1], step):
         cut = slice(k, k + step)
-        piece = jnp.concatenate([x[:, cut] for x in (first, second, third, fourth)], axis=0)
+        piece = jnp.concatenate([x[:, cut].astype(f32) for x in pieces], axis=0).astype(bf16)
         level = residual[:, cut].astype(f32) + jnp.dot(pick, piece, preferred_element_type=f32)
         out[:, cut] = level.astype(bf16)
         sums[:, cut] = level
@@ -315,32 +340,36 @@
         normed[:, cut] = (sums[:, cut] * factor * gain[:, cut].astype(f32)).astype(bf16)
 
 
-def finish(table, first, second, third, fourth, residual, gain):
+def finish(table, pieces, residual, gain):
     rows, width = residual.shape
     vm = pl.BlockSpec(memory_space=pltpu.VMEM)
     return pl.pallas_call(
         finish_kernel,
         out_shape=(jax.ShapeDtypeStruct((rows, width), bf16),) * 2,
-        in_specs=[pl.BlockSpec(memory_space=pltpu.SMEM)] + [vm] * 6,
+        in_specs=[pl.BlockSpec(memory_space=pltpu.SMEM)] + [vm] * (len(pieces) + 2),
         out_specs=(vm, vm),
-        scratch_shapes=[pltpu.VMEM((rows, width), f32), pltpu.VMEM((rows, 128), f32)],
+        scratch_shapes=[pltpu.VMEM((rows, width), f32)],
         compiler_params=pltpu.CompilerParams(vmem_limit_bytes=16 * 1024 * 1024),
         cost_estimate=pl.CostEstimate(
             flops=2 * rows * rows * width, bytes_accessed=8 * rows * width, transcendentals=0
         ),
         name="finish",
-    )(table, first, second, third, fourth, residual, gain)
+    )(table, *pieces, residual, gain)
 
 
 def swap(x, mask):
-    return lax.ppermute(x, "tensor", [(t, t ^ mask) for t in range(16)])
+    return lax.ppermute(x, "tensor", [(t, fold(fold(t) ^ mask)) for t in range(16)])
 
 
 def hand_over(x, mask):
     return lax.ppermute(
         x,
         ("group", "tensor"),
-        [(g * 16 + t, (g ^ t) * 16 + (t ^ mask)) for g in range(16) for t in range(16)],
+        [
+            (g * 16 + t, (g ^ fold(t)) * 16 + fold(fold(t) ^ mask))
+            for g in range(16)
+            for t in range(16)
+        ],
     )
 
 
@@ -364,18 +393,21 @@
     msg = ask(queries, fresh_keys, fresh_values)
     msg = lax.all_to_all(msg, "group", split_axis=0, concat_axis=0, tiled=True)
     old_keys, old_values = key_cache[:, 0], value_cache[:, 0]
-    part = 64
+    length = old_keys.shape[1]
+    part, share = 144, 176
+    both = length - 2 * share
     large, small, table = order_cache(
-        dest_table, cache_len, remaining, old_keys, old_values, part
+        dest_table, cache_len, remaining, old_keys, old_values, part, share
     )
     large = lax.all_to_all(large, "group", split_axis=0, concat_axis=0, tiled=True)
 
     def first_steps(turn):
         keep, near, far = attend(turn[None], table, msg, old_keys, old_values, out_weight)
-        far, near = swap(far, 1), swap(near, 1)
-        s = keep[16:] + far.astype(f32)
-        s = keep[:16] + near.astype(f32) + swap(s.astype(bf16), 2).astype(f32)
-        s = s[:8] + swap(s[8:].astype(bf16), 4).astype(f32)
+        far, near = swap(far, 1), swap(near, 1).astype(f32)
+        far = swap((keep[24:] + far.astype(f32)).astype(bf16), 2)
+        mid = swap((keep[16:24] + near[16:]).astype(bf16), 2)
+        far = swap((keep[8:16] + near[8:16] + far.astype(f32)).astype(bf16), 4)
+        s = keep[:8] + near[:8] + mid.astype(f32) + far.astype(f32)
         return s[:4], s[4:].astype(bf16)
 
     def no_steps(turn):
@@ -384,25 +416,47 @@
     tensor = lax.axis_index("tensor")
     s, send = lax.cond(tensor >= 0, first_steps, no_steps, tensor)
     s, send, large = lax.optimization_barrier((s, send, large))
-    s = s + swap(send, 8).astype(f32)
-    s = s.astype(bf16)
-    first = jnp.concatenate([hand_over(s, m) for m in (0, 8)], axis=0)
+    key_share = large[:, part : part + share]
+    key_other = swap(key_share, 1)
+
+    def next_steps(s, send):
+        s = (s + swap(send, 8).astype(f32)).astype(bf16)
+        return jnp.concatenate([hand_over(s, m) for m in (0, 8)], axis=0)
+
+    first = lax.cond(
+        tensor >= 0,
+        next_steps,
+        lambda s, send: jnp.zeros((8, out_width), bf16),
+        s,
+        send,
+    )
     first, small = lax.optimization_barrier((first, small))
+    by4 = swap(first, 4)
+    by2 = swap(first, 2)
+    by1 = swap(first, 1)
     small = lax.all_to_all(small, "group", split_axis=0, concat_axis=0, tiled=True)
-    first = jnp.concatenate([first, swap(first, 4)], axis=0)
-    second = swap(first, 2)
-    third = swap(first, 1)
-    fourth = swap(second, 1)
-    length = old_keys.shape[1]
-    key_out = place(table, fresh_keys, (large, 0, length))
-    value_out = place(table, fresh_values, (large, length, part), (small, 0, length - part))
-    fourth, value_out = lax.optimization_barrier((fourth, value_out))
+    key_out = place(
+        table,
+        fresh_keys,
+        (large, part + share, both, (2 * share, 2 * share)),
+        (key_share, 0, share, (0, share)),
+        (key_other, 0, share, (share, 0)),
+    )
+    by4, key_out = lax.optimization_barrier((by4, key_out))
+    by42 = swap(by4, 2)
+    later = swap(jnp.concatenate([by4, by2], axis=0), 1)
+    by42, by1 = lax.optimization_barrier((by42, by1))
+    last = swap(by42, 1)
+    value_out = place(
+        table,
+        fresh_values,
+        (large, 0, part, (0, 0)),
+        (small, 0, length - part, (part, part)),
+    )
+    last, value_out = lax.optimization_barrier((last, value_out))
     residual_out, normed = finish(
         table,
-        first,
-        second,
-        third,
-        fourth,
+        (first, by4, by2, by42, by1, later, last),
         residual_in.reshape(steps * n, out_width),
         norm_gain.reshape(1, out_width),
     )

time: 106 us -> 99 us (0.934)
  waiting for transfers between devices: 35.4 us -> 20.5 us
  starting transfers between devices: 44.9 us -> 51.9 us
    ppermute x11 -> x15, waiting for transfers between devices: 35.4 us -> 20.5 us  [the longest x13 15 us: swap(): lax.ppermute(x, 'tensor', [(t, fold(fold(t) ^ mask)) for t in range(16)])]
    ppermute x11 -> x15, starting transfers between devices: 28 us -> 34.3 us  [the longest x13 32.1 us: swap(): lax.ppermute(x, 'tensor', [(t, fold(fold(t) ^ mask)) for t in range(16)])]
    pallas_call x3, Pallas kernels: 12.7 us -> 14 us  [the longest x2 8.41 us: place(): pl.pallas_call(functools.partial(place_kernel, tuple((bases for _, _, _,...]
  transfers between devices with their start and end apart: 14 -> 18, of which waited for: 8 -> 7; matrix products, arithmetic and copies ran while one was open for 0% -> 0% of each run, Pallas kernels for 18% -> 20%
where the time goes in v3:
time: 99 us; the launch traced here: 98 us
  starting transfers between devices  51.9 us (52%)
  Pallas kernels  23.6 us (24%)
  waiting for transfers between devices  20.5 us (21%)
  local copies, waits for them, and re-layouts  1.02 us (1%)
    ppermute x13, starting transfers between devices, swap(): lax.ppermute(x, 'tensor', [(t, fold(fold(t) ^ mask)) for t in range(16)])  32.1 us
    ppermute x13, waiting for transfers between devices, swap(): lax.ppermute(x, 'tensor', [(t, fold(fold(t) ^ mask)) for t in range(16)])  15 us
    pallas_call x2, Pallas kernels, place(): pl.pallas_call(functools.partial(place_kernel, tuple((bases for _, _, _,...  8.41 us
    all_to_all x1, starting transfers between devices, on_device(): lax.all_to_all(small, 'group', split_axis=0, concat_axis=0, tiled=True)  6.01 us
    pallas_call x1, Pallas kernels, attend(): pl.pallas_call(attend_kernel, out_shape=(jax.ShapeDtypeStruct((2 * n, out...  5.79 us
    all_to_all x1, starting transfers between devices, on_device(): msg = lax.all_to_all(msg, 'group', split_axis=0, concat_axis=0, tiled=True)  5.78 us
    all_to_all x1, starting transfers between devices, on_device(): lax.all_to_all(large, 'group', split_axis=0, concat_axis=0, tiled=True)  5.73 us
    pallas_call x1, Pallas kernels, order_cache(): pl.pallas_call(order_kernel, out_shape=(jax.ShapeDtypeStruct((n, part + l...  5.61 us
  transfers between devices with their start and end apart: 18, of which 7 were waited for; matrix products, arithmetic and copies ran while one was open for 0% of the time, Pallas kernels for 20%

profile of v3, /device:TPU:24, one launch (start us, length us, event | category | flops | bytes accessed | tf_op | source)
XLA Modules:
  0.0 98.0 jit_solution(10738587959713430526)
XLA Ops:
  0.6 1.7 %ask.1 = bf16[16,32,128]{2,1,0:T(8,128)(2,1)} custom-call(bf16[4,16,4,128]{3,2,1,0:T(4,128)(2,1)} %queries.1, bf16[4,16,128]{2,1,0:T(8,128)(2,1)} %bitcast.21, bf16[4,16,128]{2,1,0:T(8,128)(2,1)} %bitcast.23), custom_call_target="tpu_custom_call" | custom-call | bytes 400000 | tf_op jit(solution)/shard_map/ask/pallas_call | solution.py:35
  2.3 5.8 %all-to-all-start = ((bf16[16,32,128]{2,1,0:T(8,128)(2,1)}), bf16[16,32,128]{2,1,0:T(8,128)(2,1)S(1)}, u32[]{:S(2)}, u32[]{:S(2)}) async-start(bf16[16,32,128]{2,1,0:T(8,128)(2,1)} %ask.1), calls=%async_computation | async-start | bytes 262144 | tf_op jit(solution)/shard_map/all_to_all | solution.py:394
  8.1 5.6 %order_cache.1 = (bf16[16,480,128]{2,1,0:T(8,128)(2,1)}, bf16[16,368,128]{2,1,0:T(8,128)(2,1)}, s32[6,16]{1,0:T(8,128)S(1)}) custom-call(s32[256]{0:T(256)} %dest.1, s32[256]{0:T(256)} %lens.1, s32[256]{0:T(256)} %rest.1, bf16[16,512,128]{2,1,0:T(8,128)(2,1)} %bitcast.15, bf16[16,512,128]{2,1,0:T(8,128)(2,1)} %bitcast.17), custom_call_target="tpu_custom_call" | custom-call | bytes 8388608 | tf_op jit(solution)/shard_map/order_cache/pallas_call | solution.py:121
  13.7 5.7 %all-to-all-start.1 = ((bf16[16,480,128]{2,1,0:T(8,128)(2,1)}), bf16[16,480,128]{2,1,0:T(8,128)(2,1)S(1)}, u32[]{:S(2)}, u32[]{:S(2)}) async-start(bf16[16,480,128]{2,1,0:T(8,128)(2,1)} %get-tuple-element.55), calls=%async_computation.1 | async-start | bytes 3932160 | tf_op jit(solution)/shard_map/all_to_all | solution.py:402
  19.5 27.9 %conditional.2 = (f32[4,5120]{1,0:T(4,128)S(1)}, bf16[4,5120]{1,0:T(4,128)(2,1)S(1)}) conditional(s32[]{:T(128)} %convert_element_type.35, () %tuple.28, (s32[]{:T(128)}, s32[6,16]{1,0:T(8,128)S(1)}, bf16[16,32,128]{2,1,0:T(8,128)(2,1)S(1)}, bf16[16,512,128]{2,1,0:T(8,128)(2,1)}, bf16[16,512,128]{2,1,0:T(8,128)(2,1)}, ...), branch_computations={%region_0.0_spmd, %region_1.0_spmd} | conditional | flops 403349504 | bytes 14598360 | solution.py:417
  19.5 5.8 %attend.1 = (f32[32,5120]{1,0:T(8,128)S(1)}, bf16[24,5120]{1,0:T(8,128)(2,1)S(1)}, bf16[8,5120]{1,0:T(8,128)(2,1)S(1)}) custom-call(s32[1]{0:T(128)} %bitcast.turn, s32[6,16]{1,0:T(8,128)S(1)} %get-tuple-element.20.table, bf16[16,32,128]{2,1,0:T(8,128)(2,1)S(1)} %get-tuple-element.21.msg, bf16[16,512,128]{2,1,0:T(8,128)(2,1)} %get-tuple-element.22.keys, ...), custom_call_target="tpu_custom_call" | custom-call | flops 402653184 | bytes 9437184 | tf_op jit(solution)/shard_map/cond/branch_1_fun/attend/pallas_call | solution.py:224
  25.3 2.0 %collective-permute-start.2 = (bf16[8,5120]{1,0:T(8,128)(2,1)S(1)}, bf16[8,5120]{1,0:T(8,128)(2,1)S(1)}, u32[]{:S(2)}, u32[]{:S(2)}) collective-permute-start(bf16[8,5120]{1,0:T(8,128)(2,1)S(1)} %get-tuple-element.27), channel_id=1, source_target_pairs={{0,1},{1,0},{2,3},{3,2},{4,5},{5,4},{6,7},{7,6},{8,9},{9,8},{10,11... | collective-permute-start | bytes 245768 | tf_op jit(solution)/shard_map/cond/branch_1_fun/ppermute | solution.py:361
  27.3 0.1 collective-permute-start
  27.4 3.0 %collective-permute-done.2 = bf16[8,5120]{1,0:T(8,128)(2,1)S(1)} collective-permute-done((bf16[8,5120]{1,0:T(8,128)(2,1)S(1)}, bf16[8,5120]{1,0:T(8,128)(2,1)S(1)}, u32[]{:S(2)}, u32[]{:S(2)}) %collective-permute-start.2) | collective-permute-done | bytes 81952 | tf_op jit(solution)/shard_map/cond/branch_1_fun/ppermute | solution.py:361
  30.4 3.4 %collective-permute-start.3 = (bf16[8,5120]{1,0:T(8,128)(2,1)S(1)}, bf16[8,5120]{1,0:T(8,128)(2,1)S(1)}, u32[]{:S(2)}, u32[]{:S(2)}) collective-permute-start(bf16[8,5120]{1,0:T(8,128)(2,1)S(1)} %add_convert_fusion), channel_id=1, source_target_pairs={{0,2},{1,3},{2,0},{3,1},{4,6},{5,7},{6,4},{7,5},{8,10},{9,11},{10,... | collective-permute-start | bytes 245768 | tf_op jit(solution)/shard_map/cond/branch_1_fun/ppermute | solution.py:361
  33.7 3.3 %collective-permute-done = bf16[24,5120]{1,0:T(8,128)(2,1)S(1)} collective-permute-done((bf16[24,5120]{1,0:T(8,128)(2,1)S(1)}, bf16[24,5120]{1,0:T(8,128)(2,1)S(1)}, u32[]{:S(2)}, u32[]{:S(2)}) %collective-permute-start) | collective-permute-done | bytes 245792 | tf_op jit(solution)/shard_map/cond/branch_1_fun/ppermute | solution.py:361
  37.2 2.8 %collective-permute-start.1 = (bf16[8,5120]{1,0:T(8,128)(2,1)S(1)}, bf16[8,5120]{1,0:T(8,128)(2,1)S(1)}, u32[]{:S(2)}, u32[]{:S(2)}) collective-permute-start(bf16[8,5120]{1,0:T(8,128)(2,1)S(1)} %get-tuple-element.76), channel_id=1, source_target_pairs={{0,2},{1,3},{2,0},{3,1},{4,6},{5,7},{6,4},{7,5},{8,10},{9,11},{10,... | collective-permute-start | bytes 245768 | tf_op jit(solution)/shard_map/cond/branch_1_fun/ppermute | solution.py:361
  39.9 4.9 %collective-permute-start.4 = (bf16[8,5120]{1,0:T(8,128)(2,1)S(1)}, bf16[8,5120]{1,0:T(8,128)(2,1)S(1)}, u32[]{:S(2)}, u32[]{:S(2)}) collective-permute-start(bf16[8,5120]{1,0:T(8,128)(2,1)S(1)} %get-tuple-element.77), channel_id=1, source_target_pairs={{0,7},{1,6},{2,5},{3,4},{4,3},{5,2},{6,1},{7,0},{8,15},{9,14},{10,... | collective-permute-start | bytes 245768 | tf_op jit(solution)/shard_map/cond/branch_1_fun/ppermute | solution.py:361
  44.8 2.5 %collective-permute-done.4 = bf16[8,5120]{1,0:T(8,128)(2,1)S(1)} collective-permute-done((bf16[8,5120]{1,0:T(8,128)(2,1)S(1)}, bf16[8,5120]{1,0:T(8,128)(2,1)S(1)}, u32[]{:S(2)}, u32[]{:S(2)}) %collective-permute-start.4) | collective-permute-done | bytes 81952 | tf_op jit(solution)/shard_map/cond/branch_1_fun/ppermute | solution.py:361
  47.5 2.9 %collective-permute-start.9 = (bf16[16,176,128]{2,1,0:T(8,128)(2,1)S(1)}, bf16[16,176,128]{2,1,0:T(8,128)(2,1)S(1)}, u32[]{:S(2)}, u32[]{:S(2)}) collective-permute-start(bf16[16,176,128]{2,1,0:T(8,128)(2,1)S(1)} %slice.31.refs_1_), channel_id=1, source_target_pairs={{0,1},{1,0},{2,3},{3,2},{4,5},{5,4},{6,7},{7,6},{8,9},{9,8},{10,11... | collective-permute-start | bytes 2162696 | tf_op jit(solution)/shard_map/ppermute | solution.py:361
  50.4 13.4 %conditional.3 = (bf16[8,5120]{1,0:T(8,128)(2,1)S(1)}) conditional(s32[]{:T(128)} %convert_element_type.35, () %tuple.27, (bf16[4,5120]{1,0:T(4,128)(2,1)S(1)}, f32[4,5120]{1,0:T(4,128)S(1)}) %tuple.31), branch_computations={%region_2.0_spmd, %region_3.0_spmd} | conditional | flops 225280 | bytes 819328 | solution.py:426
  50.4 1.2 %collective-permute-start.5 = (bf16[4,5120]{1,0:T(4,128)(2,1)S(1)}, bf16[4,5120]{1,0:T(4,128)(2,1)S(1)}, u32[]{:S(2)}, u32[]{:S(2)}) collective-permute-start(bf16[4,5120]{1,0:T(4,128)(2,1)S(1)} %get-tuple-element.29), channel_id=1, source_target_pairs={{0,8},{1,9},{2,10},{3,11},{4,12},{5,13},{6,14},{7,15},{8,0},{9,1},... | collective-permute-start | bytes 122888 | tf_op jit(solution)/shard_map/cond/branch_1_fun/ppermute | solution.py:361
  51.6 4.3 %collective-permute-done.5 = bf16[4,5120]{1,0:T(4,128)(2,1)S(1)} collective-permute-done((bf16[4,5120]{1,0:T(4,128)(2,1)S(1)}, bf16[4,5120]{1,0:T(4,128)(2,1)S(1)}, u32[]{:S(2)}, u32[]{:S(2)}) %collective-permute-start.5) | collective-permute-done | bytes 40992 | tf_op jit(solution)/shard_map/cond/branch_1_fun/ppermute | solution.py:361
  55.9 2.2 %collective-permute-start.6 = (bf16[4,5120]{1,0:T(4,128)(2,1)S(1)}, bf16[4,5120]{1,0:T(4,128)(2,1)S(1)}, u32[]{:S(2)}, u32[]{:S(2)}) collective-permute-start(bf16[4,5120]{1,0:T(4,128)(2,1)S(1)} %add_convert_fusion.1), channel_id=1, source_target_pairs={{0,0},{1,17},{2,34},{3,51},{4,116},{5,101},{6,86},{7,71},{8,136},{... | collective-permute-start | bytes 122888 | tf_op jit(solution)/shard_map/cond/branch_1_fun/ppermute | solution.py:365
  58.2 3.6 %collective-permute-done.6 = bf16[4,5120]{1,0:T(4,128)(2,1)S(1)} collective-permute-done((bf16[4,5120]{1,0:T(4,128)(2,1)S(1)}, bf16[4,5120]{1,0:T(4,128)(2,1)S(1)}, u32[]{:S(2)}, u32[]{:S(2)}) %collective-permute-start.6) | collective-permute-done | bytes 40992 | tf_op jit(solution)/shard_map/cond/branch_1_fun/ppermute | solution.py:365
  61.8 1.9 %collective-permute-done.7 = bf16[4,5120]{1,0:T(4,128)(2,1)S(1)} collective-permute-done((bf16[4,5120]{1,0:T(4,128)(2,1)S(1)}, bf16[4,5120]{1,0:T(4,128)(2,1)S(1)}, u32[]{:S(2)}, u32[]{:S(2)}) %collective-permute-start.7) | collective-permute-done | bytes 40992 | tf_op jit(solution)/shard_map/cond/branch_1_fun/ppermute | solution.py:365
  63.7 6.0 %all-to-all-start.2 = ((bf16[16,368,128]{2,1,0:T(8,128)(2,1)}), bf16[16,368,128]{2,1,0:T(8,128)(2,1)}, u32[]{:S(2)}, u32[]{:S(2)}) async-start(bf16[16,368,128]{2,1,0:T(8,128)(2,1)} %get-tuple-element.64), calls=%async_computation.2 | async-start | bytes 3014656 | tf_op jit(solution)/shard_map/all_to_all | solution.py:437
  69.8 7.6 %collective-permute-start.8 = (bf16[8,5120]{1,0:T(8,128)(2,1)S(1)}, bf16[8,5120]{1,0:T(8,128)(2,1)S(1)}, u32[]{:S(2)}, u32[]{:S(2)}) collective-permute-start(bf16[8,5120]{1,0:T(8,128)(2,1)S(1)} %get-tuple-element.82.refs_0_), channel_id=1, source_target_pairs={{0,7},{1,6},{2,5},{3,4},{4,3},{5,2},{6,1},{7,0},{8,15},{9,14},{10,... | collective-permute-start | bytes 245768 | tf_op jit(solution)/shard_map/ppermute | solution.py:361
  77.3 0.9 collective-permute-start.10
  78.2 0.9 copy-done.3
  79.1 4.2 %place.2 = bf16[16,512,128]{2,1,0:T(8,128)(2,1)} custom-call(s32[6,16]{1,0:T(8,128)S(1)} %get-tuple-element.52.table, bf16[4,16,128]{2,1,0:T(8,128)(2,1)} %bitcast.22, bf16[16,480,128]{2,1,0:T(8,128)(2,1)} %copy-done.1, bf16[16,176,128]{2,1,0:T(8,128)(2,1)} %copy-done.2, bf16[16,176,128]{2,1,0:T(8,128)(2,1)} %copy-done.3), custom_call_target="tpu_custom_call" | custom-call | bytes 4194304 | tf_op jit(solution)/shard_map/place/pallas_call | solution.py:293
  83.3 2.0 %collective-permute-start.11 = (bf16[8,5120]{1,0:T(8,128)(2,1)S(1)}, bf16[8,5120]{1,0:T(8,128)(2,1)S(1)}, u32[]{:S(2)}, u32[]{:S(2)}) collective-permute-start(bf16[8,5120]{1,0:T(8,128)(2,1)S(1)} %collective-permute-done.8.refs_1_), channel_id=1, source_target_pairs={{0,2},{1,3},{2,0},{3,1},{4,6},{5,7},{6,4},{7,5},{8,10},{9,11},{10,... | collective-permute-start | bytes 245768 | tf_op jit(solution)/shard_map/ppermute | solution.py:361
  85.4 2.1 %collective-permute-start.13 = (bf16[16,5120]{1,0:T(8,128)(2,1)S(1)}, bf16[16,5120]{1,0:T(8,128)(2,1)S(1)}, u32[]{:S(2)}, u32[]{:S(2)}) collective-permute-start(bf16[16,5120]{1,0:T(8,128)(2,1)S(1)} %pad_maximum_fusion.1), channel_id=1, source_target_pairs={{0,1},{1,0},{2,3},{3,2},{4,5},{5,4},{6,7},{7,6},{8,9},{9,8},{10,11... | collective-permute-start | bytes 491528 | tf_op jit(solution)/shard_map/ppermute | solution.py:361
  87.5 2.0 %collective-permute-done.11.refs_3_ = bf16[8,5120]{1,0:T(8,128)(2,1)S(1)} collective-permute-done((bf16[8,5120]{1,0:T(8,128)(2,1)S(1)}, bf16[8,5120]{1,0:T(8,128)(2,1)S(1)}, u32[]{:S(2)}, u32[]{:S(2)}) %collective-permute-start.11) | collective-permute-done | bytes 81952 | tf_op jit(solution)/shard_map/ppermute | solution.py:361
  89.4 2.2 %collective-permute-start.14 = (bf16[8,5120]{1,0:T(8,128)(2,1)S(1)}, bf16[8,5120]{1,0:T(8,128)(2,1)S(1)}, u32[]{:S(2)}, u32[]{:S(2)}) collective-permute-start(bf16[8,5120]{1,0:T(8,128)(2,1)S(1)} %collective-permute-done.11.refs_3_), channel_id=1, source_target_pairs={{0,1},{1,0},{2,3},{3,2},{4,5},{5,4},{6,7},{7,6},{8,9},{9,8},{10,11... | collective-permute-start | bytes 245768 | tf_op jit(solution)/shard_map/ppermute | solution.py:361
  91.7 4.2 %place.3 = bf16[16,512,128]{2,1,0:T(8,128)(2,1)} custom-call(s32[6,16]{1,0:T(8,128)S(1)} %get-tuple-element.52.table, bf16[4,16,128]{2,1,0:T(8,128)(2,1)} %bitcast.24, bf16[16,480,128]{2,1,0:T(8,128)(2,1)} %copy-done.1, bf16[16,368,128]{2,1,0:T(8,128)(2,1)} %all-to-all-done.2.refs_1_), custom_call_target="tpu_custom_call" | custom-call | bytes 4194304 | tf_op jit(solution)/shard_map/place/pallas_call | solution.py:293
  95.9 2.1 %finish.1 = (bf16[64,5120]{1,0:T(8,128)(2,1)}, bf16[64,5120]{1,0:T(8,128)(2,1)}) custom-call(s32[6,16]{1,0:T(8,128)S(1)} %get-tuple-element.52.table, bf16[8,5120]{1,0:T(8,128)(2,1)S(1)} %get-tuple-element.82.refs_0_, bf16[8,5120]{1,0:T(8,128)(2,1)S(1)} %collective-permute-done.8.refs_1_, bf16[8,5120]{1,0:T(8,128)(2,1)S(1)} %collective-permute-done.10.refs_2_, ...), custom_call_target="tpu_custom_call" | custom-call | flops 41943040 | bytes 2621440 | tf_op jit(solution)/shard_map/finish/pallas_call | solution.py:346
  (33 shorter events, 0.4 us)
Async XLA Ops:
  2.3 11.4 %all-to-all-start = ((bf16[16,32,128]{2,1,0:T(8,128)(2,1)}), bf16[16,32,128]{2,1,0:T(8,128)(2,1)S(1)}, u32[]{:S(2)}, u32[]{:S(2)}) async-start(bf16[16,32,128]{2,1,0:T(8,128)(2,1)} %ask.1), calls=%async_computation | async-start | bytes 262144 | tf_op jit(solution)/shard_map/all_to_all | solution.py:394
  13.7 33.6 %all-to-all-start.1 = ((bf16[16,480,128]{2,1,0:T(8,128)(2,1)}), bf16[16,480,128]{2,1,0:T(8,128)(2,1)S(1)}, u32[]{:S(2)}, u32[]{:S(2)}) async-start(bf16[16,480,128]{2,1,0:T(8,128)(2,1)} %get-tuple-element.55), calls=%async_computation.1 | async-start | bytes 3932160 | tf_op jit(solution)/shard_map/all_to_all | solution.py:402
  25.3 5.1 %collective-permute-start.2 = (bf16[8,5120]{1,0:T(8,128)(2,1)S(1)}, bf16[8,5120]{1,0:T(8,128)(2,1)S(1)}, u32[]{:S(2)}, u32[]{:S(2)}) collective-permute-start(bf16[8,5120]{1,0:T(8,128)(2,1)S(1)} %get-tuple-element.27), channel_id=1, source_target_pairs={{0,1},{1,0},{2,3},{3,2},{4,5},{5,4},{6,7},{7,6},{8,9},{9,8},{10,11... | collective-permute-start | bytes 245768 | tf_op jit(solution)/shard_map/cond/branch_1_fun/ppermute | solution.py:361
  27.3 9.8 %collective-permute-start = (bf16[24,5120]{1,0:T(8,128)(2,1)S(1)}, bf16[24,5120]{1,0:T(8,128)(2,1)S(1)}, u32[]{:S(2)}, u32[]{:S(2)}) collective-permute-start(bf16[24,5120]{1,0:T(8,128)(2,1)S(1)} %get-tuple-element.26), channel_id=1, source_target_pairs={{0,1},{1,0},{2,3},{3,2},{4,5},{5,4},{6,7},{7,6},{8,9},{9,8},{10,11... | collective-permute-start | bytes 737288 | tf_op jit(solution)/shard_map/cond/branch_1_fun/ppermute | solution.py:361
  30.4 6.7 %collective-permute-start.3 = (bf16[8,5120]{1,0:T(8,128)(2,1)S(1)}, bf16[8,5120]{1,0:T(8,128)(2,1)S(1)}, u32[]{:S(2)}, u32[]{:S(2)}) collective-permute-start(bf16[8,5120]{1,0:T(8,128)(2,1)S(1)} %add_convert_fusion), channel_id=1, source_target_pairs={{0,2},{1,3},{2,0},{3,1},{4,6},{5,7},{6,4},{7,5},{8,10},{9,11},{10,... | collective-permute-start | bytes 245768 | tf_op jit(solution)/shard_map/cond/branch_1_fun/ppermute | solution.py:361
  37.2 7.7 %collective-permute-start.1 = (bf16[8,5120]{1,0:T(8,128)(2,1)S(1)}, bf16[8,5120]{1,0:T(8,128)(2,1)S(1)}, u32[]{:S(2)}, u32[]{:S(2)}) collective-permute-start(bf16[8,5120]{1,0:T(8,128)(2,1)S(1)} %get-tuple-element.76), channel_id=1, source_target_pairs={{0,2},{1,3},{2,0},{3,1},{4,6},{5,7},{6,4},{7,5},{8,10},{9,11},{10,... | collective-permute-start | bytes 245768 | tf_op jit(solution)/shard_map/cond/branch_1_fun/ppermute | solution.py:361
  39.9 7.4 %collective-permute-start.4 = (bf16[8,5120]{1,0:T(8,128)(2,1)S(1)}, bf16[8,5120]{1,0:T(8,128)(2,1)S(1)}, u32[]{:S(2)}, u32[]{:S(2)}) collective-permute-start(bf16[8,5120]{1,0:T(8,128)(2,1)S(1)} %get-tuple-element.77), channel_id=1, source_target_pairs={{0,7},{1,6},{2,5},{3,4},{4,3},{5,2},{6,1},{7,0},{8,15},{9,14},{10,... | collective-permute-start | bytes 245768 | tf_op jit(solution)/shard_map/cond/branch_1_fun/ppermute | solution.py:361
  47.4 16.3 %copy-start.1 = (bf16[16,480,128]{2,1,0:T(8,128)(2,1)}, bf16[16,480,128]{2,1,0:T(8,128)(2,1)S(1)}, u32[]{:S(2)}) copy-start(bf16[16,480,128]{2,1,0:T(8,128)(2,1)S(1)} %all-to-all-done.1.refs_0_) | copy-start | bytes 5898244
  47.5 30.8 %copy-start.2 = (bf16[16,176,128]{2,1,0:T(8,128)(2,1)}, bf16[16,176,128]{2,1,0:T(8,128)(2,1)S(1)}, u32[]{:S(2)}) copy-start(bf16[16,176,128]{2,1,0:T(8,128)(2,1)S(1)} %slice.31.refs_1_) | copy-start | bytes 2162692
  47.5 30.8 %collective-permute-start.9 = (bf16[16,176,128]{2,1,0:T(8,128)(2,1)S(1)}, bf16[16,176,128]{2,1,0:T(8,128)(2,1)S(1)}, u32[]{:S(2)}, u32[]{:S(2)}) collective-permute-start(bf16[16,176,128]{2,1,0:T(8,128)(2,1)S(1)} %slice.31.refs_1_), channel_id=1, source_target_pairs={{0,1},{1,0},{2,3},{3,2},{4,5},{5,4},{6,7},{7,6},{8,9},{9,8},{10,11... | collective-permute-start | bytes 2162696 | tf_op jit(solution)/shard_map/ppermute | solution.py:361
  50.4 5.5 %collective-permute-start.5 = (bf16[4,5120]{1,0:T(4,128)(2,1)S(1)}, bf16[4,5120]{1,0:T(4,128)(2,1)S(1)}, u32[]{:S(2)}, u32[]{:S(2)}) collective-permute-start(bf16[4,5120]{1,0:T(4,128)(2,1)S(1)} %get-tuple-element.29), channel_id=1, source_target_pairs={{0,8},{1,9},{2,10},{3,11},{4,12},{5,13},{6,14},{7,15},{8,0},{9,1},... | collective-permute-start | bytes 122888 | tf_op jit(solution)/shard_map/cond/branch_1_fun/ppermute | solution.py:361
  55.9 5.9 %collective-permute-start.6 = (bf16[4,5120]{1,0:T(4,128)(2,1)S(1)}, bf16[4,5120]{1,0:T(4,128)(2,1)S(1)}, u32[]{:S(2)}, u32[]{:S(2)}) collective-permute-start(bf16[4,5120]{1,0:T(4,128)(2,1)S(1)} %add_convert_fusion.1), channel_id=1, source_target_pairs={{0,0},{1,17},{2,34},{3,51},{4,116},{5,101},{6,86},{7,71},{8,136},{... | collective-permute-start | bytes 122888 | tf_op jit(solution)/shard_map/cond/branch_1_fun/ppermute | solution.py:365
  58.1 5.6 %collective-permute-start.7 = (bf16[4,5120]{1,0:T(4,128)(2,1)S(1)}, bf16[4,5120]{1,0:T(4,128)(2,1)S(1)}, u32[]{:S(2)}, u32[]{:S(2)}) collective-permute-start(bf16[4,5120]{1,0:T(4,128)(2,1)S(1)} %add_convert_fusion.1), channel_id=1, source_target_pairs={{0,8},{1,25},{2,42},{3,59},{4,124},{5,109},{6,94},{7,79},{8,128},{... | collective-permute-start | bytes 122888 | tf_op jit(solution)/shard_map/cond/branch_1_fun/ppermute | solution.py:365
  63.7 27.9 %all-to-all-start.2 = ((bf16[16,368,128]{2,1,0:T(8,128)(2,1)}), bf16[16,368,128]{2,1,0:T(8,128)(2,1)}, u32[]{:S(2)}, u32[]{:S(2)}) async-start(bf16[16,368,128]{2,1,0:T(8,128)(2,1)} %get-tuple-element.64), calls=%async_computation.2 | async-start | bytes 3014656 | tf_op jit(solution)/shard_map/all_to_all | solution.py:437
  69.8 21.9 %copy-start.4 = (bf16[5120]{0:T(1024)(128)(2,1)S(1)}, bf16[5120]{0:T(1024)(128)(2,1)}, u32[]{:S(2)}) copy-start(bf16[5120]{0:T(1024)(128)(2,1)} %param.25) | copy-start | bytes 30724
  69.8 13.6 %collective-permute-start.8 = (bf16[8,5120]{1,0:T(8,128)(2,1)S(1)}, bf16[8,5120]{1,0:T(8,128)(2,1)S(1)}, u32[]{:S(2)}, u32[]{:S(2)}) collective-permute-start(bf16[8,5120]{1,0:T(8,128)(2,1)S(1)} %get-tuple-element.82.refs_0_), channel_id=1, source_target_pairs={{0,7},{1,6},{2,5},{3,4},{4,3},{5,2},{6,1},{7,0},{8,15},{9,14},{10,... | collective-permute-start | bytes 245768 | tf_op jit(solution)/shard_map/ppermute | solution.py:361
  77.3 8.0 %collective-permute-start.10 = (bf16[8,5120]{1,0:T(8,128)(2,1)S(1)}, bf16[8,5120]{1,0:T(8,128)(2,1)S(1)}, u32[]{:S(2)}, u32[]{:S(2)}) collective-permute-start(bf16[8,5120]{1,0:T(8,128)(2,1)S(1)} %get-tuple-element.82.refs_0_), channel_id=1, source_target_pairs={{0,2},{1,3},{2,0},{3,1},{4,6},{5,7},{6,4},{7,5},{8,10},{9,11},{10,... | collective-permute-start | bytes 245768 | tf_op jit(solution)/shard_map/ppermute | solution.py:361
  78.2 9.3 %collective-permute-start.12 = (bf16[8,5120]{1,0:T(8,128)(2,1)S(1)}, bf16[8,5120]{1,0:T(8,128)(2,1)S(1)}, u32[]{:S(2)}, u32[]{:S(2)}) collective-permute-start(bf16[8,5120]{1,0:T(8,128)(2,1)S(1)} %get-tuple-element.82.refs_0_), channel_id=1, source_target_pairs={{0,1},{1,0},{2,3},{3,2},{4,5},{5,4},{6,7},{7,6},{8,9},{9,8},{10,11... | collective-permute-start | bytes 245768 | tf_op jit(solution)/shard_map/ppermute | solution.py:361
  78.2 0.9 copy-start.3
  83.3 6.1 %collective-permute-start.11 = (bf16[8,5120]{1,0:T(8,128)(2,1)S(1)}, bf16[8,5120]{1,0:T(8,128)(2,1)S(1)}, u32[]{:S(2)}, u32[]{:S(2)}) collective-permute-start(bf16[8,5120]{1,0:T(8,128)(2,1)S(1)} %collective-permute-done.8.refs_1_), channel_id=1, source_target_pairs={{0,2},{1,3},{2,0},{3,1},{4,6},{5,7},{6,4},{7,5},{8,10},{9,11},{10,... | collective-permute-start | bytes 245768 | tf_op jit(solution)/shard_map/ppermute | solution.py:361
  85.4 10.5 %collective-permute-start.13 = (bf16[16,5120]{1,0:T(8,128)(2,1)S(1)}, bf16[16,5120]{1,0:T(8,128)(2,1)S(1)}, u32[]{:S(2)}, u32[]{:S(2)}) collective-permute-start(bf16[16,5120]{1,0:T(8,128)(2,1)S(1)} %pad_maximum_fusion.1), channel_id=1, source_target_pairs={{0,1},{1,0},{2,3},{3,2},{4,5},{5,4},{6,7},{7,6},{8,9},{9,8},{10,11... | collective-permute-start | bytes 491528 | tf_op jit(solution)/shard_map/ppermute | solution.py:361
  89.4 6.4 %collective-permute-start.14 = (bf16[8,5120]{1,0:T(8,128)(2,1)S(1)}, bf16[8,5120]{1,0:T(8,128)(2,1)S(1)}, u32[]{:S(2)}, u32[]{:S(2)}) collective-permute-start(bf16[8,5120]{1,0:T(8,128)(2,1)S(1)} %collective-permute-done.11.refs_3_), channel_id=1, source_target_pairs={{0,1},{1,0},{2,3},{3,2},{4,5},{5,4},{6,7},{7,6},{8,9},{9,8},{10,11... | collective-permute-start | bytes 245768 | tf_op jit(solution)/shard_map/ppermute | solution.py:361
  91.6 4.3 %copy-start = (bf16[4,16,5120]{2,1,0:T(8,128)(2,1)S(1)}, bf16[4,16,5120]{2,1,0:T(8,128)(2,1)}, u32[]{:S(2)}) copy-start(bf16[4,16,5120]{2,1,0:T(8,128)(2,1)} %param.23) | copy-start | bytes 1966084

commit v4 on v3

--- a/solution.py
+++ b/solution.py
@@ -54,9 +54,7 @@
 def order_kernel(dest, lens, rest, keys, values, large, small, table, kbuf, vbuf, sems):
     n, length, _ = keys.shape
     part = length - small.shape[1]
-    rest_rows = large.shape[1] - part
-    share = length - rest_rows
-    both = length - 2 * share
+    share = large.shape[1] - part
     group = lax.axis_index("group")
     tensor = lax.axis_index("tensor")
     table[5, 0] = fold(tensor) ^ group
@@ -72,17 +70,14 @@
         j = table[0, d]
         return (
             pltpu.make_async_copy(
-                keys.at[j, pl.ds(base, share)], kbuf.at[d, pl.ds(0, share)], sems.at[0, d]
-            ),
-            pltpu.make_async_copy(
-                keys.at[j, pl.ds(2 * share, both)], kbuf.at[d, pl.ds(share, both)], sems.at[5, d]
+                keys.at[j, pl.ds(base, share)], kbuf.at[d], sems.at[0, d]
             ),
             pltpu.make_async_copy(values.at[j], vbuf.at[d], sems.at[1, d]),
         )
 
     def store(d):
         return (
-            pltpu.make_async_copy(kbuf.at[d], large.at[d, pl.ds(part, rest_rows)], sems.at[2, d]),
+            pltpu.make_async_copy(kbuf.at[d], large.at[d, pl.ds(part, share)], sems.at[2, d]),
             pltpu.make_async_copy(
                 vbuf.at[d, pl.ds(0, part)], large.at[d, pl.ds(0, part)], sems.at[3, d]
             ),
@@ -114,23 +109,23 @@
             c.wait()
 
 
-def order_cache(dest, lens, rest, keys, values, part, share):
+def order_cache(dest, lens, rest, keys, values, part):
     n, length, width = keys.shape
     sm = pl.BlockSpec(memory_space=pltpu.SMEM)
     hbm = pl.BlockSpec(memory_space=pl.ANY)
     return pl.pallas_call(
         order_kernel,
         out_shape=(
-            jax.ShapeDtypeStruct((n, part + length - share, width), keys.dtype),
+            jax.ShapeDtypeStruct((n, part + length // 2, width), keys.dtype),
             jax.ShapeDtypeStruct((n, length - part, width), keys.dtype),
             jax.ShapeDtypeStruct((6, n), jnp.int32),
         ),
         in_specs=[sm, sm, sm, hbm, hbm],
         out_specs=(hbm, hbm, sm),
         scratch_shapes=[
-            pltpu.VMEM((n, length - share, width), keys.dtype),
+            pltpu.VMEM((n, length // 2, width), keys.dtype),
             pltpu.VMEM(values.shape, values.dtype),
-            pltpu.SemaphoreType.DMA((6, n)),
+            pltpu.SemaphoreType.DMA((5, n)),
         ],
         compiler_params=pltpu.CompilerParams(vmem_limit_bytes=60 * 1024 * 1024),
         cost_estimate=pl.CostEstimate(
@@ -169,7 +164,7 @@
     rowd = lax.broadcasted_iota(jnp.int32, (16, 128), 0) % 4
     scale = 128 ** (-0.5)
     nt = (((1,), (1,)), ((), ()))
-    batch = 4
+    batch = 8
     for start in range(0, n, batch):
         ps = range(start, start + batch)
         for p in ps:
@@ -289,7 +284,7 @@
 def place(table, fresh, *pieces):
     n, _, width = pieces[0][0].shape
     length = sum(rows for _, _, rows, _ in pieces)
-    count = 4
+    count = 8
     return pl.pallas_call(
         functools.partial(place_kernel, tuple(bases for _, _, _, bases in pieces)),
         out_shape=jax.ShapeDtypeStruct((n, length, width), bf16),
@@ -394,10 +389,9 @@
     msg = lax.all_to_all(msg, "group", split_axis=0, concat_axis=0, tiled=True)
     old_keys, old_values = key_cache[:, 0], value_cache[:, 0]
     length = old_keys.shape[1]
-    part, share = 144, 176
-    both = length - 2 * share
+    part, share = 224, length // 2
     large, small, table = order_cache(
-        dest_table, cache_len, remaining, old_keys, old_values, part, share
+        dest_table, cache_len, remaining, old_keys, old_values, part
     )
     large = lax.all_to_all(large, "group", split_axis=0, concat_axis=0, tiled=True)
 
@@ -416,7 +410,7 @@
     tensor = lax.axis_index("tensor")
     s, send = lax.cond(tensor >= 0, first_steps, no_steps, tensor)
     s, send, large = lax.optimization_barrier((s, send, large))
-    key_share = large[:, part : part + share]
+    key_share = large[:, part:]
     key_other = swap(key_share, 1)
 
     def next_steps(s, send):
@@ -438,7 +432,6 @@
     key_out = place(
         table,
         fresh_keys,
-        (large, part + share, both, (2 * share, 2 * share)),
         (key_share, 0, share, (0, share)),
         (key_other, 0, share, (share, 0)),
     )

time: 99 us -> 94.7 us (0.957)
  Pallas kernels: 23.6 us -> 20.8 us
    pallas_call x2, Pallas kernels: 8.41 us -> 6.23 us  [place(): pl.pallas_call(functools.partial(place_kernel, tuple((bases for _, _, _,...]
  transfers between devices with their start and end apart: 18 -> 18, of which waited for: 7 -> 8; matrix products, arithmetic and copies ran while one was open for 0% -> 0% of each run, Pallas kernels for 20% -> 18%
where the time goes in v4:
time: 94.7 us; the launch traced here: 94.3 us
  starting transfers between devices  51.7 us (55%)
  Pallas kernels  20.8 us (22%)
  waiting for transfers between devices  20.6 us (22%)
    ppermute x13, starting transfers between devices, swap(): lax.ppermute(x, 'tensor', [(t, fold(fold(t) ^ mask)) for t in range(16)])  31.9 us
    ppermute x13, waiting for transfers between devices, swap(): lax.ppermute(x, 'tensor', [(t, fold(fold(t) ^ mask)) for t in range(16)])  15.1 us
    pallas_call x2, Pallas kernels, place(): pl.pallas_call(functools.partial(place_kernel, tuple((bases for _, _, _,...  6.23 us
    all_to_all x1, starting transfers between devices, on_device(): lax.all_to_all(small, 'group', split_axis=0, concat_axis=0, tiled=True)  5.95 us
    all_to_all x1, starting transfers between devices, on_device(): msg = lax.all_to_all(msg, 'group', split_axis=0, concat_axis=0, tiled=True)  5.78 us
    all_to_all x1, starting transfers between devices, on_device(): lax.all_to_all(large, 'group', split_axis=0, concat_axis=0, tiled=True)  5.73 us
    ppermute x2, waiting for transfers between devices, hand_over(): lax.ppermute(x, ('group', 'tensor'), [(g * 16 + t, (g ^ fold(t)) * 16 + f...  5.49 us
    pallas_call x1, Pallas kernels, attend(): pl.pallas_call(attend_kernel, out_shape=(jax.ShapeDtypeStruct((2 * n, out...  5.45 us
  transfers between devices with their start and end apart: 18, of which 8 were waited for; matrix products, arithmetic and copies ran while one was open for 0% of the time, Pallas kernels for 18%

profile of v4, /device:TPU:24, one launch (start us, length us, event | category | flops | bytes accessed | tf_op | source)
XLA Modules:
  0.0 94.3 jit_solution(3696569508880661576)
XLA Ops:
  0.6 1.7 %ask.1 = bf16[16,32,128]{2,1,0:T(8,128)(2,1)} custom-call(bf16[4,16,4,128]{3,2,1,0:T(4,128)(2,1)} %queries.1, bf16[4,16,128]{2,1,0:T(8,128)(2,1)} %bitcast.21, bf16[4,16,128]{2,1,0:T(8,128)(2,1)} %bitcast.23), custom_call_target="tpu_custom_call" | custom-call | bytes 400000 | tf_op jit(solution)/shard_map/ask/pallas_call | solution.py:35
  2.3 5.8 %all-to-all-start = ((bf16[16,32,128]{2,1,0:T(8,128)(2,1)}), bf16[16,32,128]{2,1,0:T(8,128)(2,1)S(1)}, u32[]{:S(2)}, u32[]{:S(2)}) async-start(bf16[16,32,128]{2,1,0:T(8,128)(2,1)} %ask.1), calls=%async_computation | async-start | bytes 262144 | tf_op jit(solution)/shard_map/all_to_all | solution.py:389
  8.1 5.3 %order_cache.1 = (bf16[16,480,128]{2,1,0:T(8,128)(2,1)}, bf16[16,288,128]{2,1,0:T(8,128)(2,1)}, s32[6,16]{1,0:T(8,128)S(1)}) custom-call(s32[256]{0:T(256)} %dest.1, s32[256]{0:T(256)} %lens.1, s32[256]{0:T(256)} %rest.1, bf16[16,512,128]{2,1,0:T(8,128)(2,1)} %bitcast.15, bf16[16,512,128]{2,1,0:T(8,128)(2,1)} %bitcast.17), custom_call_target="tpu_custom_call" | custom-call | bytes 8388608 | tf_op jit(solution)/shard_map/order_cache/pallas_call | solution.py:116
  13.5 5.7 %all-to-all-start.1 = ((bf16[16,480,128]{2,1,0:T(8,128)(2,1)}), bf16[16,480,128]{2,1,0:T(8,128)(2,1)S(1)}, u32[]{:S(2)}, u32[]{:S(2)}) async-start(bf16[16,480,128]{2,1,0:T(8,128)(2,1)} %get-tuple-element.55), calls=%async_computation.1 | async-start | bytes 3932160 | tf_op jit(solution)/shard_map/all_to_all | solution.py:396
  19.2 27.5 %conditional.2 = (f32[4,5120]{1,0:T(4,128)S(1)}, bf16[4,5120]{1,0:T(4,128)(2,1)S(1)}) conditional(s32[]{:T(128)} %convert_element_type.35, () %tuple.28, (s32[]{:T(128)}, s32[6,16]{1,0:T(8,128)S(1)}, bf16[16,32,128]{2,1,0:T(8,128)(2,1)S(1)}, bf16[16,512,128]{2,1,0:T(8,128)(2,1)}, bf16[16,512,128]{2,1,0:T(8,128)(2,1)}, ...), branch_computations={%region_0.0_spmd, %region_1.0_spmd} | conditional | flops 403349504 | bytes 14598360 | solution.py:411
  19.2 5.4 %attend.1 = (f32[32,5120]{1,0:T(8,128)S(1)}, bf16[24,5120]{1,0:T(8,128)(2,1)S(1)}, bf16[8,5120]{1,0:T(8,128)(2,1)S(1)}) custom-call(s32[1]{0:T(128)} %bitcast.turn, s32[6,16]{1,0:T(8,128)S(1)} %get-tuple-element.20.table, bf16[16,32,128]{2,1,0:T(8,128)(2,1)S(1)} %get-tuple-element.21.msg, bf16[16,512,128]{2,1,0:T(8,128)(2,1)} %get-tuple-element.22.keys, ...), custom_call_target="tpu_custom_call" | custom-call | flops 402653184 | bytes 9437184 | tf_op jit(solution)/shard_map/cond/branch_1_fun/attend/pallas_call | solution.py:219
  24.6 2.0 %collective-permute-start.2 = (bf16[8,5120]{1,0:T(8,128)(2,1)S(1)}, bf16[8,5120]{1,0:T(8,128)(2,1)S(1)}, u32[]{:S(2)}, u32[]{:S(2)}) collective-permute-start(bf16[8,5120]{1,0:T(8,128)(2,1)S(1)} %get-tuple-element.27), channel_id=1, source_target_pairs={{0,1},{1,0},{2,3},{3,2},{4,5},{5,4},{6,7},{7,6},{8,9},{9,8},{10,11... | collective-permute-start | bytes 245768 | tf_op jit(solution)/shard_map/cond/branch_1_fun/ppermute | solution.py:356
  26.7 0.1 collective-permute-start
  26.8 3.0 %collective-permute-done.2 = bf16[8,5120]{1,0:T(8,128)(2,1)S(1)} collective-permute-done((bf16[8,5120]{1,0:T(8,128)(2,1)S(1)}, bf16[8,5120]{1,0:T(8,128)(2,1)S(1)}, u32[]{:S(2)}, u32[]{:S(2)}) %collective-permute-start.2) | collective-permute-done | bytes 81952 | tf_op jit(solution)/shard_map/cond/branch_1_fun/ppermute | solution.py:356
  29.7 3.4 %collective-permute-start.3 = (bf16[8,5120]{1,0:T(8,128)(2,1)S(1)}, bf16[8,5120]{1,0:T(8,128)(2,1)S(1)}, u32[]{:S(2)}, u32[]{:S(2)}) collective-permute-start(bf16[8,5120]{1,0:T(8,128)(2,1)S(1)} %add_convert_fusion), channel_id=1, source_target_pairs={{0,2},{1,3},{2,0},{3,1},{4,6},{5,7},{6,4},{7,5},{8,10},{9,11},{10,... | collective-permute-start | bytes 245768 | tf_op jit(solution)/shard_map/cond/branch_1_fun/ppermute | solution.py:356
  33.1 3.3 %collective-permute-done = bf16[24,5120]{1,0:T(8,128)(2,1)S(1)} collective-permute-done((bf16[24,5120]{1,0:T(8,128)(2,1)S(1)}, bf16[24,5120]{1,0:T(8,128)(2,1)S(1)}, u32[]{:S(2)}, u32[]{:S(2)}) %collective-permute-start) | collective-permute-done | bytes 245792 | tf_op jit(solution)/shard_map/cond/branch_1_fun/ppermute | solution.py:356
  36.5 2.7 %collective-permute-start.1 = (bf16[8,5120]{1,0:T(8,128)(2,1)S(1)}, bf16[8,5120]{1,0:T(8,128)(2,1)S(1)}, u32[]{:S(2)}, u32[]{:S(2)}) collective-permute-start(bf16[8,5120]{1,0:T(8,128)(2,1)S(1)} %get-tuple-element.76), channel_id=1, source_target_pairs={{0,2},{1,3},{2,0},{3,1},{4,6},{5,7},{6,4},{7,5},{8,10},{9,11},{10,... | collective-permute-start | bytes 245768 | tf_op jit(solution)/shard_map/cond/branch_1_fun/ppermute | solution.py:356
  39.3 4.9 %collective-permute-start.4 = (bf16[8,5120]{1,0:T(8,128)(2,1)S(1)}, bf16[8,5120]{1,0:T(8,128)(2,1)S(1)}, u32[]{:S(2)}, u32[]{:S(2)}) collective-permute-start(bf16[8,5120]{1,0:T(8,128)(2,1)S(1)} %get-tuple-element.77), channel_id=1, source_target_pairs={{0,7},{1,6},{2,5},{3,4},{4,3},{5,2},{6,1},{7,0},{8,15},{9,14},{10,... | collective-permute-start | bytes 245768 | tf_op jit(solution)/shard_map/cond/branch_1_fun/ppermute | solution.py:356
  44.2 2.4 %collective-permute-done.4 = bf16[8,5120]{1,0:T(8,128)(2,1)S(1)} collective-permute-done((bf16[8,5120]{1,0:T(8,128)(2,1)S(1)}, bf16[8,5120]{1,0:T(8,128)(2,1)S(1)}, u32[]{:S(2)}, u32[]{:S(2)}) %collective-permute-start.4) | collective-permute-done | bytes 81952 | tf_op jit(solution)/shard_map/cond/branch_1_fun/ppermute | solution.py:356
  46.9 2.9 %collective-permute-start.9 = (bf16[16,256,128]{2,1,0:T(8,128)(2,1)S(1)}, bf16[16,256,128]{2,1,0:T(8,128)(2,1)}, u32[]{:S(2)}, u32[]{:S(2)}) collective-permute-start(bf16[16,256,128]{2,1,0:T(8,128)(2,1)S(1)} %slice.31.refs_0_), channel_id=1, source_target_pairs={{0,1},{1,0},{2,3},{3,2},{4,5},{5,4},{6,7},{7,6},{8,9},{9,8},{10,11... | collective-permute-start | bytes 3145736 | tf_op jit(solution)/shard_map/ppermute | solution.py:356
  49.8 13.4 %conditional.3 = (bf16[8,5120]{1,0:T(8,128)(2,1)S(1)}) conditional(s32[]{:T(128)} %convert_element_type.35, () %tuple.27, (bf16[4,5120]{1,0:T(4,128)(2,1)S(1)}, f32[4,5120]{1,0:T(4,128)S(1)}) %tuple.31), branch_computations={%region_2.0_spmd, %region_3.0_spmd} | conditional | flops 225280 | bytes 819328 | solution.py:420
  49.8 1.2 %collective-permute-start.5 = (bf16[4,5120]{1,0:T(4,128)(2,1)S(1)}, bf16[4,5120]{1,0:T(4,128)(2,1)S(1)}, u32[]{:S(2)}, u32[]{:S(2)}) collective-permute-start(bf16[4,5120]{1,0:T(4,128)(2,1)S(1)} %get-tuple-element.29), channel_id=1, source_target_pairs={{0,8},{1,9},{2,10},{3,11},{4,12},{5,13},{6,14},{7,15},{8,0},{9,1},... | collective-permute-start | bytes 122888 | tf_op jit(solution)/shard_map/cond/branch_1_fun/ppermute | solution.py:356
  51.0 4.3 %collective-permute-done.5 = bf16[4,5120]{1,0:T(4,128)(2,1)S(1)} collective-permute-done((bf16[4,5120]{1,0:T(4,128)(2,1)S(1)}, bf16[4,5120]{1,0:T(4,128)(2,1)S(1)}, u32[]{:S(2)}, u32[]{:S(2)}) %collective-permute-start.5) | collective-permute-done | bytes 40992 | tf_op jit(solution)/shard_map/cond/branch_1_fun/ppermute | solution.py:356
  55.3 2.3 %collective-permute-start.6 = (bf16[4,5120]{1,0:T(4,128)(2,1)S(1)}, bf16[4,5120]{1,0:T(4,128)(2,1)S(1)}, u32[]{:S(2)}, u32[]{:S(2)}) collective-permute-start(bf16[4,5120]{1,0:T(4,128)(2,1)S(1)} %add_convert_fusion.1), channel_id=1, source_target_pairs={{0,0},{1,17},{2,34},{3,51},{4,116},{5,101},{6,86},{7,71},{8,136},{... | collective-permute-start | bytes 122888 | tf_op jit(solution)/shard_map/cond/branch_1_fun/ppermute | solution.py:360
  57.7 3.5 %collective-permute-done.6 = bf16[4,5120]{1,0:T(4,128)(2,1)S(1)} collective-permute-done((bf16[4,5120]{1,0:T(4,128)(2,1)S(1)}, bf16[4,5120]{1,0:T(4,128)(2,1)S(1)}, u32[]{:S(2)}, u32[]{:S(2)}) %collective-permute-start.6) | collective-permute-done | bytes 40992 | tf_op jit(solution)/shard_map/cond/branch_1_fun/ppermute | solution.py:360
  61.2 2.0 %collective-permute-done.7 = bf16[4,5120]{1,0:T(4,128)(2,1)S(1)} collective-permute-done((bf16[4,5120]{1,0:T(4,128)(2,1)S(1)}, bf16[4,5120]{1,0:T(4,128)(2,1)S(1)}, u32[]{:S(2)}, u32[]{:S(2)}) %collective-permute-start.7) | collective-permute-done | bytes 40992 | tf_op jit(solution)/shard_map/cond/branch_1_fun/ppermute | solution.py:360
  63.2 5.9 %all-to-all-start.2 = ((bf16[16,288,128]{2,1,0:T(8,128)(2,1)}), bf16[16,288,128]{2,1,0:T(8,128)(2,1)}, u32[]{:S(2)}, u32[]{:S(2)}) async-start(bf16[16,288,128]{2,1,0:T(8,128)(2,1)} %get-tuple-element.64), calls=%async_computation.2 | async-start | bytes 2359296 | tf_op jit(solution)/shard_map/all_to_all | solution.py:431
  69.2 7.5 %collective-permute-start.8 = (bf16[8,5120]{1,0:T(8,128)(2,1)S(1)}, bf16[8,5120]{1,0:T(8,128)(2,1)S(1)}, u32[]{:S(2)}, u32[]{:S(2)}) collective-permute-start(bf16[8,5120]{1,0:T(8,128)(2,1)S(1)} %get-tuple-element.82.refs_0_), channel_id=1, source_target_pairs={{0,7},{1,6},{2,5},{3,4},{4,3},{5,2},{6,1},{7,0},{8,15},{9,14},{10,... | collective-permute-start | bytes 245768 | tf_op jit(solution)/shard_map/ppermute | solution.py:356
  76.7 0.9 collective-permute-start.10
  77.6 3.1 %place.2 = bf16[16,512,128]{2,1,0:T(8,128)(2,1)} custom-call(s32[6,16]{1,0:T(8,128)S(1)} %get-tuple-element.52.table, bf16[4,16,128]{2,1,0:T(8,128)(2,1)} %bitcast.22, bf16[16,256,128]{2,1,0:T(8,128)(2,1)} %copy-done.2, bf16[16,256,128]{2,1,0:T(8,128)(2,1)} %collective-permute-done.9.refs_1_), custom_call_target="tpu_custom_call" | custom-call | bytes 4194304 | tf_op jit(solution)/shard_map/place/pallas_call | solution.py:288
  80.7 2.1 %collective-permute-start.11 = (bf16[8,5120]{1,0:T(8,128)(2,1)S(1)}, bf16[8,5120]{1,0:T(8,128)(2,1)S(1)}, u32[]{:S(2)}, u32[]{:S(2)}) collective-permute-start(bf16[8,5120]{1,0:T(8,128)(2,1)S(1)} %collective-permute-done.8.refs_1_), channel_id=1, source_target_pairs={{0,2},{1,3},{2,0},{3,1},{4,6},{5,7},{6,4},{7,5},{8,10},{9,11},{10,... | collective-permute-start | bytes 245768 | tf_op jit(solution)/shard_map/ppermute | solution.py:356
  82.8 0.1 collective-permute-done.10.refs_2_
  83.0 1.9 %collective-permute-start.13 = (bf16[16,5120]{1,0:T(8,128)(2,1)S(1)}, bf16[16,5120]{1,0:T(8,128)(2,1)S(1)}, u32[]{:S(2)}, u32[]{:S(2)}) collective-permute-start(bf16[16,5120]{1,0:T(8,128)(2,1)S(1)} %pad_maximum_fusion.1), channel_id=1, source_target_pairs={{0,1},{1,0},{2,3},{3,2},{4,5},{5,4},{6,7},{7,6},{8,9},{9,8},{10,11... | collective-permute-start | bytes 491528 | tf_op jit(solution)/shard_map/ppermute | solution.py:356
  84.9 2.0 %collective-permute-done.11.refs_3_ = bf16[8,5120]{1,0:T(8,128)(2,1)S(1)} collective-permute-done((bf16[8,5120]{1,0:T(8,128)(2,1)S(1)}, bf16[8,5120]{1,0:T(8,128)(2,1)S(1)}, u32[]{:S(2)}, u32[]{:S(2)}) %collective-permute-start.11) | collective-permute-done | bytes 81952 | tf_op jit(solution)/shard_map/ppermute | solution.py:356
  86.8 2.2 %collective-permute-start.14 = (bf16[8,5120]{1,0:T(8,128)(2,1)S(1)}, bf16[8,5120]{1,0:T(8,128)(2,1)S(1)}, u32[]{:S(2)}, u32[]{:S(2)}) collective-permute-start(bf16[8,5120]{1,0:T(8,128)(2,1)S(1)} %collective-permute-done.11.refs_3_), channel_id=1, source_target_pairs={{0,1},{1,0},{2,3},{3,2},{4,5},{5,4},{6,7},{7,6},{8,9},{9,8},{10,11... | collective-permute-start | bytes 245768 | tf_op jit(solution)/shard_map/ppermute | solution.py:356
  89.1 3.1 %place.3 = bf16[16,512,128]{2,1,0:T(8,128)(2,1)} custom-call(s32[6,16]{1,0:T(8,128)S(1)} %get-tuple-element.52.table, bf16[4,16,128]{2,1,0:T(8,128)(2,1)} %bitcast.24, bf16[16,480,128]{2,1,0:T(8,128)(2,1)} %copy-done.1, bf16[16,288,128]{2,1,0:T(8,128)(2,1)} %all-to-all-done.2.refs_1_), custom_call_target="tpu_custom_call" | custom-call | bytes 4194304 | tf_op jit(solution)/shard_map/place/pallas_call | solution.py:288
  92.2 2.1 %finish.1 = (bf16[64,5120]{1,0:T(8,128)(2,1)}, bf16[64,5120]{1,0:T(8,128)(2,1)}) custom-call(s32[6,16]{1,0:T(8,128)S(1)} %get-tuple-element.52.table, bf16[8,5120]{1,0:T(8,128)(2,1)S(1)} %get-tuple-element.82.refs_0_, bf16[8,5120]{1,0:T(8,128)(2,1)S(1)} %collective-permute-done.8.refs_1_, bf16[8,5120]{1,0:T(8,128)(2,1)S(1)} %collective-permute-done.10.refs_2_, ...), custom_call_target="tpu_custom_call" | custom-call | flops 41943040 | bytes 2621440 | tf_op jit(solution)/shard_map/finish/pallas_call | solution.py:341
  (31 shorter events, 0.5 us)
Async XLA Ops:
  2.3 11.1 %all-to-all-start = ((bf16[16,32,128]{2,1,0:T(8,128)(2,1)}), bf16[16,32,128]{2,1,0:T(8,128)(2,1)S(1)}, u32[]{:S(2)}, u32[]{:S(2)}) async-start(bf16[16,32,128]{2,1,0:T(8,128)(2,1)} %ask.1), calls=%async_computation | async-start | bytes 262144 | tf_op jit(solution)/shard_map/all_to_all | solution.py:389
  13.5 33.3 %all-to-all-start.1 = ((bf16[16,480,128]{2,1,0:T(8,128)(2,1)}), bf16[16,480,128]{2,1,0:T(8,128)(2,1)S(1)}, u32[]{:S(2)}, u32[]{:S(2)}) async-start(bf16[16,480,128]{2,1,0:T(8,128)(2,1)} %get-tuple-element.55), calls=%async_computation.1 | async-start | bytes 3932160 | tf_op jit(solution)/shard_map/all_to_all | solution.py:396
  24.6 5.1 %collective-permute-start.2 = (bf16[8,5120]{1,0:T(8,128)(2,1)S(1)}, bf16[8,5120]{1,0:T(8,128)(2,1)S(1)}, u32[]{:S(2)}, u32[]{:S(2)}) collective-permute-start(bf16[8,5120]{1,0:T(8,128)(2,1)S(1)} %get-tuple-element.27), channel_id=1, source_target_pairs={{0,1},{1,0},{2,3},{3,2},{4,5},{5,4},{6,7},{7,6},{8,9},{9,8},{10,11... | collective-permute-start | bytes 245768 | tf_op jit(solution)/shard_map/cond/branch_1_fun/ppermute | solution.py:356
  26.7 9.8 %collective-permute-start = (bf16[24,5120]{1,0:T(8,128)(2,1)S(1)}, bf16[24,5120]{1,0:T(8,128)(2,1)S(1)}, u32[]{:S(2)}, u32[]{:S(2)}) collective-permute-start(bf16[24,5120]{1,0:T(8,128)(2,1)S(1)} %get-tuple-element.26), channel_id=1, source_target_pairs={{0,1},{1,0},{2,3},{3,2},{4,5},{5,4},{6,7},{7,6},{8,9},{9,8},{10,11... | collective-permute-start | bytes 737288 | tf_op jit(solution)/shard_map/cond/branch_1_fun/ppermute | solution.py:356
  29.7 6.7 %collective-permute-start.3 = (bf16[8,5120]{1,0:T(8,128)(2,1)S(1)}, bf16[8,5120]{1,0:T(8,128)(2,1)S(1)}, u32[]{:S(2)}, u32[]{:S(2)}) collective-permute-start(bf16[8,5120]{1,0:T(8,128)(2,1)S(1)} %add_convert_fusion), channel_id=1, source_target_pairs={{0,2},{1,3},{2,0},{3,1},{4,6},{5,7},{6,4},{7,5},{8,10},{9,11},{10,... | collective-permute-start | bytes 245768 | tf_op jit(solution)/shard_map/cond/branch_1_fun/ppermute | solution.py:356
  36.5 7.7 %collective-permute-start.1 = (bf16[8,5120]{1,0:T(8,128)(2,1)S(1)}, bf16[8,5120]{1,0:T(8,128)(2,1)S(1)}, u32[]{:S(2)}, u32[]{:S(2)}) collective-permute-start(bf16[8,5120]{1,0:T(8,128)(2,1)S(1)} %get-tuple-element.76), channel_id=1, source_target_pairs={{0,2},{1,3},{2,0},{3,1},{4,6},{5,7},{6,4},{7,5},{8,10},{9,11},{10,... | collective-permute-start | bytes 245768 | tf_op jit(solution)/shard_map/cond/branch_1_fun/ppermute | solution.py:356
  39.3 7.4 %collective-permute-start.4 = (bf16[8,5120]{1,0:T(8,128)(2,1)S(1)}, bf16[8,5120]{1,0:T(8,128)(2,1)S(1)}, u32[]{:S(2)}, u32[]{:S(2)}) collective-permute-start(bf16[8,5120]{1,0:T(8,128)(2,1)S(1)} %get-tuple-element.77), channel_id=1, source_target_pairs={{0,7},{1,6},{2,5},{3,4},{4,3},{5,2},{6,1},{7,0},{8,15},{9,14},{10,... | collective-permute-start | bytes 245768 | tf_op jit(solution)/shard_map/cond/branch_1_fun/ppermute | solution.py:356
  46.8 16.5 %copy-start.1 = (bf16[16,480,128]{2,1,0:T(8,128)(2,1)}, bf16[16,480,128]{2,1,0:T(8,128)(2,1)S(1)}, u32[]{:S(2)}) copy-start(bf16[16,480,128]{2,1,0:T(8,128)(2,1)S(1)} %all-to-all-done.1.refs_0_) | copy-start | bytes 5898244
  46.9 30.7 %copy-start.2 = (bf16[16,256,128]{2,1,0:T(8,128)(2,1)}, bf16[16,256,128]{2,1,0:T(8,128)(2,1)S(1)}, u32[]{:S(2)}) copy-start(bf16[16,256,128]{2,1,0:T(8,128)(2,1)S(1)} %slice.31.refs_0_) | copy-start | bytes 3145732
  46.9 30.7 %collective-permute-start.9 = (bf16[16,256,128]{2,1,0:T(8,128)(2,1)S(1)}, bf16[16,256,128]{2,1,0:T(8,128)(2,1)}, u32[]{:S(2)}, u32[]{:S(2)}) collective-permute-start(bf16[16,256,128]{2,1,0:T(8,128)(2,1)S(1)} %slice.31.refs_0_), channel_id=1, source_target_pairs={{0,1},{1,0},{2,3},{3,2},{4,5},{5,4},{6,7},{7,6},{8,9},{9,8},{10,11... | collective-permute-start | bytes 3145736 | tf_op jit(solution)/shard_map/ppermute | solution.py:356
  49.8 5.5 %collective-permute-start.5 = (bf16[4,5120]{1,0:T(4,128)(2,1)S(1)}, bf16[4,5120]{1,0:T(4,128)(2,1)S(1)}, u32[]{:S(2)}, u32[]{:S(2)}) collective-permute-start(bf16[4,5120]{1,0:T(4,128)(2,1)S(1)} %get-tuple-element.29), channel_id=1, source_target_pairs={{0,8},{1,9},{2,10},{3,11},{4,12},{5,13},{6,14},{7,15},{8,0},{9,1},... | collective-permute-start | bytes 122888 | tf_op jit(solution)/shard_map/cond/branch_1_fun/ppermute | solution.py:356
  55.3 5.9 %collective-permute-start.6 = (bf16[4,5120]{1,0:T(4,128)(2,1)S(1)}, bf16[4,5120]{1,0:T(4,128)(2,1)S(1)}, u32[]{:S(2)}, u32[]{:S(2)}) collective-permute-start(bf16[4,5120]{1,0:T(4,128)(2,1)S(1)} %add_convert_fusion.1), channel_id=1, source_target_pairs={{0,0},{1,17},{2,34},{3,51},{4,116},{5,101},{6,86},{7,71},{8,136},{... | collective-permute-start | bytes 122888 | tf_op jit(solution)/shard_map/cond/branch_1_fun/ppermute | solution.py:360
  57.6 5.6 %collective-permute-start.7 = (bf16[4,5120]{1,0:T(4,128)(2,1)S(1)}, bf16[4,5120]{1,0:T(4,128)(2,1)S(1)}, u32[]{:S(2)}, u32[]{:S(2)}) collective-permute-start(bf16[4,5120]{1,0:T(4,128)(2,1)S(1)} %add_convert_fusion.1), channel_id=1, source_target_pairs={{0,8},{1,25},{2,42},{3,59},{4,124},{5,109},{6,94},{7,79},{8,128},{... | collective-permute-start | bytes 122888 | tf_op jit(solution)/shard_map/cond/branch_1_fun/ppermute | solution.py:360
  63.2 25.8 %all-to-all-start.2 = ((bf16[16,288,128]{2,1,0:T(8,128)(2,1)}), bf16[16,288,128]{2,1,0:T(8,128)(2,1)}, u32[]{:S(2)}, u32[]{:S(2)}) async-start(bf16[16,288,128]{2,1,0:T(8,128)(2,1)} %get-tuple-element.64), calls=%async_computation.2 | async-start | bytes 2359296 | tf_op jit(solution)/shard_map/all_to_all | solution.py:431
  69.2 19.8 %copy-start.3 = (bf16[5120]{0:T(1024)(128)(2,1)S(1)}, bf16[5120]{0:T(1024)(128)(2,1)}, u32[]{:S(2)}) copy-start(bf16[5120]{0:T(1024)(128)(2,1)} %param.25) | copy-start | bytes 30724
  69.2 11.5 %collective-permute-start.8 = (bf16[8,5120]{1,0:T(8,128)(2,1)S(1)}, bf16[8,5120]{1,0:T(8,128)(2,1)S(1)}, u32[]{:S(2)}, u32[]{:S(2)}) collective-permute-start(bf16[8,5120]{1,0:T(8,128)(2,1)S(1)} %get-tuple-element.82.refs_0_), channel_id=1, source_target_pairs={{0,7},{1,6},{2,5},{3,4},{4,3},{5,2},{6,1},{7,0},{8,15},{9,14},{10,... | collective-permute-start | bytes 245768 | tf_op jit(solution)/shard_map/ppermute | solution.py:356
  76.7 6.2 %collective-permute-start.10 = (bf16[8,5120]{1,0:T(8,128)(2,1)S(1)}, bf16[8,5120]{1,0:T(8,128)(2,1)S(1)}, u32[]{:S(2)}, u32[]{:S(2)}) collective-permute-start(bf16[8,5120]{1,0:T(8,128)(2,1)S(1)} %get-tuple-element.82.refs_0_), channel_id=1, source_target_pairs={{0,2},{1,3},{2,0},{3,1},{4,6},{5,7},{6,4},{7,5},{8,10},{9,11},{10,... | collective-permute-start | bytes 245768 | tf_op jit(solution)/shard_map/ppermute | solution.py:356
  77.6 7.3 %collective-permute-start.12 = (bf16[8,5120]{1,0:T(8,128)(2,1)S(1)}, bf16[8,5120]{1,0:T(8,128)(2,1)S(1)}, u32[]{:S(2)}, u32[]{:S(2)}) collective-permute-start(bf16[8,5120]{1,0:T(8,128)(2,1)S(1)} %get-tuple-element.82.refs_0_), channel_id=1, source_target_pairs={{0,1},{1,0},{2,3},{3,2},{4,5},{5,4},{6,7},{7,6},{8,9},{9,8},{10,11... | collective-permute-start | bytes 245768 | tf_op jit(solution)/shard_map/ppermute | solution.py:356
  80.7 6.1 %collective-permute-start.11 = (bf16[8,5120]{1,0:T(8,128)(2,1)S(1)}, bf16[8,5120]{1,0:T(8,128)(2,1)S(1)}, u32[]{:S(2)}, u32[]{:S(2)}) collective-permute-start(bf16[8,5120]{1,0:T(8,128)(2,1)S(1)} %collective-permute-done.8.refs_1_), channel_id=1, source_target_pairs={{0,2},{1,3},{2,0},{3,1},{4,6},{5,7},{6,4},{7,5},{8,10},{9,11},{10,... | collective-permute-start | bytes 245768 | tf_op jit(solution)/shard_map/ppermute | solution.py:356
  83.0 9.2 %collective-permute-start.13 = (bf16[16,5120]{1,0:T(8,128)(2,1)S(1)}, bf16[16,5120]{1,0:T(8,128)(2,1)S(1)}, u32[]{:S(2)}, u32[]{:S(2)}) collective-permute-start(bf16[16,5120]{1,0:T(8,128)(2,1)S(1)} %pad_maximum_fusion.1), channel_id=1, source_target_pairs={{0,1},{1,0},{2,3},{3,2},{4,5},{5,4},{6,7},{7,6},{8,9},{9,8},{10,11... | collective-permute-start | bytes 491528 | tf_op jit(solution)/shard_map/ppermute | solution.py:356
  86.8 5.4 %collective-permute-start.14 = (bf16[8,5120]{1,0:T(8,128)(2,1)S(1)}, bf16[8,5120]{1,0:T(8,128)(2,1)S(1)}, u32[]{:S(2)}, u32[]{:S(2)}) collective-permute-start(bf16[8,5120]{1,0:T(8,128)(2,1)S(1)} %collective-permute-done.11.refs_3_), channel_id=1, source_target_pairs={{0,1},{1,0},{2,3},{3,2},{4,5},{5,4},{6,7},{7,6},{8,9},{9,8},{10,11... | collective-permute-start | bytes 245768 | tf_op jit(solution)/shard_map/ppermute | solution.py:356
  89.0 3.2 %copy-start = (bf16[4,16,5120]{2,1,0:T(8,128)(2,1)S(1)}, bf16[4,16,5120]{2,1,0:T(8,128)(2,1)}, u32[]{:S(2)}) copy-start(bf16[4,16,5120]{2,1,0:T(8,128)(2,1)} %param.23) | copy-start | bytes 1966084

commit v5 on v4

--- a/solution.py
+++ b/solution.py
@@ -435,10 +435,9 @@
         (key_share, 0, share, (0, share)),
         (key_other, 0, share, (share, 0)),
     )
-    by4, key_out = lax.optimization_barrier((by4, key_out))
     by42 = swap(by4, 2)
     later = swap(jnp.concatenate([by4, by2], axis=0), 1)
-    by42, by1 = lax.optimization_barrier((by42, by1))
+    by42, by1, key_out = lax.optimization_barrier((by42, by1, key_out))
     last = swap(by42, 1)
     value_out = place(
         table,

time: 94.7 us -> 94.2 us (level)
  starting transfers between devices: 51.7 us -> 50.1 us
    ppermute x13, starting transfers between devices: 31.9 us -> 30.3 us  [swap(): lax.ppermute(x, 'tensor', [(t, fold(fold(t) ^ mask)) for t in range(16)])]
  transfers between devices with their start and end apart: 18 -> 18, of which waited for: 8 -> 10; matrix products, arithmetic and copies ran while one was open for 0% -> 0% of each run, Pallas kernels for 18% -> 18%
where the time goes in v5:
time: 94.2 us; the launch traced here: 93.5 us
  starting transfers between devices  50.1 us (53%)
  waiting for transfers between devices  21.4 us (23%)
  Pallas kernels  20.8 us (22%)
    ppermute x13, starting transfers between devices, swap(): lax.ppermute(x, 'tensor', [(t, fold(fold(t) ^ mask)) for t in range(16)])  30.3 us
    ppermute x13, waiting for transfers between devices, swap(): lax.ppermute(x, 'tensor', [(t, fold(fold(t) ^ mask)) for t in range(16)])  15.9 us
    pallas_call x2, Pallas kernels, place(): pl.pallas_call(functools.partial(place_kernel, tuple((bases for _, _, _,...  6.22 us
    all_to_all x1, starting transfers between devices, on_device(): lax.all_to_all(small, 'group', split_axis=0, concat_axis=0, tiled=True)  5.95 us
    all_to_all x1, starting transfers between devices, on_device(): msg = lax.all_to_all(msg, 'group', split_axis=0, concat_axis=0, tiled=True)  5.78 us
    all_to_all x1, starting transfers between devices, on_device(): lax.all_to_all(large, 'group', split_axis=0, concat_axis=0, tiled=True)  5.73 us
    ppermute x2, waiting for transfers between devices, hand_over(): lax.ppermute(x, ('group', 'tensor'), [(g * 16 + t, (g ^ fold(t)) * 16 + f...  5.49 us
    pallas_call x1, Pallas kernels, attend(): pl.pallas_call(attend_kernel, out_shape=(jax.ShapeDtypeStruct((2 * n, out...  5.45 us
  transfers between devices with their start and end apart: 18, of which 10 were waited for; matrix products, arithmetic and copies ran while one was open for 0% of the time, Pallas kernels for 18%

profile of v5, /device:TPU:24, one launch (start us, length us, event | category | flops | bytes accessed | tf_op | source)
XLA Modules:
  0.0 93.5 jit_solution(959015512004680966)
XLA Ops:
  0.6 1.7 %ask.1 = bf16[16,32,128]{2,1,0:T(8,128)(2,1)} custom-call(bf16[4,16,4,128]{3,2,1,0:T(4,128)(2,1)} %queries.1, bf16[4,16,128]{2,1,0:T(8,128)(2,1)} %bitcast.21, bf16[4,16,128]{2,1,0:T(8,128)(2,1)} %bitcast.23), custom_call_target="tpu_custom_call" | custom-call | bytes 400000 | tf_op jit(solution)/shard_map/ask/pallas_call | solution.py:35
  2.3 5.8 %all-to-all-start = ((bf16[16,32,128]{2,1,0:T(8,128)(2,1)}), bf16[16,32,128]{2,1,0:T(8,128)(2,1)S(1)}, u32[]{:S(2)}, u32[]{:S(2)}) async-start(bf16[16,32,128]{2,1,0:T(8,128)(2,1)} %ask.1), calls=%async_computation | async-start | bytes 262144 | tf_op jit(solution)/shard_map/all_to_all | solution.py:389
  8.1 5.3 %order_cache.1 = (bf16[16,480,128]{2,1,0:T(8,128)(2,1)}, bf16[16,288,128]{2,1,0:T(8,128)(2,1)}, s32[6,16]{1,0:T(8,128)S(1)}) custom-call(s32[256]{0:T(256)} %dest.1, s32[256]{0:T(256)} %lens.1, s32[256]{0:T(256)} %rest.1, bf16[16,512,128]{2,1,0:T(8,128)(2,1)} %bitcast.15, bf16[16,512,128]{2,1,0:T(8,128)(2,1)} %bitcast.17), custom_call_target="tpu_custom_call" | custom-call | bytes 8388608 | tf_op jit(solution)/shard_map/order_cache/pallas_call | solution.py:116
  13.5 5.7 %all-to-all-start.1 = ((bf16[16,480,128]{2,1,0:T(8,128)(2,1)}), bf16[16,480,128]{2,1,0:T(8,128)(2,1)S(1)}, u32[]{:S(2)}, u32[]{:S(2)}) async-start(bf16[16,480,128]{2,1,0:T(8,128)(2,1)} %get-tuple-element.54), calls=%async_computation.1 | async-start | bytes 3932160 | tf_op jit(solution)/shard_map/all_to_all | solution.py:396
  19.2 27.5 %conditional.2 = (f32[4,5120]{1,0:T(4,128)S(1)}, bf16[4,5120]{1,0:T(4,128)(2,1)S(1)}) conditional(s32[]{:T(128)} %convert_element_type.35, () %tuple.27, (s32[]{:T(128)}, s32[6,16]{1,0:T(8,128)S(1)}, bf16[16,32,128]{2,1,0:T(8,128)(2,1)S(1)}, bf16[16,512,128]{2,1,0:T(8,128)(2,1)}, bf16[16,512,128]{2,1,0:T(8,128)(2,1)}, ...), branch_computations={%region_0.0_spmd, %region_1.0_spmd} | conditional | flops 403349504 | bytes 14598360 | solution.py:411
  19.2 5.4 %attend.1 = (f32[32,5120]{1,0:T(8,128)S(1)}, bf16[24,5120]{1,0:T(8,128)(2,1)S(1)}, bf16[8,5120]{1,0:T(8,128)(2,1)S(1)}) custom-call(s32[1]{0:T(128)} %bitcast.turn, s32[6,16]{1,0:T(8,128)S(1)} %get-tuple-element.20.table, bf16[16,32,128]{2,1,0:T(8,128)(2,1)S(1)} %get-tuple-element.21.msg, bf16[16,512,128]{2,1,0:T(8,128)(2,1)} %get-tuple-element.22.keys, ...), custom_call_target="tpu_custom_call" | custom-call | flops 402653184 | bytes 9437184 | tf_op jit(solution)/shard_map/cond/branch_1_fun/attend/pallas_call | solution.py:219
  24.6 2.0 %collective-permute-start.2 = (bf16[8,5120]{1,0:T(8,128)(2,1)S(1)}, bf16[8,5120]{1,0:T(8,128)(2,1)S(1)}, u32[]{:S(2)}, u32[]{:S(2)}) collective-permute-start(bf16[8,5120]{1,0:T(8,128)(2,1)S(1)} %get-tuple-element.27), channel_id=1, source_target_pairs={{0,1},{1,0},{2,3},{3,2},{4,5},{5,4},{6,7},{7,6},{8,9},{9,8},{10,11... | collective-permute-start | bytes 245768 | tf_op jit(solution)/shard_map/cond/branch_1_fun/ppermute | solution.py:356
  26.7 0.1 collective-permute-start
  26.8 3.0 %collective-permute-done.2 = bf16[8,5120]{1,0:T(8,128)(2,1)S(1)} collective-permute-done((bf16[8,5120]{1,0:T(8,128)(2,1)S(1)}, bf16[8,5120]{1,0:T(8,128)(2,1)S(1)}, u32[]{:S(2)}, u32[]{:S(2)}) %collective-permute-start.2) | collective-permute-done | bytes 81952 | tf_op jit(solution)/shard_map/cond/branch_1_fun/ppermute | solution.py:356
  29.7 3.4 %collective-permute-start.3 = (bf16[8,5120]{1,0:T(8,128)(2,1)S(1)}, bf16[8,5120]{1,0:T(8,128)(2,1)S(1)}, u32[]{:S(2)}, u32[]{:S(2)}) collective-permute-start(bf16[8,5120]{1,0:T(8,128)(2,1)S(1)} %add_convert_fusion), channel_id=1, source_target_pairs={{0,2},{1,3},{2,0},{3,1},{4,6},{5,7},{6,4},{7,5},{8,10},{9,11},{10,... | collective-permute-start | bytes 245768 | tf_op jit(solution)/shard_map/cond/branch_1_fun/ppermute | solution.py:356
  33.1 3.3 %collective-permute-done = bf16[24,5120]{1,0:T(8,128)(2,1)S(1)} collective-permute-done((bf16[24,5120]{1,0:T(8,128)(2,1)S(1)}, bf16[24,5120]{1,0:T(8,128)(2,1)S(1)}, u32[]{:S(2)}, u32[]{:S(2)}) %collective-permute-start) | collective-permute-done | bytes 245792 | tf_op jit(solution)/shard_map/cond/branch_1_fun/ppermute | solution.py:356
  36.5 2.7 %collective-permute-start.1 = (bf16[8,5120]{1,0:T(8,128)(2,1)S(1)}, bf16[8,5120]{1,0:T(8,128)(2,1)S(1)}, u32[]{:S(2)}, u32[]{:S(2)}) collective-permute-start(bf16[8,5120]{1,0:T(8,128)(2,1)S(1)} %get-tuple-element.74), channel_id=1, source_target_pairs={{0,2},{1,3},{2,0},{3,1},{4,6},{5,7},{6,4},{7,5},{8,10},{9,11},{10,... | collective-permute-start | bytes 245768 | tf_op jit(solution)/shard_map/cond/branch_1_fun/ppermute | solution.py:356
  39.3 4.9 %collective-permute-start.4 = (bf16[8,5120]{1,0:T(8,128)(2,1)S(1)}, bf16[8,5120]{1,0:T(8,128)(2,1)S(1)}, u32[]{:S(2)}, u32[]{:S(2)}) collective-permute-start(bf16[8,5120]{1,0:T(8,128)(2,1)S(1)} %get-tuple-element.75), channel_id=1, source_target_pairs={{0,7},{1,6},{2,5},{3,4},{4,3},{5,2},{6,1},{7,0},{8,15},{9,14},{10,... | collective-permute-start | bytes 245768 | tf_op jit(solution)/shard_map/cond/branch_1_fun/ppermute | solution.py:356
  44.2 2.4 %collective-permute-done.4 = bf16[8,5120]{1,0:T(8,128)(2,1)S(1)} collective-permute-done((bf16[8,5120]{1,0:T(8,128)(2,1)S(1)}, bf16[8,5120]{1,0:T(8,128)(2,1)S(1)}, u32[]{:S(2)}, u32[]{:S(2)}) %collective-permute-start.4) | collective-permute-done | bytes 81952 | tf_op jit(solution)/shard_map/cond/branch_1_fun/ppermute | solution.py:356
  46.9 2.9 %collective-permute-start.12 = (bf16[16,256,128]{2,1,0:T(8,128)(2,1)S(1)}, bf16[16,256,128]{2,1,0:T(8,128)(2,1)}, u32[]{:S(2)}, u32[]{:S(2)}) collective-permute-start(bf16[16,256,128]{2,1,0:T(8,128)(2,1)S(1)} %slice.31.refs_0_), channel_id=1, source_target_pairs={{0,1},{1,0},{2,3},{3,2},{4,5},{5,4},{6,7},{7,6},{8,9},{9,8},{10,11... | collective-permute-start | bytes 3145736 | tf_op jit(solution)/shard_map/ppermute | solution.py:356
  49.8 13.4 %conditional.3 = (bf16[8,5120]{1,0:T(8,128)(2,1)S(1)}) conditional(s32[]{:T(128)} %convert_element_type.35, () %tuple.26, (bf16[4,5120]{1,0:T(4,128)(2,1)S(1)}, f32[4,5120]{1,0:T(4,128)S(1)}) %tuple.30), branch_computations={%region_2.0_spmd, %region_3.0_spmd} | conditional | flops 225280 | bytes 819328 | solution.py:420
  49.8 1.2 %collective-permute-start.5 = (bf16[4,5120]{1,0:T(4,128)(2,1)S(1)}, bf16[4,5120]{1,0:T(4,128)(2,1)S(1)}, u32[]{:S(2)}, u32[]{:S(2)}) collective-permute-start(bf16[4,5120]{1,0:T(4,128)(2,1)S(1)} %get-tuple-element.29), channel_id=1, source_target_pairs={{0,8},{1,9},{2,10},{3,11},{4,12},{5,13},{6,14},{7,15},{8,0},{9,1},... | collective-permute-start | bytes 122888 | tf_op jit(solution)/shard_map/cond/branch_1_fun/ppermute | solution.py:356
  51.0 4.3 %collective-permute-done.5 = bf16[4,5120]{1,0:T(4,128)(2,1)S(1)} collective-permute-done((bf16[4,5120]{1,0:T(4,128)(2,1)S(1)}, bf16[4,5120]{1,0:T(4,128)(2,1)S(1)}, u32[]{:S(2)}, u32[]{:S(2)}) %collective-permute-start.5) | collective-permute-done | bytes 40992 | tf_op jit(solution)/shard_map/cond/branch_1_fun/ppermute | solution.py:356
  55.3 2.3 %collective-permute-start.6 = (bf16[4,5120]{1,0:T(4,128)(2,1)S(1)}, bf16[4,5120]{1,0:T(4,128)(2,1)S(1)}, u32[]{:S(2)}, u32[]{:S(2)}) collective-permute-start(bf16[4,5120]{1,0:T(4,128)(2,1)S(1)} %add_convert_fusion.1), channel_id=1, source_target_pairs={{0,0},{1,17},{2,34},{3,51},{4,116},{5,101},{6,86},{7,71},{8,136},{... | collective-permute-start | bytes 122888 | tf_op jit(solution)/shard_map/cond/branch_1_fun/ppermute | solution.py:360
  57.7 3.5 %collective-permute-done.6 = bf16[4,5120]{1,0:T(4,128)(2,1)S(1)} collective-permute-done((bf16[4,5120]{1,0:T(4,128)(2,1)S(1)}, bf16[4,5120]{1,0:T(4,128)(2,1)S(1)}, u32[]{:S(2)}, u32[]{:S(2)}) %collective-permute-start.6) | collective-permute-done | bytes 40992 | tf_op jit(solution)/shard_map/cond/branch_1_fun/ppermute | solution.py:360
  61.2 2.0 %collective-permute-done.7 = bf16[4,5120]{1,0:T(4,128)(2,1)S(1)} collective-permute-done((bf16[4,5120]{1,0:T(4,128)(2,1)S(1)}, bf16[4,5120]{1,0:T(4,128)(2,1)S(1)}, u32[]{:S(2)}, u32[]{:S(2)}) %collective-permute-start.7) | collective-permute-done | bytes 40992 | tf_op jit(solution)/shard_map/cond/branch_1_fun/ppermute | solution.py:360
  63.2 5.9 %all-to-all-start.2 = ((bf16[16,288,128]{2,1,0:T(8,128)(2,1)}), bf16[16,288,128]{2,1,0:T(8,128)(2,1)}, u32[]{:S(2)}, u32[]{:S(2)}) async-start(bf16[16,288,128]{2,1,0:T(8,128)(2,1)} %get-tuple-element.62), calls=%async_computation.2 | async-start | bytes 2359296 | tf_op jit(solution)/shard_map/all_to_all | solution.py:431
  69.2 7.4 %collective-permute-start.8 = (bf16[8,5120]{1,0:T(8,128)(2,1)S(1)}, bf16[8,5120]{1,0:T(8,128)(2,1)S(1)}, u32[]{:S(2)}, u32[]{:S(2)}) collective-permute-start(bf16[8,5120]{1,0:T(8,128)(2,1)S(1)} %get-tuple-element.80.refs_0_), channel_id=1, source_target_pairs={{0,7},{1,6},{2,5},{3,4},{4,3},{5,2},{6,1},{7,0},{8,15},{9,14},{10,... | collective-permute-start | bytes 245768 | tf_op jit(solution)/shard_map/ppermute | solution.py:356
  76.6 0.9 collective-permute-start.9
  77.5 2.4 %collective-permute-done.8.refs_1_ = bf16[8,5120]{1,0:T(8,128)(2,1)S(1)} collective-permute-done((bf16[8,5120]{1,0:T(8,128)(2,1)S(1)}, bf16[8,5120]{1,0:T(8,128)(2,1)S(1)}, u32[]{:S(2)}, u32[]{:S(2)}) %collective-permute-start.8) | collective-permute-done | bytes 81952 | tf_op jit(solution)/shard_map/ppermute | solution.py:356
  79.9 2.6 %collective-permute-start.10 = (bf16[8,5120]{1,0:T(8,128)(2,1)S(1)}, bf16[8,5120]{1,0:T(8,128)(2,1)S(1)}, u32[]{:S(2)}, u32[]{:S(2)}) collective-permute-start(bf16[8,5120]{1,0:T(8,128)(2,1)S(1)} %collective-permute-done.8.refs_1_), channel_id=1, source_target_pairs={{0,2},{1,3},{2,0},{3,1},{4,6},{5,7},{6,4},{7,5},{8,10},{9,11},{10,... | collective-permute-start | bytes 245768 | tf_op jit(solution)/shard_map/ppermute | solution.py:356
  82.5 0.4 collective-permute-done.9.refs_2_
  82.9 0.9 collective-permute-start.13
  83.8 3.1 %place.2 = bf16[16,512,128]{2,1,0:T(8,128)(2,1)} custom-call(s32[6,16]{1,0:T(8,128)S(1)} %get-tuple-element.51.table, bf16[4,16,128]{2,1,0:T(8,128)(2,1)} %bitcast.22, bf16[16,256,128]{2,1,0:T(8,128)(2,1)} %copy-done.2, bf16[16,256,128]{2,1,0:T(8,128)(2,1)} %collective-permute-done.12.refs_1_), custom_call_target="tpu_custom_call" | custom-call | bytes 4194304 | tf_op jit(solution)/shard_map/place/pallas_call | solution.py:288
  87.0 1.2 %collective-permute-start.14 = (bf16[8,5120]{1,0:T(8,128)(2,1)S(1)}, bf16[8,5120]{1,0:T(8,128)(2,1)S(1)}, u32[]{:S(2)}, u32[]{:S(2)}) collective-permute-start(bf16[8,5120]{1,0:T(8,128)(2,1)S(1)} %collective-permute-done.10.refs_3_), channel_id=1, source_target_pairs={{0,1},{1,0},{2,3},{3,2},{4,5},{5,4},{6,7},{7,6},{8,9},{9,8},{10,11... | collective-permute-start | bytes 245768 | tf_op jit(solution)/shard_map/ppermute | solution.py:356
  88.2 3.1 %place.3 = bf16[16,512,128]{2,1,0:T(8,128)(2,1)} custom-call(s32[6,16]{1,0:T(8,128)S(1)} %get-tuple-element.51.table, bf16[4,16,128]{2,1,0:T(8,128)(2,1)} %bitcast.24, bf16[16,480,128]{2,1,0:T(8,128)(2,1)} %copy-done.1, bf16[16,288,128]{2,1,0:T(8,128)(2,1)} %all-to-all-done.2.refs_1_), custom_call_target="tpu_custom_call" | custom-call | bytes 4194304 | tf_op jit(solution)/shard_map/place/pallas_call | solution.py:288
  91.4 2.1 %finish.1 = (bf16[64,5120]{1,0:T(8,128)(2,1)}, bf16[64,5120]{1,0:T(8,128)(2,1)}) custom-call(s32[6,16]{1,0:T(8,128)S(1)} %get-tuple-element.51.table, bf16[8,5120]{1,0:T(8,128)(2,1)S(1)} %get-tuple-element.80.refs_0_, bf16[8,5120]{1,0:T(8,128)(2,1)S(1)} %collective-permute-done.8.refs_1_, bf16[8,5120]{1,0:T(8,128)(2,1)S(1)} %collective-permute-done.9.refs_2_, ...), custom_call_target="tpu_custom_call" | custom-call | flops 41943040 | bytes 2621440 | tf_op jit(solution)/shard_map/finish/pallas_call | solution.py:341
  (31 shorter events, 0.6 us)
Async XLA Ops:
  2.3 11.1 %all-to-all-start = ((bf16[16,32,128]{2,1,0:T(8,128)(2,1)}), bf16[16,32,128]{2,1,0:T(8,128)(2,1)S(1)}, u32[]{:S(2)}, u32[]{:S(2)}) async-start(bf16[16,32,128]{2,1,0:T(8,128)(2,1)} %ask.1), calls=%async_computation | async-start | bytes 262144 | tf_op jit(solution)/shard_map/all_to_all | solution.py:389
  13.5 33.3 %all-to-all-start.1 = ((bf16[16,480,128]{2,1,0:T(8,128)(2,1)}), bf16[16,480,128]{2,1,0:T(8,128)(2,1)S(1)}, u32[]{:S(2)}, u32[]{:S(2)}) async-start(bf16[16,480,128]{2,1,0:T(8,128)(2,1)} %get-tuple-element.54), calls=%async_computation.1 | async-start | bytes 3932160 | tf_op jit(solution)/shard_map/all_to_all | solution.py:396
  24.6 5.1 %collective-permute-start.2 = (bf16[8,5120]{1,0:T(8,128)(2,1)S(1)}, bf16[8,5120]{1,0:T(8,128)(2,1)S(1)}, u32[]{:S(2)}, u32[]{:S(2)}) collective-permute-start(bf16[8,5120]{1,0:T(8,128)(2,1)S(1)} %get-tuple-element.27), channel_id=1, source_target_pairs={{0,1},{1,0},{2,3},{3,2},{4,5},{5,4},{6,7},{7,6},{8,9},{9,8},{10,11... | collective-permute-start | bytes 245768 | tf_op jit(solution)/shard_map/cond/branch_1_fun/ppermute | solution.py:356
  26.7 9.8 %collective-permute-start = (bf16[24,5120]{1,0:T(8,128)(2,1)S(1)}, bf16[24,5120]{1,0:T(8,128)(2,1)S(1)}, u32[]{:S(2)}, u32[]{:S(2)}) collective-permute-start(bf16[24,5120]{1,0:T(8,128)(2,1)S(1)} %get-tuple-element.26), channel_id=1, source_target_pairs={{0,1},{1,0},{2,3},{3,2},{4,5},{5,4},{6,7},{7,6},{8,9},{9,8},{10,11... | collective-permute-start | bytes 737288 | tf_op jit(solution)/shard_map/cond/branch_1_fun/ppermute | solution.py:356
  29.7 6.7 %collective-permute-start.3 = (bf16[8,5120]{1,0:T(8,128)(2,1)S(1)}, bf16[8,5120]{1,0:T(8,128)(2,1)S(1)}, u32[]{:S(2)}, u32[]{:S(2)}) collective-permute-start(bf16[8,5120]{1,0:T(8,128)(2,1)S(1)} %add_convert_fusion), channel_id=1, source_target_pairs={{0,2},{1,3},{2,0},{3,1},{4,6},{5,7},{6,4},{7,5},{8,10},{9,11},{10,... | collective-permute-start | bytes 245768 | tf_op jit(solution)/shard_map/cond/branch_1_fun/ppermute | solution.py:356
  36.5 7.7 %collective-permute-start.1 = (bf16[8,5120]{1,0:T(8,128)(2,1)S(1)}, bf16[8,5120]{1,0:T(8,128)(2,1)S(1)}, u32[]{:S(2)}, u32[]{:S(2)}) collective-permute-start(bf16[8,5120]{1,0:T(8,128)(2,1)S(1)} %get-tuple-element.74), channel_id=1, source_target_pairs={{0,2},{1,3},{2,0},{3,1},{4,6},{5,7},{6,4},{7,5},{8,10},{9,11},{10,... | collective-permute-start | bytes 245768 | tf_op jit(solution)/shard_map/cond/branch_1_fun/ppermute | solution.py:356
  39.3 7.4 %collective-permute-start.4 = (bf16[8,5120]{1,0:T(8,128)(2,1)S(1)}, bf16[8,5120]{1,0:T(8,128)(2,1)S(1)}, u32[]{:S(2)}, u32[]{:S(2)}) collective-permute-start(bf16[8,5120]{1,0:T(8,128)(2,1)S(1)} %get-tuple-element.75), channel_id=1, source_target_pairs={{0,7},{1,6},{2,5},{3,4},{4,3},{5,2},{6,1},{7,0},{8,15},{9,14},{10,... | collective-permute-start | bytes 245768 | tf_op jit(solution)/shard_map/cond/branch_1_fun/ppermute | solution.py:356
  46.8 16.5 %copy-start.1 = (bf16[16,480,128]{2,1,0:T(8,128)(2,1)}, bf16[16,480,128]{2,1,0:T(8,128)(2,1)S(1)}, u32[]{:S(2)}) copy-start(bf16[16,480,128]{2,1,0:T(8,128)(2,1)S(1)} %all-to-all-done.1.refs_0_) | copy-start | bytes 5898244
  46.9 36.9 %copy-start.2 = (bf16[16,256,128]{2,1,0:T(8,128)(2,1)}, bf16[16,256,128]{2,1,0:T(8,128)(2,1)S(1)}, u32[]{:S(2)}) copy-start(bf16[16,256,128]{2,1,0:T(8,128)(2,1)S(1)} %slice.31.refs_0_) | copy-start | bytes 3145732
  46.9 36.9 %collective-permute-start.12 = (bf16[16,256,128]{2,1,0:T(8,128)(2,1)S(1)}, bf16[16,256,128]{2,1,0:T(8,128)(2,1)}, u32[]{:S(2)}, u32[]{:S(2)}) collective-permute-start(bf16[16,256,128]{2,1,0:T(8,128)(2,1)S(1)} %slice.31.refs_0_), channel_id=1, source_target_pairs={{0,1},{1,0},{2,3},{3,2},{4,5},{5,4},{6,7},{7,6},{8,9},{9,8},{10,11... | collective-permute-start | bytes 3145736 | tf_op jit(solution)/shard_map/ppermute | solution.py:356
  49.8 5.5 %collective-permute-start.5 = (bf16[4,5120]{1,0:T(4,128)(2,1)S(1)}, bf16[4,5120]{1,0:T(4,128)(2,1)S(1)}, u32[]{:S(2)}, u32[]{:S(2)}) collective-permute-start(bf16[4,5120]{1,0:T(4,128)(2,1)S(1)} %get-tuple-element.29), channel_id=1, source_target_pairs={{0,8},{1,9},{2,10},{3,11},{4,12},{5,13},{6,14},{7,15},{8,0},{9,1},... | collective-permute-start | bytes 122888 | tf_op jit(solution)/shard_map/cond/branch_1_fun/ppermute | solution.py:356
  55.3 5.9 %collective-permute-start.6 = (bf16[4,5120]{1,0:T(4,128)(2,1)S(1)}, bf16[4,5120]{1,0:T(4,128)(2,1)S(1)}, u32[]{:S(2)}, u32[]{:S(2)}) collective-permute-start(bf16[4,5120]{1,0:T(4,128)(2,1)S(1)} %add_convert_fusion.1), channel_id=1, source_target_pairs={{0,0},{1,17},{2,34},{3,51},{4,116},{5,101},{6,86},{7,71},{8,136},{... | collective-permute-start | bytes 122888 | tf_op jit(solution)/shard_map/cond/branch_1_fun/ppermute | solution.py:360
  57.6 5.6 %collective-permute-start.7 = (bf16[4,5120]{1,0:T(4,128)(2,1)S(1)}, bf16[4,5120]{1,0:T(4,128)(2,1)S(1)}, u32[]{:S(2)}, u32[]{:S(2)}) collective-permute-start(bf16[4,5120]{1,0:T(4,128)(2,1)S(1)} %add_convert_fusion.1), channel_id=1, source_target_pairs={{0,8},{1,25},{2,42},{3,59},{4,124},{5,109},{6,94},{7,79},{8,128},{... | collective-permute-start | bytes 122888 | tf_op jit(solution)/shard_map/cond/branch_1_fun/ppermute | solution.py:360
  63.2 25.0 %all-to-all-start.2 = ((bf16[16,288,128]{2,1,0:T(8,128)(2,1)}), bf16[16,288,128]{2,1,0:T(8,128)(2,1)}, u32[]{:S(2)}, u32[]{:S(2)}) async-start(bf16[16,288,128]{2,1,0:T(8,128)(2,1)} %get-tuple-element.62), calls=%async_computation.2 | async-start | bytes 2359296 | tf_op jit(solution)/shard_map/all_to_all | solution.py:431
  69.2 10.7 %collective-permute-start.8 = (bf16[8,5120]{1,0:T(8,128)(2,1)S(1)}, bf16[8,5120]{1,0:T(8,128)(2,1)S(1)}, u32[]{:S(2)}, u32[]{:S(2)}) collective-permute-start(bf16[8,5120]{1,0:T(8,128)(2,1)S(1)} %get-tuple-element.80.refs_0_), channel_id=1, source_target_pairs={{0,7},{1,6},{2,5},{3,4},{4,3},{5,2},{6,1},{7,0},{8,15},{9,14},{10,... | collective-permute-start | bytes 245768 | tf_op jit(solution)/shard_map/ppermute | solution.py:356
  76.6 6.2 %collective-permute-start.9 = (bf16[8,5120]{1,0:T(8,128)(2,1)S(1)}, bf16[8,5120]{1,0:T(8,128)(2,1)S(1)}, u32[]{:S(2)}, u32[]{:S(2)}) collective-permute-start(bf16[8,5120]{1,0:T(8,128)(2,1)S(1)} %get-tuple-element.80.refs_0_), channel_id=1, source_target_pairs={{0,2},{1,3},{2,0},{3,1},{4,6},{5,7},{6,4},{7,5},{8,10},{9,11},{10,... | collective-permute-start | bytes 245768 | tf_op jit(solution)/shard_map/ppermute | solution.py:356
  77.5 9.4 %collective-permute-start.11 = (bf16[8,5120]{1,0:T(8,128)(2,1)S(1)}, bf16[8,5120]{1,0:T(8,128)(2,1)S(1)}, u32[]{:S(2)}, u32[]{:S(2)}) collective-permute-start(bf16[8,5120]{1,0:T(8,128)(2,1)S(1)} %get-tuple-element.80.refs_0_), channel_id=1, source_target_pairs={{0,1},{1,0},{2,3},{3,2},{4,5},{5,4},{6,7},{7,6},{8,9},{9,8},{10,11... | collective-permute-start | bytes 245768 | tf_op jit(solution)/shard_map/ppermute | solution.py:356
  79.9 7.1 %collective-permute-start.10 = (bf16[8,5120]{1,0:T(8,128)(2,1)S(1)}, bf16[8,5120]{1,0:T(8,128)(2,1)S(1)}, u32[]{:S(2)}, u32[]{:S(2)}) collective-permute-start(bf16[8,5120]{1,0:T(8,128)(2,1)S(1)} %collective-permute-done.8.refs_1_), channel_id=1, source_target_pairs={{0,2},{1,3},{2,0},{3,1},{4,6},{5,7},{6,4},{7,5},{8,10},{9,11},{10,... | collective-permute-start | bytes 245768 | tf_op jit(solution)/shard_map/ppermute | solution.py:356
  82.9 5.3 %copy-start.3 = (bf16[5120]{0:T(1024)(128)(2,1)S(1)}, bf16[5120]{0:T(1024)(128)(2,1)}, u32[]{:S(2)}) copy-start(bf16[5120]{0:T(1024)(128)(2,1)} %param.25) | copy-start | bytes 30724
  82.9 8.5 %collective-permute-start.13 = (bf16[16,5120]{1,0:T(8,128)(2,1)S(1)}, bf16[16,5120]{1,0:T(8,128)(2,1)S(1)}, u32[]{:S(2)}, u32[]{:S(2)}) collective-permute-start(bf16[16,5120]{1,0:T(8,128)(2,1)S(1)} %pad_maximum_fusion.1), channel_id=1, source_target_pairs={{0,1},{1,0},{2,3},{3,2},{4,5},{5,4},{6,7},{7,6},{8,9},{9,8},{10,11... | collective-permute-start | bytes 491528 | tf_op jit(solution)/shard_map/ppermute | solution.py:356
  87.0 4.5 %collective-permute-start.14 = (bf16[8,5120]{1,0:T(8,128)(2,1)S(1)}, bf16[8,5120]{1,0:T(8,128)(2,1)S(1)}, u32[]{:S(2)}, u32[]{:S(2)}) collective-permute-start(bf16[8,5120]{1,0:T(8,128)(2,1)S(1)} %collective-permute-done.10.refs_3_), channel_id=1, source_target_pairs={{0,1},{1,0},{2,3},{3,2},{4,5},{5,4},{6,7},{7,6},{8,9},{9,8},{10,11... | collective-permute-start | bytes 245768 | tf_op jit(solution)/shard_map/ppermute | solution.py:356
  88.2 3.2 %copy-start = (bf16[4,16,5120]{2,1,0:T(8,128)(2,1)S(1)}, bf16[4,16,5120]{2,1,0:T(8,128)(2,1)}, u32[]{:S(2)}) copy-start(bf16[4,16,5120]{2,1,0:T(8,128)(2,1)} %param.23) | copy-start | bytes 1966084

commit v6 on v5

--- a/solution.py
+++ b/solution.py
@@ -389,7 +389,7 @@
     msg = lax.all_to_all(msg, "group", split_axis=0, concat_axis=0, tiled=True)
     old_keys, old_values = key_cache[:, 0], value_cache[:, 0]
     length = old_keys.shape[1]
-    part, share = 224, length // 2
+    part, share = 208, length // 2
     large, small, table = order_cache(
         dest_table, cache_len, remaining, old_keys, old_values, part
     )

time: 94.2 us -> 116 us (1.23)
  starting transfers between devices: 50.1 us -> 75.3 us
  waiting for transfers between devices: 21.4 us -> 18.5 us
    ppermute x13, starting transfers between devices: 30.3 us -> 55.5 us  [swap(): lax.ppermute(x, 'tensor', [(t, fold(fold(t) ^ mask)) for t in range(16)])]
    ppermute x13, waiting for transfers between devices: 15.9 us -> 13 us  [swap(): lax.ppermute(x, 'tensor', [(t, fold(fold(t) ^ mask)) for t in range(16)])]
  transfers between devices with their start and end apart: 18 -> 18, of which waited for: 10 -> 6; matrix products, arithmetic and copies ran while one was open for 0% -> 0% of each run, Pallas kernels for 18% -> 15%
where the time goes in v6:
time: 116 us
  starting transfers between devices  75.3 us (65%)
  Pallas kernels  20.7 us (18%)
  waiting for transfers between devices  18.5 us (16%)
    ppermute x13, starting transfers between devices, swap(): lax.ppermute(x, 'tensor', [(t, fold(fold(t) ^ mask)) for t in range(16)])  55.5 us
    ppermute x13, waiting for transfers between devices, swap(): lax.ppermute(x, 'tensor', [(t, fold(fold(t) ^ mask)) for t in range(16)])  13 us
    pallas_call x2, Pallas kernels, place(): pl.pallas_call(functools.partial(place_kernel, tuple((bases for _, _, _,...  6.21 us
    all_to_all x1, starting transfers between devices, on_device(): msg = lax.all_to_all(msg, 'group', split_axis=0, concat_axis=0, tiled=True)  5.78 us
    all_to_all x1, starting transfers between devices, on_device(): lax.all_to_all(large, 'group', split_axis=0, concat_axis=0, tiled=True)  5.73 us
    all_to_all x1, starting transfers between devices, on_device(): lax.all_to_all(small, 'group', split_axis=0, concat_axis=0, tiled=True)  5.67 us
    ppermute x2, waiting for transfers between devices, hand_over(): lax.ppermute(x, ('group', 'tensor'), [(g * 16 + t, (g ^ fold(t)) * 16 + f...  5.49 us
    pallas_call x1, Pallas kernels, attend(): pl.pallas_call(attend_kernel, out_shape=(jax.ShapeDtypeStruct((2 * n, out...  5.45 us
  transfers between devices with their start and end apart: 18, of which 6 were waited for; matrix products, arithmetic and copies ran while one was open for 0% of the time, Pallas kernels for 15%

profile of v6, /device:TPU:24, one launch (start us, length us, event | category | flops | bytes accessed | tf_op | source)
XLA Modules:
  0.0 115.8 jit_solution(11420572045062748030)
XLA Ops:
  0.6 1.7 %ask.1 = bf16[16,32,128]{2,1,0:T(8,128)(2,1)} custom-call(bf16[4,16,4,128]{3,2,1,0:T(4,128)(2,1)} %queries.1, bf16[4,16,128]{2,1,0:T(8,128)(2,1)} %bitcast.21, bf16[4,16,128]{2,1,0:T(8,128)(2,1)} %bitcast.23), custom_call_target="tpu_custom_call" | custom-call | bytes 400000 | tf_op jit(solution)/shard_map/ask/pallas_call | solution.py:35
  2.3 5.8 %all-to-all-start = ((bf16[16,32,128]{2,1,0:T(8,128)(2,1)}), bf16[16,32,128]{2,1,0:T(8,128)(2,1)S(1)}, u32[]{:S(2)}, u32[]{:S(2)}) async-start(bf16[16,32,128]{2,1,0:T(8,128)(2,1)} %ask.1), calls=%async_computation | async-start | bytes 262144 | tf_op jit(solution)/shard_map/all_to_all | solution.py:389
  8.1 5.3 %order_cache.1 = (bf16[16,464,128]{2,1,0:T(8,128)(2,1)}, bf16[16,304,128]{2,1,0:T(8,128)(2,1)}, s32[6,16]{1,0:T(8,128)S(1)}) custom-call(s32[256]{0:T(256)} %dest.1, s32[256]{0:T(256)} %lens.1, s32[256]{0:T(256)} %rest.1, bf16[16,512,128]{2,1,0:T(8,128)(2,1)} %bitcast.15, bf16[16,512,128]{2,1,0:T(8,128)(2,1)} %bitcast.17), custom_call_target="tpu_custom_call" | custom-call | bytes 8388608 | tf_op jit(solution)/shard_map/order_cache/pallas_call | solution.py:116
  13.4 5.7 %all-to-all-start.1 = ((bf16[16,464,128]{2,1,0:T(8,128)(2,1)}), bf16[16,464,128]{2,1,0:T(8,128)(2,1)S(1)}, u32[]{:S(2)}, u32[]{:S(2)}) async-start(bf16[16,464,128]{2,1,0:T(8,128)(2,1)} %get-tuple-element.54), calls=%async_computation.1 | async-start | bytes 3801088 | tf_op jit(solution)/shard_map/all_to_all | solution.py:396
  19.2 27.6 %conditional.2 = (f32[4,5120]{1,0:T(4,128)S(1)}, bf16[4,5120]{1,0:T(4,128)(2,1)S(1)}) conditional(s32[]{:T(128)} %convert_element_type.35, () %tuple.27, (s32[]{:T(128)}, s32[6,16]{1,0:T(8,128)S(1)}, bf16[16,32,128]{2,1,0:T(8,128)(2,1)S(1)}, bf16[16,512,128]{2,1,0:T(8,128)(2,1)}, bf16[16,512,128]{2,1,0:T(8,128)(2,1)}, ...), branch_computations={%region_0.0_spmd, %region_1.0_spmd} | conditional | flops 403349504 | bytes 14598360 | solution.py:411
  19.2 5.4 %attend.1 = (f32[32,5120]{1,0:T(8,128)S(1)}, bf16[24,5120]{1,0:T(8,128)(2,1)S(1)}, bf16[8,5120]{1,0:T(8,128)(2,1)S(1)}) custom-call(s32[1]{0:T(128)} %bitcast.turn, s32[6,16]{1,0:T(8,128)S(1)} %get-tuple-element.20.table, bf16[16,32,128]{2,1,0:T(8,128)(2,1)S(1)} %get-tuple-element.21.msg, bf16[16,512,128]{2,1,0:T(8,128)(2,1)} %get-tuple-element.22.keys, ...), custom_call_target="tpu_custom_call" | custom-call | flops 402653184 | bytes 9437184 | tf_op jit(solution)/shard_map/cond/branch_1_fun/attend/pallas_call | solution.py:219
  24.6 2.0 %collective-permute-start.2 = (bf16[8,5120]{1,0:T(8,128)(2,1)S(1)}, bf16[8,5120]{1,0:T(8,128)(2,1)S(1)}, u32[]{:S(2)}, u32[]{:S(2)}) collective-permute-start(bf16[8,5120]{1,0:T(8,128)(2,1)S(1)} %get-tuple-element.27), channel_id=1, source_target_pairs={{0,1},{1,0},{2,3},{3,2},{4,5},{5,4},{6,7},{7,6},{8,9},{9,8},{10,11... | collective-permute-start | bytes 245768 | tf_op jit(solution)/shard_map/cond/branch_1_fun/ppermute | solution.py:356
  26.6 0.1 collective-permute-start
  26.8 3.0 %collective-permute-done.2 = bf16[8,5120]{1,0:T(8,128)(2,1)S(1)} collective-permute-done((bf16[8,5120]{1,0:T(8,128)(2,1)S(1)}, bf16[8,5120]{1,0:T(8,128)(2,1)S(1)}, u32[]{:S(2)}, u32[]{:S(2)}) %collective-permute-start.2) | collective-permute-done | bytes 81952 | tf_op jit(solution)/shard_map/cond/branch_1_fun/ppermute | solution.py:356
  29.7 3.4 %collective-permute-start.3 = (bf16[8,5120]{1,0:T(8,128)(2,1)S(1)}, bf16[8,5120]{1,0:T(8,128)(2,1)S(1)}, u32[]{:S(2)}, u32[]{:S(2)}) collective-permute-start(bf16[8,5120]{1,0:T(8,128)(2,1)S(1)} %add_convert_fusion), channel_id=1, source_target_pairs={{0,2},{1,3},{2,0},{3,1},{4,6},{5,7},{6,4},{7,5},{8,10},{9,11},{10,... | collective-permute-start | bytes 245768 | tf_op jit(solution)/shard_map/cond/branch_1_fun/ppermute | solution.py:356
  33.1 3.3 %collective-permute-done = bf16[24,5120]{1,0:T(8,128)(2,1)S(1)} collective-permute-done((bf16[24,5120]{1,0:T(8,128)(2,1)S(1)}, bf16[24,5120]{1,0:T(8,128)(2,1)S(1)}, u32[]{:S(2)}, u32[]{:S(2)}) %collective-permute-start) | collective-permute-done | bytes 245792 | tf_op jit(solution)/shard_map/cond/branch_1_fun/ppermute | solution.py:356
  36.5 2.8 %collective-permute-start.1 = (bf16[8,5120]{1,0:T(8,128)(2,1)S(1)}, bf16[8,5120]{1,0:T(8,128)(2,1)S(1)}, u32[]{:S(2)}, u32[]{:S(2)}) collective-permute-start(bf16[8,5120]{1,0:T(8,128)(2,1)S(1)} %get-tuple-element.74), channel_id=1, source_target_pairs={{0,2},{1,3},{2,0},{3,1},{4,6},{5,7},{6,4},{7,5},{8,10},{9,11},{10,... | collective-permute-start | bytes 245768 | tf_op jit(solution)/shard_map/cond/branch_1_fun/ppermute | solution.py:356
  39.3 4.9 %collective-permute-start.4 = (bf16[8,5120]{1,0:T(8,128)(2,1)S(1)}, bf16[8,5120]{1,0:T(8,128)(2,1)S(1)}, u32[]{:S(2)}, u32[]{:S(2)}) collective-permute-start(bf16[8,5120]{1,0:T(8,128)(2,1)S(1)} %get-tuple-element.75), channel_id=1, source_target_pairs={{0,7},{1,6},{2,5},{3,4},{4,3},{5,2},{6,1},{7,0},{8,15},{9,14},{10,... | collective-permute-start | bytes 245768 | tf_op jit(solution)/shard_map/cond/branch_1_fun/ppermute | solution.py:356
  44.2 2.4 %collective-permute-done.4 = bf16[8,5120]{1,0:T(8,128)(2,1)S(1)} collective-permute-done((bf16[8,5120]{1,0:T(8,128)(2,1)S(1)}, bf16[8,5120]{1,0:T(8,128)(2,1)S(1)}, u32[]{:S(2)}, u32[]{:S(2)}) %collective-permute-start.4) | collective-permute-done | bytes 81952 | tf_op jit(solution)/shard_map/cond/branch_1_fun/ppermute | solution.py:356
  46.8 13.8 %conditional.3 = (bf16[8,5120]{1,0:T(8,128)(2,1)S(1)}) conditional(s32[]{:T(128)} %convert_element_type.35, () %tuple.26, (bf16[4,5120]{1,0:T(4,128)(2,1)S(1)}, f32[4,5120]{1,0:T(4,128)S(1)}) %tuple.30), branch_computations={%region_2.0_spmd, %region_3.0_spmd} | conditional | flops 225280 | bytes 819328 | solution.py:420
  46.8 1.3 %collective-permute-start.5 = (bf16[4,5120]{1,0:T(4,128)(2,1)S(1)}, bf16[4,5120]{1,0:T(4,128)(2,1)S(1)}, u32[]{:S(2)}, u32[]{:S(2)}) collective-permute-start(bf16[4,5120]{1,0:T(4,128)(2,1)S(1)} %get-tuple-element.29), channel_id=1, source_target_pairs={{0,8},{1,9},{2,10},{3,11},{4,12},{5,13},{6,14},{7,15},{8,0},{9,1},... | collective-permute-start | bytes 122888 | tf_op jit(solution)/shard_map/cond/branch_1_fun/ppermute | solution.py:356
  48.1 4.3 %collective-permute-done.5 = bf16[4,5120]{1,0:T(4,128)(2,1)S(1)} collective-permute-done((bf16[4,5120]{1,0:T(4,128)(2,1)S(1)}, bf16[4,5120]{1,0:T(4,128)(2,1)S(1)}, u32[]{:S(2)}, u32[]{:S(2)}) %collective-permute-start.5) | collective-permute-done | bytes 40992 | tf_op jit(solution)/shard_map/cond/branch_1_fun/ppermute | solution.py:356
  52.4 2.5 %collective-permute-start.6 = (bf16[4,5120]{1,0:T(4,128)(2,1)S(1)}, bf16[4,5120]{1,0:T(4,128)(2,1)S(1)}, u32[]{:S(2)}, u32[]{:S(2)}) collective-permute-start(bf16[4,5120]{1,0:T(4,128)(2,1)S(1)} %add_convert_fusion.1), channel_id=1, source_target_pairs={{0,0},{1,17},{2,34},{3,51},{4,116},{5,101},{6,86},{7,71},{8,136},{... | collective-permute-start | bytes 122888 | tf_op jit(solution)/shard_map/cond/branch_1_fun/ppermute | solution.py:360
  55.0 3.3 %collective-permute-done.6 = bf16[4,5120]{1,0:T(4,128)(2,1)S(1)} collective-permute-done((bf16[4,5120]{1,0:T(4,128)(2,1)S(1)}, bf16[4,5120]{1,0:T(4,128)(2,1)S(1)}, u32[]{:S(2)}, u32[]{:S(2)}) %collective-permute-start.6) | collective-permute-done | bytes 40992 | tf_op jit(solution)/shard_map/cond/branch_1_fun/ppermute | solution.py:360
  58.3 2.2 %collective-permute-done.7 = bf16[4,5120]{1,0:T(4,128)(2,1)S(1)} collective-permute-done((bf16[4,5120]{1,0:T(4,128)(2,1)S(1)}, bf16[4,5120]{1,0:T(4,128)(2,1)S(1)}, u32[]{:S(2)}, u32[]{:S(2)}) %collective-permute-start.7) | collective-permute-done | bytes 40992 | tf_op jit(solution)/shard_map/cond/branch_1_fun/ppermute | solution.py:360
  60.6 5.7 %all-to-all-start.2 = ((bf16[16,304,128]{2,1,0:T(8,128)(2,1)}), bf16[16,304,128]{2,1,0:T(8,128)(2,1)}, u32[]{:S(2)}, u32[]{:S(2)}) async-start(bf16[16,304,128]{2,1,0:T(8,128)(2,1)} %get-tuple-element.62), calls=%async_computation.2 | async-start | bytes 2490368 | tf_op jit(solution)/shard_map/all_to_all | solution.py:431
  66.3 0.1 slice.31.refs_0_
  66.4 2.0 %collective-permute-start.12 = (bf16[16,256,128]{2,1,0:T(8,128)(2,1)S(1)}, bf16[16,256,128]{2,1,0:T(8,128)(2,1)}, u32[]{:S(2)}, u32[]{:S(2)}) collective-permute-start(bf16[16,256,128]{2,1,0:T(8,128)(2,1)S(1)} %slice.31.refs_0_), channel_id=1, source_target_pairs={{0,1},{1,0},{2,3},{3,2},{4,5},{5,4},{6,7},{7,6},{8,9},{9,8},{10,11... | collective-permute-start | bytes 3145736 | tf_op jit(solution)/shard_map/ppermute | solution.py:356
  68.4 6.1 %collective-permute-start.8 = (bf16[8,5120]{1,0:T(8,128)(2,1)S(1)}, bf16[8,5120]{1,0:T(8,128)(2,1)S(1)}, u32[]{:S(2)}, u32[]{:S(2)}) collective-permute-start(bf16[8,5120]{1,0:T(8,128)(2,1)S(1)} %get-tuple-element.80.refs_0_), channel_id=1, source_target_pairs={{0,7},{1,6},{2,5},{3,4},{4,3},{5,2},{6,1},{7,0},{8,15},{9,14},{10,... | collective-permute-start | bytes 245768 | tf_op jit(solution)/shard_map/ppermute | solution.py:356
  74.5 3.1 %collective-permute-start.9 = (bf16[8,5120]{1,0:T(8,128)(2,1)S(1)}, bf16[8,5120]{1,0:T(8,128)(2,1)S(1)}, u32[]{:S(2)}, u32[]{:S(2)}) collective-permute-start(bf16[8,5120]{1,0:T(8,128)(2,1)S(1)} %get-tuple-element.80.refs_0_), channel_id=1, source_target_pairs={{0,2},{1,3},{2,0},{3,1},{4,6},{5,7},{6,4},{7,5},{8,10},{9,11},{10,... | collective-permute-start | bytes 245768 | tf_op jit(solution)/shard_map/ppermute | solution.py:356
  77.6 1.0 collective-permute-start.11
  78.6 26.6 %collective-permute-start.10 = (bf16[8,5120]{1,0:T(8,128)(2,1)S(1)}, bf16[8,5120]{1,0:T(8,128)(2,1)S(1)}, u32[]{:S(2)}, u32[]{:S(2)}) collective-permute-start(bf16[8,5120]{1,0:T(8,128)(2,1)S(1)} %collective-permute-done.8.refs_1_), channel_id=1, source_target_pairs={{0,2},{1,3},{2,0},{3,1},{4,6},{5,7},{6,4},{7,5},{8,10},{9,11},{10,... | collective-permute-start | bytes 245768 | tf_op jit(solution)/shard_map/ppermute | solution.py:356
  105.2 0.1 collective-permute-start.13
  105.3 3.1 %place.2 = bf16[16,512,128]{2,1,0:T(8,128)(2,1)} custom-call(s32[6,16]{1,0:T(8,128)S(1)} %get-tuple-element.51.table, bf16[4,16,128]{2,1,0:T(8,128)(2,1)} %bitcast.22, bf16[16,256,128]{2,1,0:T(8,128)(2,1)} %copy-done.2, bf16[16,256,128]{2,1,0:T(8,128)(2,1)} %collective-permute-done.12.refs_1_), custom_call_target="tpu_custom_call" | custom-call | bytes 4194304 | tf_op jit(solution)/shard_map/place/pallas_call | solution.py:288
  108.5 2.1 %collective-permute-start.14 = (bf16[8,5120]{1,0:T(8,128)(2,1)S(1)}, bf16[8,5120]{1,0:T(8,128)(2,1)S(1)}, u32[]{:S(2)}, u32[]{:S(2)}) collective-permute-start(bf16[8,5120]{1,0:T(8,128)(2,1)S(1)} %collective-permute-done.10.refs_3_), channel_id=1, source_target_pairs={{0,1},{1,0},{2,3},{3,2},{4,5},{5,4},{6,7},{7,6},{8,9},{9,8},{10,11... | collective-permute-start | bytes 245768 | tf_op jit(solution)/shard_map/ppermute | solution.py:356
  110.6 3.1 %place.3 = bf16[16,512,128]{2,1,0:T(8,128)(2,1)} custom-call(s32[6,16]{1,0:T(8,128)S(1)} %get-tuple-element.51.table, bf16[4,16,128]{2,1,0:T(8,128)(2,1)} %bitcast.24, bf16[16,464,128]{2,1,0:T(8,128)(2,1)} %copy-done.1, bf16[16,304,128]{2,1,0:T(8,128)(2,1)} %all-to-all-done.2.refs_1_), custom_call_target="tpu_custom_call" | custom-call | bytes 4194304 | tf_op jit(solution)/shard_map/place/pallas_call | solution.py:288
  113.7 2.1 %finish.1 = (bf16[64,5120]{1,0:T(8,128)(2,1)}, bf16[64,5120]{1,0:T(8,128)(2,1)}) custom-call(s32[6,16]{1,0:T(8,128)S(1)} %get-tuple-element.51.table, bf16[8,5120]{1,0:T(8,128)(2,1)S(1)} %get-tuple-element.80.refs_0_, bf16[8,5120]{1,0:T(8,128)(2,1)S(1)} %collective-permute-done.8.refs_1_, bf16[8,5120]{1,0:T(8,128)(2,1)S(1)} %collective-permute-done.9.refs_2_, ...), custom_call_target="tpu_custom_call" | custom-call | flops 41943040 | bytes 2621440 | tf_op jit(solution)/shard_map/finish/pallas_call | solution.py:341
  (31 shorter events, 0.4 us)
Async XLA Ops:
  2.3 11.1 %all-to-all-start = ((bf16[16,32,128]{2,1,0:T(8,128)(2,1)}), bf16[16,32,128]{2,1,0:T(8,128)(2,1)S(1)}, u32[]{:S(2)}, u32[]{:S(2)}) async-start(bf16[16,32,128]{2,1,0:T(8,128)(2,1)} %ask.1), calls=%async_computation | async-start | bytes 262144 | tf_op jit(solution)/shard_map/all_to_all | solution.py:389
  13.4 33.3 %all-to-all-start.1 = ((bf16[16,464,128]{2,1,0:T(8,128)(2,1)}), bf16[16,464,128]{2,1,0:T(8,128)(2,1)S(1)}, u32[]{:S(2)}, u32[]{:S(2)}) async-start(bf16[16,464,128]{2,1,0:T(8,128)(2,1)} %get-tuple-element.54), calls=%async_computation.1 | async-start | bytes 3801088 | tf_op jit(solution)/shard_map/all_to_all | solution.py:396
  24.6 5.1 %collective-permute-start.2 = (bf16[8,5120]{1,0:T(8,128)(2,1)S(1)}, bf16[8,5120]{1,0:T(8,128)(2,1)S(1)}, u32[]{:S(2)}, u32[]{:S(2)}) collective-permute-start(bf16[8,5120]{1,0:T(8,128)(2,1)S(1)} %get-tuple-element.27), channel_id=1, source_target_pairs={{0,1},{1,0},{2,3},{3,2},{4,5},{5,4},{6,7},{7,6},{8,9},{9,8},{10,11... | collective-permute-start | bytes 245768 | tf_op jit(solution)/shard_map/cond/branch_1_fun/ppermute | solution.py:356
  26.6 9.8 %collective-permute-start = (bf16[24,5120]{1,0:T(8,128)(2,1)S(1)}, bf16[24,5120]{1,0:T(8,128)(2,1)S(1)}, u32[]{:S(2)}, u32[]{:S(2)}) collective-permute-start(bf16[24,5120]{1,0:T(8,128)(2,1)S(1)} %get-tuple-element.26), channel_id=1, source_target_pairs={{0,1},{1,0},{2,3},{3,2},{4,5},{5,4},{6,7},{7,6},{8,9},{9,8},{10,11... | collective-permute-start | bytes 737288 | tf_op jit(solution)/shard_map/cond/branch_1_fun/ppermute | solution.py:356
  29.7 6.7 %collective-permute-start.3 = (bf16[8,5120]{1,0:T(8,128)(2,1)S(1)}, bf16[8,5120]{1,0:T(8,128)(2,1)S(1)}, u32[]{:S(2)}, u32[]{:S(2)}) collective-permute-start(bf16[8,5120]{1,0:T(8,128)(2,1)S(1)} %add_convert_fusion), channel_id=1, source_target_pairs={{0,2},{1,3},{2,0},{3,1},{4,6},{5,7},{6,4},{7,5},{8,10},{9,11},{10,... | collective-permute-start | bytes 245768 | tf_op jit(solution)/shard_map/cond/branch_1_fun/ppermute | solution.py:356
  36.5 7.7 %collective-permute-start.1 = (bf16[8,5120]{1,0:T(8,128)(2,1)S(1)}, bf16[8,5120]{1,0:T(8,128)(2,1)S(1)}, u32[]{:S(2)}, u32[]{:S(2)}) collective-permute-start(bf16[8,5120]{1,0:T(8,128)(2,1)S(1)} %get-tuple-element.74), channel_id=1, source_target_pairs={{0,2},{1,3},{2,0},{3,1},{4,6},{5,7},{6,4},{7,5},{8,10},{9,11},{10,... | collective-permute-start | bytes 245768 | tf_op jit(solution)/shard_map/cond/branch_1_fun/ppermute | solution.py:356
  39.3 7.4 %collective-permute-start.4 = (bf16[8,5120]{1,0:T(8,128)(2,1)S(1)}, bf16[8,5120]{1,0:T(8,128)(2,1)S(1)}, u32[]{:S(2)}, u32[]{:S(2)}) collective-permute-start(bf16[8,5120]{1,0:T(8,128)(2,1)S(1)} %get-tuple-element.75), channel_id=1, source_target_pairs={{0,7},{1,6},{2,5},{3,4},{4,3},{5,2},{6,1},{7,0},{8,15},{9,14},{10,... | collective-permute-start | bytes 245768 | tf_op jit(solution)/shard_map/cond/branch_1_fun/ppermute | solution.py:356
  46.8 19.6 %copy-start.1 = (bf16[16,464,128]{2,1,0:T(8,128)(2,1)}, bf16[16,464,128]{2,1,0:T(8,128)(2,1)S(1)}, u32[]{:S(2)}) copy-start(bf16[16,464,128]{2,1,0:T(8,128)(2,1)S(1)} %all-to-all-done.1.refs_0_) | copy-start | bytes 5701636
  46.8 5.6 %collective-permute-start.5 = (bf16[4,5120]{1,0:T(4,128)(2,1)S(1)}, bf16[4,5120]{1,0:T(4,128)(2,1)S(1)}, u32[]{:S(2)}, u32[]{:S(2)}) collective-permute-start(bf16[4,5120]{1,0:T(4,128)(2,1)S(1)} %get-tuple-element.29), channel_id=1, source_target_pairs={{0,8},{1,9},{2,10},{3,11},{4,12},{5,13},{6,14},{7,15},{8,0},{9,1},... | collective-permute-start | bytes 122888 | tf_op jit(solution)/shard_map/cond/branch_1_fun/ppermute | solution.py:356
  52.4 5.9 %collective-permute-start.6 = (bf16[4,5120]{1,0:T(4,128)(2,1)S(1)}, bf16[4,5120]{1,0:T(4,128)(2,1)S(1)}, u32[]{:S(2)}, u32[]{:S(2)}) collective-permute-start(bf16[4,5120]{1,0:T(4,128)(2,1)S(1)} %add_convert_fusion.1), channel_id=1, source_target_pairs={{0,0},{1,17},{2,34},{3,51},{4,116},{5,101},{6,86},{7,71},{8,136},{... | collective-permute-start | bytes 122888 | tf_op jit(solution)/shard_map/cond/branch_1_fun/ppermute | solution.py:360
  55.0 5.6 %collective-permute-start.7 = (bf16[4,5120]{1,0:T(4,128)(2,1)S(1)}, bf16[4,5120]{1,0:T(4,128)(2,1)S(1)}, u32[]{:S(2)}, u32[]{:S(2)}) collective-permute-start(bf16[4,5120]{1,0:T(4,128)(2,1)S(1)} %add_convert_fusion.1), channel_id=1, source_target_pairs={{0,8},{1,25},{2,42},{3,59},{4,124},{5,109},{6,94},{7,79},{8,128},{... | collective-permute-start | bytes 122888 | tf_op jit(solution)/shard_map/cond/branch_1_fun/ppermute | solution.py:360
  60.6 50.0 %all-to-all-start.2 = ((bf16[16,304,128]{2,1,0:T(8,128)(2,1)}), bf16[16,304,128]{2,1,0:T(8,128)(2,1)}, u32[]{:S(2)}, u32[]{:S(2)}) async-start(bf16[16,304,128]{2,1,0:T(8,128)(2,1)} %get-tuple-element.62), calls=%async_computation.2 | async-start | bytes 2490368 | tf_op jit(solution)/shard_map/all_to_all | solution.py:431
  66.4 38.8 %copy-start.2 = (bf16[16,256,128]{2,1,0:T(8,128)(2,1)}, bf16[16,256,128]{2,1,0:T(8,128)(2,1)S(1)}, u32[]{:S(2)}) copy-start(bf16[16,256,128]{2,1,0:T(8,128)(2,1)S(1)} %slice.31.refs_0_) | copy-start | bytes 3145732
  66.4 39.0 %collective-permute-start.12 = (bf16[16,256,128]{2,1,0:T(8,128)(2,1)S(1)}, bf16[16,256,128]{2,1,0:T(8,128)(2,1)}, u32[]{:S(2)}, u32[]{:S(2)}) collective-permute-start(bf16[16,256,128]{2,1,0:T(8,128)(2,1)S(1)} %slice.31.refs_0_), channel_id=1, source_target_pairs={{0,1},{1,0},{2,3},{3,2},{4,5},{5,4},{6,7},{7,6},{8,9},{9,8},{10,11... | collective-permute-start | bytes 3145736 | tf_op jit(solution)/shard_map/ppermute | solution.py:356
  68.4 10.2 %collective-permute-start.8 = (bf16[8,5120]{1,0:T(8,128)(2,1)S(1)}, bf16[8,5120]{1,0:T(8,128)(2,1)S(1)}, u32[]{:S(2)}, u32[]{:S(2)}) collective-permute-start(bf16[8,5120]{1,0:T(8,128)(2,1)S(1)} %get-tuple-element.80.refs_0_), channel_id=1, source_target_pairs={{0,7},{1,6},{2,5},{3,4},{4,3},{5,2},{6,1},{7,0},{8,15},{9,14},{10,... | collective-permute-start | bytes 245768 | tf_op jit(solution)/shard_map/ppermute | solution.py:356
  74.5 30.7 %collective-permute-start.9 = (bf16[8,5120]{1,0:T(8,128)(2,1)S(1)}, bf16[8,5120]{1,0:T(8,128)(2,1)S(1)}, u32[]{:S(2)}, u32[]{:S(2)}) collective-permute-start(bf16[8,5120]{1,0:T(8,128)(2,1)S(1)} %get-tuple-element.80.refs_0_), channel_id=1, source_target_pairs={{0,2},{1,3},{2,0},{3,1},{4,6},{5,7},{6,4},{7,5},{8,10},{9,11},{10,... | collective-permute-start | bytes 245768 | tf_op jit(solution)/shard_map/ppermute | solution.py:356
  77.6 30.9 %collective-permute-start.11 = (bf16[8,5120]{1,0:T(8,128)(2,1)S(1)}, bf16[8,5120]{1,0:T(8,128)(2,1)S(1)}, u32[]{:S(2)}, u32[]{:S(2)}) collective-permute-start(bf16[8,5120]{1,0:T(8,128)(2,1)S(1)} %get-tuple-element.80.refs_0_), channel_id=1, source_target_pairs={{0,1},{1,0},{2,3},{3,2},{4,5},{5,4},{6,7},{7,6},{8,9},{9,8},{10,11... | collective-permute-start | bytes 245768 | tf_op jit(solution)/shard_map/ppermute | solution.py:356
  78.6 29.8 %collective-permute-start.10 = (bf16[8,5120]{1,0:T(8,128)(2,1)S(1)}, bf16[8,5120]{1,0:T(8,128)(2,1)S(1)}, u32[]{:S(2)}, u32[]{:S(2)}) collective-permute-start(bf16[8,5120]{1,0:T(8,128)(2,1)S(1)} %collective-permute-done.8.refs_1_), channel_id=1, source_target_pairs={{0,2},{1,3},{2,0},{3,1},{4,6},{5,7},{6,4},{7,5},{8,10},{9,11},{10,... | collective-permute-start | bytes 245768 | tf_op jit(solution)/shard_map/ppermute | solution.py:356
  105.2 5.3 %copy-start.3 = (bf16[5120]{0:T(1024)(128)(2,1)S(1)}, bf16[5120]{0:T(1024)(128)(2,1)}, u32[]{:S(2)}) copy-start(bf16[5120]{0:T(1024)(128)(2,1)} %param.25) | copy-start | bytes 30724
  105.2 8.4 %collective-permute-start.13 = (bf16[16,5120]{1,0:T(8,128)(2,1)S(1)}, bf16[16,5120]{1,0:T(8,128)(2,1)S(1)}, u32[]{:S(2)}, u32[]{:S(2)}) collective-permute-start(bf16[16,5120]{1,0:T(8,128)(2,1)S(1)} %pad_maximum_fusion.1), channel_id=1, source_target_pairs={{0,1},{1,0},{2,3},{3,2},{4,5},{5,4},{6,7},{7,6},{8,9},{9,8},{10,11... | collective-permute-start | bytes 491528 | tf_op jit(solution)/shard_map/ppermute | solution.py:356
  108.5 5.2 %collective-permute-start.14 = (bf16[8,5120]{1,0:T(8,128)(2,1)S(1)}, bf16[8,5120]{1,0:T(8,128)(2,1)S(1)}, u32[]{:S(2)}, u32[]{:S(2)}) collective-permute-start(bf16[8,5120]{1,0:T(8,128)(2,1)S(1)} %collective-permute-done.10.refs_3_), channel_id=1, source_target_pairs={{0,1},{1,0},{2,3},{3,2},{4,5},{5,4},{6,7},{7,6},{8,9},{9,8},{10,11... | collective-permute-start | bytes 245768 | tf_op jit(solution)/shard_map/ppermute | solution.py:356
  110.6 3.1 %copy-start = (bf16[4,16,5120]{2,1,0:T(8,128)(2,1)S(1)}, bf16[4,16,5120]{2,1,0:T(8,128)(2,1)}, u32[]{:S(2)}) copy-start(bf16[4,16,5120]{2,1,0:T(8,128)(2,1)} %param.23) | copy-start | bytes 1966084
